TPU v7x, 128 devices: a whole 4x4x4 slice. The times are simulated.
128 devices in a mesh: gx: 16 (over z, y), gy: 8 (over x, core).
Axes of the slice: x: 4, y: 4, z: 4, core: 2. Of those that a mesh axis runs over, the one named last changes fastest.
Arguments:
- right_side: float32 [2, 3, 8, 256, 1024], P(None, None, None, 'gx', 'gy'), may hold values from -20 to 20
- conductivity: float32 [3, 8, 256, 1024], P(None, None, 'gx', 'gy'), may hold values from 0 to 8
- bloch_index: int32 [2], replicated, may hold values from 1 to 15
Outputs:
- solution: float32 [2, 3, 8, 256, 1024], P(None, None, None, 'gx', 'gy')
- residual: float32 [2, 3, 8, 256, 1024], P(None, None, None, 'gx', 'gy')
All inputs are finite; a program needn't handle non-finite values.
Results may differ from a plain program's by a relative error of at most 0.00045.
Values sent between devices are 32-bit elements; how exact they have to be, the bound alone decides.
No kernel may reach another device: no remote copies, remote signals or barrier semaphores. Data moves between devices by JAX's collectives and lax.ppermute only.
A program may use at most 128 MiB of HBM per device.

v0:
```python
import math

import jax
import jax.numpy as jnp
from jax import lax
from jax.sharding import PartitionSpec as P

S = 4
OUTER = 3


shift_real = 0.5
level_step = 0.4
basis_scale = 16.0
ridge_share = 0.001
bloch_steps = 16.0


def with_halo(value, sides, width):
    for axis, dim in sides:
        peers, length = (lax.axis_size(axis), value.shape[dim])
        up = [(i, (i + 1) % peers) for i in range(peers)]
        down = [(j, i) for i, j in up]
        last = lax.slice_in_dim(value, length - width, length, axis=dim)
        initial = lax.slice_in_dim(value, 0, width, axis=dim)
        before = lax.ppermute(last, axis, up)
        after = lax.ppermute(initial, axis, down)
        value = jnp.concatenate([before, value, after], axis=dim)
    return value


def rotate(field, cosine, sine):
    return jnp.stack([field[0] * cosine - field[1] * sine, field[0] * sine + field[1] * cosine])


def zahead(field):
    return jnp.concatenate([field[..., 1:, :, :], jnp.zeros_like(field[..., :1, :, :])], axis=-3)


def zbehind(field):
    return jnp.concatenate([jnp.zeros_like(field[..., :1, :, :]), field[..., :-1, :, :]], axis=-3)


def curl_curl(field):
    edge_x, edge_y, edge_z = (field[:, 0], field[:, 1], field[:, 2])

    def ahead_x(part):
        return part[..., 1:, :-1] - part[..., :-1, :-1]

    def ahead_y(part):
        return part[..., :-1, 1:] - part[..., :-1, :-1]

    def ahead_z(part):
        center = part[..., :-1, :-1]
        return zahead(center) - center

    curl_x = ahead_y(edge_z) - ahead_z(edge_y)
    curl_y = ahead_z(edge_x) - ahead_x(edge_z)
    curl_z = ahead_x(edge_y) - ahead_y(edge_x)

    def back_x(part):
        return part[..., :-1, 1:] - part[..., 1:, 1:]

    def back_y(part):
        return part[..., 1:, :-1] - part[..., 1:, 1:]

    def back_z(part):
        center = part[..., 1:, 1:]
        return zbehind(center) - center

    out_x = back_z(curl_y) - back_y(curl_z)
    out_y = back_x(curl_z) - back_z(curl_x)
    out_z = back_y(curl_x) - back_x(curl_y)
    return jnp.stack([out_x, out_y, out_z], axis=1)


def apply_operator(padded, conductivity):
    center = padded[..., 1:-1, 1:-1]
    swirl = curl_curl(padded)
    scaled = level_step * conductivity
    real_part = swirl[0] + shift_real * center[0] - scaled * center[1]
    imag_part = swirl[1] + shift_real * center[1] + scaled * center[0]
    return jnp.stack([real_part, imag_part]) / basis_scale


def bloch_fix(padded, rim_width, theta_x, theta_y):
    size_x = padded.shape[3]
    size_y = padded.shape[4]
    first_x = lax.axis_index("gx") == 0
    last_x = lax.axis_index("gx") == lax.axis_size("gx") - 1
    first_y = lax.axis_index("gy") == 0
    last_y = lax.axis_index("gy") == lax.axis_size("gy") - 1
    row_x = jnp.arange(size_x)
    row_y = jnp.arange(size_y)
    angle_x = jnp.where((row_x < rim_width) & first_x, -theta_x, 0.0) + jnp.where(
        (row_x >= size_x - rim_width) & last_x, theta_x, 0.0
    )
    angle_y = jnp.where((row_y < rim_width) & first_y, -theta_y, 0.0) + jnp.where(
        (row_y >= size_y - rim_width) & last_y, theta_y, 0.0
    )
    angle_all = angle_x[:, None] + angle_y[None, :]
    return rotate(padded, jnp.cos(angle_all), jnp.sin(angle_all))


def gram_matrix(basis):
    stacked = jnp.stack(basis).reshape(len(basis), 2, -1)
    real_rows, imag_rows = (stacked[:, 0], stacked[:, 1])
    highest = lax.Precision.HIGHEST
    gram_real = jnp.dot(real_rows, real_rows.T, precision=highest) + jnp.dot(
        imag_rows, imag_rows.T, precision=highest
    )
    gram_imag = jnp.dot(real_rows, imag_rows.T, precision=highest) - jnp.dot(
        imag_rows, real_rows.T, precision=highest
    )
    return (gram_real, gram_imag)


def coefficients(gram_real, gram_imag):
    herm_real = basis_scale * basis_scale * gram_real[1:, 1:]
    herm_imag = basis_scale * basis_scale * gram_imag[1:, 1:]
    load_real = basis_scale * gram_real[1:, 0]
    load_imag = basis_scale * gram_imag[1:, 0]
    count = herm_real.shape[0]
    shift_diag = ridge_share * jnp.trace(herm_real) / count * jnp.eye(count, dtype=herm_real.dtype)
    system = jnp.concatenate(
        [
            jnp.concatenate([herm_real + shift_diag, -herm_imag], axis=1),
            jnp.concatenate([herm_imag, herm_real + shift_diag], axis=1),
        ],
        axis=0,
    )
    target = jnp.concatenate([load_real, load_imag])
    factor = jnp.linalg.cholesky(system)
    answer = jax.scipy.linalg.cho_solve((factor, True), target)
    return (answer[:count], answer[count:])


def combine(vectors, coef_real, coef_imag):
    summed = rotate(vectors[0], coef_real[0], coef_imag[0])
    for index in range(1, len(vectors)):
        summed = summed + rotate(vectors[index], coef_real[index], coef_imag[index])
    return summed


def shards(right_side, conductivity, bloch_index):
    theta = 2.0 * math.pi * bloch_index.astype(jnp.float32) / bloch_steps
    theta_x, theta_y = (theta[0], theta[1])
    solution = jnp.zeros_like(right_side)
    residual = right_side
    for sweep in range(OUTER):
        basis = [residual]
        current = residual
        for power in range(S):
            padded = with_halo(current, (("gx", 3), ("gy", 4)), 1)
            padded = bloch_fix(padded, 1, theta_x, theta_y)
            current = apply_operator(padded, conductivity)
            basis.append(current)
        local_real, local_imag = gram_matrix(basis)
        gram_real, gram_imag = lax.psum((local_real, local_imag), ("gx", "gy"))
        coef_real, coef_imag = coefficients(gram_real, gram_imag)
        solution = solution + combine(basis[:S], coef_real, coef_imag)
        residual = residual - basis_scale * combine(basis[1:], coef_real, coef_imag)
    return (solution, residual)


def solution(mesh):
    in_specs = (P(None, None, None, "gx", "gy"), P(None, None, "gx", "gy"), P())
    out_specs = (P(None, None, None, "gx", "gy"), P(None, None, None, "gx", "gy"))
    return jax.shard_map(shards, mesh=mesh, in_specs=in_specs, out_specs=out_specs, check_vma=False)
```

profile of v0, /device:TPU:1, one launch (start us, length us, event | category | flops | bytes accessed | tf_op | source)
XLA Modules:
  0.0 553.5 jit_solution(12485641983861625083)
XLA Ops:
  4.6 5.0 collective-permute-start.1
  21.3 5.4 pad_maximum_fusion
  35.6 4.8 collective-permute-start.5
  50.4 5.6 %collective-permute-start.9 = (f32[2,3,8,1,128]{4,2,3,1,0:T(8,128)S(1)}, f32[2,3,8,1,128]{4,2,3,1,0:T(8,128)S(1)}, u32[]{:S(2)}, u32[]{:S(2)}) collective-permute-start(f32[2,3,8,1,128]{4,2,3,1,0:T(8,128)S(1)} %get-tuple-element.197), channel_id=1, source_target_pairs={{8,0},{16,8},{24,16},{32,24},{40,32},{48,40},{56,48},{64,56},{72,6... | collective-permute-start | bytes 73736 | tf_op jit(solution)/shard_map/ppermute | solution.py:27
  66.6 4.8 collective-permute-start.13
  87.2 3.5 fusion.36
  90.7 3.8 fusion.32
  94.4 3.9 fusion.57
  98.4 3.6 fusion.48
  102.0 68.7 %all-reduce.50 = (f32[5,5]{0,1:T(8,128)S(1)}, f32[5,5]{0,1:T(8,128)S(1)}) all-reduce(f32[5,5]{0,1:T(8,128)S(1)} %fusion.48, f32[5,5]{0,1:T(8,128)S(1)} %fusion.57), channel_id=1, replica_groups=mesh['gx'=16,'gy'=8] {'gx','gy'}, use_global_device_ids=true, to_apply=%region_0.1 | all-reduce | flops 50 | bytes 400 | tf_op jit(solution)/shard_map/psum | solution.py:159
  177.5 3.5 multiply_subtract_fusion.29
  188.0 4.8 collective-permute-start.17
  201.5 5.3 collective-permute-start.21
  215.5 5.4 collective-permute-start.25
  236.3 5.2 collective-permute-start.29
  246.9 3.5 collective-permute-start.31
  260.7 3.5 fusion.20
  264.1 3.8 fusion.16
  267.9 3.9 fusion.62
  271.9 3.6 fusion.51
  275.5 67.2 %all-reduce.49 = (f32[5,5]{0,1:T(8,128)S(1)}, f32[5,5]{0,1:T(8,128)S(1)}) all-reduce(f32[5,5]{0,1:T(8,128)S(1)} %fusion.51, f32[5,5]{0,1:T(8,128)S(1)} %fusion.62), channel_id=1, replica_groups=mesh['gx'=16,'gy'=8] {'gx','gy'}, use_global_device_ids=true, to_apply=%region_5.8 | all-reduce | flops 50 | bytes 400 | tf_op jit(solution)/shard_map/psum | solution.py:159
  349.7 3.6 multiply_subtract_fusion.21
  360.8 4.8 collective-permute-start.33
  374.3 5.3 collective-permute-start.37
  398.2 4.8 collective-permute-start.41
  426.6 5.2 collective-permute-start.45
  437.1 3.5 collective-permute-start.47
  451.0 3.5 fusion.4
  454.4 3.8 fusion
  458.2 3.9 fusion.67
  462.1 3.6 fusion.54
  465.8 67.2 %all-reduce.48 = (f32[5,5]{0,1:T(8,128)S(1)}, f32[5,5]{0,1:T(8,128)S(1)}) all-reduce(f32[5,5]{0,1:T(8,128)S(1)} %fusion.54, f32[5,5]{0,1:T(8,128)S(1)} %fusion.67), channel_id=1, replica_groups=mesh['gx'=16,'gy'=8] {'gx','gy'}, use_global_device_ids=true, to_apply=%region_8.11 | all-reduce | flops 50 | bytes 400 | tf_op jit(solution)/shard_map/psum | solution.py:159
  (648 shorter events, 218.9 us)
Async XLA Ops:
  2.5 14.3 %collective-permute-start = (f32[2,3,8,1,128]{4,2,3,1,0:T(8,128)S(1)}, f32[2,3,8,1,128]{4,2,3,1,0:T(8,128)S(1)}, u32[]{:S(2)}, u32[]{:S(2)}) collective-permute-start(f32[2,3,8,1,128]{4,2,3,1,0:T(8,128)S(1)} %get-tuple-element.200), channel_id=1, source_target_pairs={{0,8},{8,16},{16,24},{24,32},{32,40},{40,48},{48,56},{56,64},{64,7... | collective-permute-start | bytes 73736 | tf_op jit(solution)/shard_map/ppermute | solution.py:26
  4.6 14.4 %collective-permute-start.1 = (f32[2,3,8,1,128]{4,2,3,1,0:T(8,128)S(1)}, f32[2,3,8,1,128]{4,2,3,1,0:T(8,128)S(1)}, u32[]{:S(2)}, u32[]{:S(2)}) collective-permute-start(f32[2,3,8,1,128]{4,2,3,1,0:T(8,128)S(1)} %get-tuple-element.201), channel_id=1, source_target_pairs={{8,0},{16,8},{24,16},{32,24},{40,32},{48,40},{56,48},{64,56},{72,6... | collective-permute-start | bytes 73736 | tf_op jit(solution)/shard_map/ppermute | solution.py:27
  35.5 6.1 %collective-permute-start.4 = (f32[2,3,8,1,128]{4,2,3,1,0:T(8,128)S(1)}, f32[2,3,8,1,128]{4,2,3,1,0:T(8,128)S(1)}, u32[]{:S(2)}, u32[]{:S(2)}) collective-permute-start(f32[2,3,8,1,128]{4,2,3,1,0:T(8,128)S(1)} %get-tuple-element.198), channel_id=1, source_target_pairs={{0,8},{8,16},{16,24},{24,32},{32,40},{40,48},{48,56},{56,64},{64,7... | collective-permute-start | bytes 73736 | tf_op jit(solution)/shard_map/ppermute | solution.py:26
  50.3 7.9 %collective-permute-start.8 = (f32[2,3,8,1,128]{4,2,3,1,0:T(8,128)S(1)}, f32[2,3,8,1,128]{4,2,3,1,0:T(8,128)S(1)}, u32[]{:S(2)}, u32[]{:S(2)}) collective-permute-start(f32[2,3,8,1,128]{4,2,3,1,0:T(8,128)S(1)} %get-tuple-element.196), channel_id=1, source_target_pairs={{0,8},{8,16},{16,24},{24,32},{32,40},{40,48},{48,56},{56,64},{64,7... | collective-permute-start | bytes 73736 | tf_op jit(solution)/shard_map/ppermute | solution.py:26
  50.4 7.8 %collective-permute-start.9 = (f32[2,3,8,1,128]{4,2,3,1,0:T(8,128)S(1)}, f32[2,3,8,1,128]{4,2,3,1,0:T(8,128)S(1)}, u32[]{:S(2)}, u32[]{:S(2)}) collective-permute-start(f32[2,3,8,1,128]{4,2,3,1,0:T(8,128)S(1)} %get-tuple-element.197), channel_id=1, source_target_pairs={{8,0},{16,8},{24,16},{32,24},{40,32},{48,40},{56,48},{64,56},{72,6... | collective-permute-start | bytes 73736 | tf_op jit(solution)/shard_map/ppermute | solution.py:27
  66.6 6.8 %collective-permute-start.12 = (f32[2,3,8,1,128]{4,2,3,1,0:T(8,128)S(1)}, f32[2,3,8,1,128]{4,2,3,1,0:T(8,128)S(1)}, u32[]{:S(2)}, u32[]{:S(2)}) collective-permute-start(f32[2,3,8,1,128]{4,2,3,1,0:T(8,128)S(1)} %get-tuple-element.194), channel_id=1, source_target_pairs={{0,8},{8,16},{16,24},{24,32},{32,40},{40,48},{48,56},{56,64},{64,7... | collective-permute-start | bytes 73736 | tf_op jit(solution)/shard_map/ppermute | solution.py:26
  66.6 6.7 %collective-permute-start.13 = (f32[2,3,8,1,128]{4,2,3,1,0:T(8,128)S(1)}, f32[2,3,8,1,128]{4,2,3,1,0:T(8,128)S(1)}, u32[]{:S(2)}, u32[]{:S(2)}) collective-permute-start(f32[2,3,8,1,128]{4,2,3,1,0:T(8,128)S(1)} %get-tuple-element.195), channel_id=1, source_target_pairs={{8,0},{16,8},{24,16},{32,24},{40,32},{48,40},{56,48},{64,56},{72,6... | collective-permute-start | bytes 73736 | tf_op jit(solution)/shard_map/ppermute | solution.py:27
  74.0 6.0 %collective-permute-start.14 = (f32[2,3,8,18,1]{3,2,4,1,0:T(8,128)S(1)}, f32[2,3,8,18,1]{3,2,4,1,0:T(8,128)S(1)}, u32[]{:S(2)}, u32[]{:S(2)}) collective-permute-start(f32[2,3,8,18,1]{3,2,4,1,0:T(8,128)S(1)} %copy.847), channel_id=1, source_target_pairs={{0,1},{1,2},{2,3},{3,4},{4,5},{5,6},{6,7},{7,0},{8,9},{9,10},{10,1... | collective-permute-start | bytes 10376 | tf_op jit(solution)/shard_map/ppermute | solution.py:26
  187.9 6.1 %collective-permute-start.16 = (f32[2,3,8,1,128]{4,2,3,1,0:T(8,128)S(1)}, f32[2,3,8,1,128]{4,2,3,1,0:T(8,128)S(1)}, u32[]{:S(2)}, u32[]{:S(2)}) collective-permute-start(f32[2,3,8,1,128]{4,2,3,1,0:T(8,128)S(1)} %get-tuple-element.176), channel_id=1, source_target_pairs={{0,8},{8,16},{16,24},{24,32},{32,40},{40,48},{48,56},{56,64},{64,7... | collective-permute-start | bytes 73736 | tf_op jit(solution)/shard_map/ppermute | solution.py:26
  188.0 6.0 %collective-permute-start.17 = (f32[2,3,8,1,128]{4,2,3,1,0:T(8,128)S(1)}, f32[2,3,8,1,128]{4,2,3,1,0:T(8,128)S(1)}, u32[]{:S(2)}, u32[]{:S(2)}) collective-permute-start(f32[2,3,8,1,128]{4,2,3,1,0:T(8,128)S(1)} %get-tuple-element.177), channel_id=1, source_target_pairs={{8,0},{16,8},{24,16},{32,24},{40,32},{48,40},{56,48},{64,56},{72,6... | collective-permute-start | bytes 73736 | tf_op jit(solution)/shard_map/ppermute | solution.py:27
  201.4 6.3 %collective-permute-start.20 = (f32[2,3,8,1,128]{4,2,3,1,0:T(8,128)S(1)}, f32[2,3,8,1,128]{4,2,3,1,0:T(8,128)S(1)}, u32[]{:S(2)}, u32[]{:S(2)}) collective-permute-start(f32[2,3,8,1,128]{4,2,3,1,0:T(8,128)S(1)} %get-tuple-element.174), channel_id=1, source_target_pairs={{0,8},{8,16},{16,24},{24,32},{32,40},{40,48},{48,56},{56,64},{64,7... | collective-permute-start | bytes 73736 | tf_op jit(solution)/shard_map/ppermute | solution.py:26
  201.5 6.3 %collective-permute-start.21 = (f32[2,3,8,1,128]{4,2,3,1,0:T(8,128)S(1)}, f32[2,3,8,1,128]{4,2,3,1,0:T(8,128)S(1)}, u32[]{:S(2)}, u32[]{:S(2)}) collective-permute-start(f32[2,3,8,1,128]{4,2,3,1,0:T(8,128)S(1)} %get-tuple-element.175), channel_id=1, source_target_pairs={{8,0},{16,8},{24,16},{32,24},{40,32},{48,40},{56,48},{64,56},{72,6... | collective-permute-start | bytes 73736 | tf_op jit(solution)/shard_map/ppermute | solution.py:27
  215.4 7.7 %collective-permute-start.24 = (f32[2,3,8,1,128]{4,2,3,1,0:T(8,128)S(1)}, f32[2,3,8,1,128]{4,2,3,1,0:T(8,128)S(1)}, u32[]{:S(2)}, u32[]{:S(2)}) collective-permute-start(f32[2,3,8,1,128]{4,2,3,1,0:T(8,128)S(1)} %get-tuple-element.172), channel_id=1, source_target_pairs={{0,8},{8,16},{16,24},{24,32},{32,40},{40,48},{48,56},{56,64},{64,7... | collective-permute-start | bytes 73736 | tf_op jit(solution)/shard_map/ppermute | solution.py:26
  215.5 7.6 %collective-permute-start.25 = (f32[2,3,8,1,128]{4,2,3,1,0:T(8,128)S(1)}, f32[2,3,8,1,128]{4,2,3,1,0:T(8,128)S(1)}, u32[]{:S(2)}, u32[]{:S(2)}) collective-permute-start(f32[2,3,8,1,128]{4,2,3,1,0:T(8,128)S(1)} %get-tuple-element.173), channel_id=1, source_target_pairs={{8,0},{16,8},{24,16},{32,24},{40,32},{48,40},{56,48},{64,56},{72,6... | collective-permute-start | bytes 73736 | tf_op jit(solution)/shard_map/ppermute | solution.py:27
  223.7 8.2 %collective-permute-start.26 = (f32[2,3,8,18,1]{3,2,4,1,0:T(8,128)S(1)}, f32[2,3,8,18,1]{3,2,4,1,0:T(8,128)S(1)}, u32[]{:S(2)}, u32[]{:S(2)}) collective-permute-start(f32[2,3,8,18,1]{3,2,4,1,0:T(8,128)S(1)} %copy.862), channel_id=1, source_target_pairs={{0,1},{1,2},{2,3},{3,4},{4,5},{5,6},{6,7},{7,0},{8,9},{9,10},{10,1... | collective-permute-start | bytes 10376 | tf_op jit(solution)/shard_map/ppermute | solution.py:26
  224.1 8.2 %collective-permute-start.27 = (f32[2,3,8,18,1]{3,2,4,1,0:T(8,128)S(1)}, f32[2,3,8,18,1]{3,2,4,1,0:T(8,128)S(1)}, u32[]{:S(2)}, u32[]{:S(2)}) collective-permute-start(f32[2,3,8,18,1]{3,2,4,1,0:T(8,128)S(1)} %copy.863), channel_id=1, source_target_pairs={{1,0},{2,1},{3,2},{4,3},{5,4},{6,5},{7,6},{0,7},{9,8},{10,9},{11,1... | collective-permute-start | bytes 10376 | tf_op jit(solution)/shard_map/ppermute | solution.py:27
  236.2 7.9 %collective-permute-start.28 = (f32[2,3,8,1,128]{4,2,3,1,0:T(8,128)S(1)}, f32[2,3,8,1,128]{4,2,3,1,0:T(8,128)S(1)}, u32[]{:S(2)}, u32[]{:S(2)}) collective-permute-start(f32[2,3,8,1,128]{4,2,3,1,0:T(8,128)S(1)} %get-tuple-element.170), channel_id=1, source_target_pairs={{0,8},{8,16},{16,24},{24,32},{32,40},{40,48},{48,56},{56,64},{64,7... | collective-permute-start | bytes 73736 | tf_op jit(solution)/shard_map/ppermute | solution.py:26
  236.3 7.8 %collective-permute-start.29 = (f32[2,3,8,1,128]{4,2,3,1,0:T(8,128)S(1)}, f32[2,3,8,1,128]{4,2,3,1,0:T(8,128)S(1)}, u32[]{:S(2)}, u32[]{:S(2)}) collective-permute-start(f32[2,3,8,1,128]{4,2,3,1,0:T(8,128)S(1)} %get-tuple-element.171), channel_id=1, source_target_pairs={{8,0},{16,8},{24,16},{32,24},{40,32},{48,40},{56,48},{64,56},{72,6... | collective-permute-start | bytes 73736 | tf_op jit(solution)/shard_map/ppermute | solution.py:27
  246.5 6.1 %collective-permute-start.30 = (f32[2,3,8,18,1]{3,2,4,1,0:T(8,128)S(1)}, f32[2,3,8,18,1]{3,2,4,1,0:T(8,128)S(1)}, u32[]{:S(2)}, u32[]{:S(2)}) collective-permute-start(f32[2,3,8,18,1]{3,2,4,1,0:T(8,128)S(1)} %copy.867), channel_id=1, source_target_pairs={{0,1},{1,2},{2,3},{3,4},{4,5},{5,6},{6,7},{7,0},{8,9},{9,10},{10,1... | collective-permute-start | bytes 10376 | tf_op jit(solution)/shard_map/ppermute | solution.py:26
  246.9 6.9 %collective-permute-start.31 = (f32[2,3,8,18,1]{3,2,4,1,0:T(8,128)S(1)}, f32[2,3,8,18,1]{3,2,4,1,0:T(8,128)S(1)}, u32[]{:S(2)}, u32[]{:S(2)}) collective-permute-start(f32[2,3,8,18,1]{3,2,4,1,0:T(8,128)S(1)} %copy.868), channel_id=1, source_target_pairs={{1,0},{2,1},{3,2},{4,3},{5,4},{6,5},{7,6},{0,7},{9,8},{10,9},{11,1... | collective-permute-start | bytes 10376 | tf_op jit(solution)/shard_map/ppermute | solution.py:27
  360.8 6.0 %collective-permute-start.32 = (f32[2,3,8,1,128]{4,2,3,1,0:T(8,128)S(1)}, f32[2,3,8,1,128]{4,2,3,1,0:T(8,128)S(1)}, u32[]{:S(2)}, u32[]{:S(2)}) collective-permute-start(f32[2,3,8,1,128]{4,2,3,1,0:T(8,128)S(1)} %get-tuple-element.152), channel_id=1, source_target_pairs={{0,8},{8,16},{16,24},{24,32},{32,40},{40,48},{48,56},{56,64},{64,7... | collective-permute-start | bytes 73736 | tf_op jit(solution)/shard_map/ppermute | solution.py:26
  360.8 6.0 %collective-permute-start.33 = (f32[2,3,8,1,128]{4,2,3,1,0:T(8,128)S(1)}, f32[2,3,8,1,128]{4,2,3,1,0:T(8,128)S(1)}, u32[]{:S(2)}, u32[]{:S(2)}) collective-permute-start(f32[2,3,8,1,128]{4,2,3,1,0:T(8,128)S(1)} %get-tuple-element.153), channel_id=1, source_target_pairs={{8,0},{16,8},{24,16},{32,24},{40,32},{48,40},{56,48},{64,56},{72,6... | collective-permute-start | bytes 73736 | tf_op jit(solution)/shard_map/ppermute | solution.py:27
  374.2 13.5 %collective-permute-start.36 = (f32[2,3,8,1,128]{4,2,3,1,0:T(8,128)S(1)}, f32[2,3,8,1,128]{4,2,3,1,0:T(8,128)S(1)}, u32[]{:S(2)}, u32[]{:S(2)}) collective-permute-start(f32[2,3,8,1,128]{4,2,3,1,0:T(8,128)S(1)} %get-tuple-element.150), channel_id=1, source_target_pairs={{0,8},{8,16},{16,24},{24,32},{32,40},{40,48},{48,56},{56,64},{64,7... | collective-permute-start | bytes 73736 | tf_op jit(solution)/shard_map/ppermute | solution.py:26
  374.3 13.4 %collective-permute-start.37 = (f32[2,3,8,1,128]{4,2,3,1,0:T(8,128)S(1)}, f32[2,3,8,1,128]{4,2,3,1,0:T(8,128)S(1)}, u32[]{:S(2)}, u32[]{:S(2)}) collective-permute-start(f32[2,3,8,1,128]{4,2,3,1,0:T(8,128)S(1)} %get-tuple-element.151), channel_id=1, source_target_pairs={{8,0},{16,8},{24,16},{32,24},{40,32},{48,40},{56,48},{64,56},{72,6... | collective-permute-start | bytes 73736 | tf_op jit(solution)/shard_map/ppermute | solution.py:27
  398.1 13.3 %collective-permute-start.40 = (f32[2,3,8,1,128]{4,2,3,1,0:T(8,128)S(1)}, f32[2,3,8,1,128]{4,2,3,1,0:T(8,128)S(1)}, u32[]{:S(2)}, u32[]{:S(2)}) collective-permute-start(f32[2,3,8,1,128]{4,2,3,1,0:T(8,128)S(1)} %get-tuple-element.148), channel_id=1, source_target_pairs={{0,8},{8,16},{16,24},{24,32},{32,40},{40,48},{48,56},{56,64},{64,7... | collective-permute-start | bytes 73736 | tf_op jit(solution)/shard_map/ppermute | solution.py:26
  398.2 13.2 %collective-permute-start.41 = (f32[2,3,8,1,128]{4,2,3,1,0:T(8,128)S(1)}, f32[2,3,8,1,128]{4,2,3,1,0:T(8,128)S(1)}, u32[]{:S(2)}, u32[]{:S(2)}) collective-permute-start(f32[2,3,8,1,128]{4,2,3,1,0:T(8,128)S(1)} %get-tuple-element.149), channel_id=1, source_target_pairs={{8,0},{16,8},{24,16},{32,24},{40,32},{48,40},{56,48},{64,56},{72,6... | collective-permute-start | bytes 73736 | tf_op jit(solution)/shard_map/ppermute | solution.py:27
  413.8 7.5 %collective-permute-start.42 = (f32[2,3,8,18,1]{3,2,4,1,0:T(8,128)S(1)}, f32[2,3,8,18,1]{3,2,4,1,0:T(8,128)S(1)}, u32[]{:S(2)}, u32[]{:S(2)}) collective-permute-start(f32[2,3,8,18,1]{3,2,4,1,0:T(8,128)S(1)} %copy.882), channel_id=1, source_target_pairs={{0,1},{1,2},{2,3},{3,4},{4,5},{5,6},{6,7},{7,0},{8,9},{9,10},{10,1... | collective-permute-start | bytes 10376 | tf_op jit(solution)/shard_map/ppermute | solution.py:26
  414.7 7.8 %collective-permute-start.43 = (f32[2,3,8,18,1]{3,2,4,1,0:T(8,128)S(1)}, f32[2,3,8,18,1]{3,2,4,1,0:T(8,128)S(1)}, u32[]{:S(2)}, u32[]{:S(2)}) collective-permute-start(f32[2,3,8,18,1]{3,2,4,1,0:T(8,128)S(1)} %copy.883), channel_id=1, source_target_pairs={{1,0},{2,1},{3,2},{4,3},{5,4},{6,5},{7,6},{0,7},{9,8},{10,9},{11,1... | collective-permute-start | bytes 10376 | tf_op jit(solution)/shard_map/ppermute | solution.py:27
  426.5 7.9 %collective-permute-start.44 = (f32[2,3,8,1,128]{4,2,3,1,0:T(8,128)S(1)}, f32[2,3,8,1,128]{4,2,3,1,0:T(8,128)S(1)}, u32[]{:S(2)}, u32[]{:S(2)}) collective-permute-start(f32[2,3,8,1,128]{4,2,3,1,0:T(8,128)S(1)} %get-tuple-element.146), channel_id=1, source_target_pairs={{0,8},{8,16},{16,24},{24,32},{32,40},{40,48},{48,56},{56,64},{64,7... | collective-permute-start | bytes 73736 | tf_op jit(solution)/shard_map/ppermute | solution.py:26
  426.6 7.8 %collective-permute-start.45 = (f32[2,3,8,1,128]{4,2,3,1,0:T(8,128)S(1)}, f32[2,3,8,1,128]{4,2,3,1,0:T(8,128)S(1)}, u32[]{:S(2)}, u32[]{:S(2)}) collective-permute-start(f32[2,3,8,1,128]{4,2,3,1,0:T(8,128)S(1)} %get-tuple-element.147), channel_id=1, source_target_pairs={{8,0},{16,8},{24,16},{32,24},{40,32},{48,40},{56,48},{64,56},{72,6... | collective-permute-start | bytes 73736 | tf_op jit(solution)/shard_map/ppermute | solution.py:27
  436.7 6.1 %collective-permute-start.46 = (f32[2,3,8,18,1]{3,2,4,1,0:T(8,128)S(1)}, f32[2,3,8,18,1]{3,2,4,1,0:T(8,128)S(1)}, u32[]{:S(2)}, u32[]{:S(2)}) collective-permute-start(f32[2,3,8,18,1]{3,2,4,1,0:T(8,128)S(1)} %copy.887), channel_id=1, source_target_pairs={{0,1},{1,2},{2,3},{3,4},{4,5},{5,6},{6,7},{7,0},{8,9},{9,10},{10,1... | collective-permute-start | bytes 10376 | tf_op jit(solution)/shard_map/ppermute | solution.py:26
  437.1 6.9 %collective-permute-start.47 = (f32[2,3,8,18,1]{3,2,4,1,0:T(8,128)S(1)}, f32[2,3,8,18,1]{3,2,4,1,0:T(8,128)S(1)}, u32[]{:S(2)}, u32[]{:S(2)}) collective-permute-start(f32[2,3,8,18,1]{3,2,4,1,0:T(8,128)S(1)} %copy.888), channel_id=1, source_target_pairs={{1,0},{2,1},{3,2},{4,3},{5,4},{6,5},{7,6},{0,7},{9,8},{10,9},{11,1... | collective-permute-start | bytes 10376 | tf_op jit(solution)/shard_map/ppermute | solution.py:27
  (114 other events, 730.5 us)
where the time goes:
time: 563 us; the launch traced here: 553 us
  blocking collectives  203 us (36%)
  other arithmetic  99.2 us (18%)
  starting transfers between devices  96.6 us (17%)
  local copies, waits for them, and re-layouts  91.5 us (16%)
  matrix products  45.3 us (8%)
  waiting for transfers between devices  11 us (2%)
  between operations  6.69 us (1%)
    psum x3, blocking collectives, shards(): gram_real, gram_imag = lax.psum((local_real, local_imag), ('gx', 'gy'))  203 us
    ppermute x24, starting transfers between devices, with_halo(): after = lax.ppermute(initial, axis, down)  84.9 us
    sub x15, other arithmetic, rotate(): field[0] * cosine - field[1] * sine  36.9 us
    unnamed x224, local copies, waits for them, and re-layouts  26 us
    concatenate x24, other arithmetic, with_halo(): value = jnp.concatenate([before, value, after], axis=dim)  18.2 us
    unnamed x9, other arithmetic  16.5 us
    dot_general x3, matrix products, gram_matrix(): jnp.dot(real_rows, imag_rows.T, precision=highest)  11.8 us
    ppermute x24, starting transfers between devices, with_halo(): before = lax.ppermute(last, axis, up)  11.8 us
  transfers between devices with their start and end apart: 48, of which 10 were waited for; matrix products, arithmetic and copies ran while one was open for 13% of the time, Pallas kernels for 0%

commit v1 on v0

v1 whole, which is shorter than its diff:
```python
import functools
import math

import jax
import jax.numpy as jnp
from jax import lax
from jax.experimental import pallas as pl
from jax.experimental.pallas import tpu as pltpu
from jax.sharding import PartitionSpec as P

S = 4
NZ = 8
ROWS = 16
LANES = 128
WIDE = 48
MID = 32
SPAN = 256

shift_real = 0.5
level_step = 0.4
basis_scale = 16.0
ridge_share = 0.001
bloch_steps = 16.0

VMEM = pl.BlockSpec(memory_space=pltpu.VMEM)
SMEM = pl.BlockSpec(memory_space=pltpu.SMEM)
LIMIT = 16 * 1024 * 1024
PAIRS = [(j, k) for j in range(S + 1) for k in range(j, S + 1) if k > 0]


def lane_index(rows):
    return lax.broadcasted_iota(jnp.int32, (rows, LANES), 1)


def sub_index(rows):
    return lax.broadcasted_iota(jnp.int32, (rows, LANES), 0)


def pack_kernel(rs_ref, cond_ref, last_ref, first_ref, left_ref, right_ref):
    lanes = lane_index(ROWS)
    subs = sub_index(8)

    def pack(source, offset):
        def body(group, _):
            left = jnp.zeros((ROWS, LANES), jnp.float32)
            right = jnp.zeros((ROWS, LANES), jnp.float32)
            low, high = None, None
            for spot in range(8):
                plane = source[(group - offset) * 8 + spot]
                top, bottom = plane[:8], plane[8:]
                last_ref[group * 8 + spot] = bottom
                first_ref[group * 8 + spot] = top
                if spot % 2 == 0:
                    low, high = top, bottom
                else:
                    half = 72 + group * 4 + spot // 2
                    last_ref[half] = jnp.where(subs < 4, pltpu.roll(low, 4, 0), top)
                    first_ref[half] = jnp.where(subs < 4, high, pltpu.roll(bottom, 4, 0))
                inside = (lanes >= 16 * spot) & (lanes < 16 * spot + 16)
                ahead = pltpu.roll(plane, (16 * spot + 16) % LANES, 1)
                behind = plane if spot == 0 else pltpu.roll(plane, 16 * spot, 1)
                right = jnp.where(inside, ahead, right)
                left = jnp.where(inside, behind, left)
            left_ref[group] = left
            right_ref[group] = right
            return 0

        return body

    lax.fori_loop(0, 6, pack(rs_ref, 0), 0)
    lax.fori_loop(6, 9, pack(cond_ref, 6), 0)


def pack_messages(right_side, conductivity):
    lines = jax.ShapeDtypeStruct((108, 8, LANES), jnp.float32)
    strips = jax.ShapeDtypeStruct((9, ROWS, LANES), jnp.float32)
    return pl.pallas_call(
        pack_kernel,
        out_shape=(lines, lines, strips, strips),
        in_specs=[VMEM, VMEM],
        out_specs=(VMEM,) * 4,
        compiler_params=pltpu.CompilerParams(vmem_limit_bytes=LIMIT),
        name="pack_messages",
    )(right_side.reshape(48, ROWS, LANES), conductivity.reshape(24, ROWS, LANES))


def turn(real, imag, cosine, sine):
    return real * cosine - imag * sine, real * sine + imag * cosine


def fill(scal_ref, rs_ref, cond_ref, last_ref, first_ref, sides_ref, above_ref, below_ref, basis_ref, sigma_ref):
    lanes16 = lane_index(ROWS)
    lanes = lane_index(1)
    cos_b = jnp.where(lanes < 64, scal_ref[6], scal_ref[4])
    sin_b = jnp.where(lanes < 64, scal_ref[7], scal_ref[5])
    low_c, low_s, high_c, high_s = (scal_ref[k] for k in range(4))

    def strip(ref, group, spot):
        left, right = ref[group], ref[9 + group]
        left = pltpu.roll(left, (112 - 16 * spot) % LANES, 1) if spot != 7 else left
        right = pltpu.roll(right, (128 - 16 * spot) % LANES, 1) if spot else right
        return jnp.where(lanes16 < 64, right, left)

    def column(group, spot):
        return jnp.concatenate(
            [strip(above_ref, group, spot), strip(sides_ref, group, spot), strip(below_ref, group, spot)], axis=0
        )

    def lines(source, group, base, spot):
        subs = sub_index(8)
        plane = group * 8 + spot
        half = 72 + group * 4 + spot // 2
        before, after = last_ref[half], first_ref[half]
        if spot % 2 == 0:
            before = pltpu.roll(before, 4, 0)
        else:
            after = pltpu.roll(after, 4, 0)
        zero = jnp.zeros((8, LANES), jnp.float32)
        before = jnp.where(subs < 4, zero, before)
        after = jnp.where(subs < 4, after, zero)
        return jnp.concatenate(
            [before, last_ref[plane], source[(group - base) * 8 + spot], first_ref[plane], after], axis=0
        )

    def body(comp, _):
        for spot in range(NZ):
            real, imag = lines(rs_ref, comp, 0, spot), lines(rs_ref, comp + 3, 0, spot)
            real_b, imag_b = column(comp, spot), column(comp + 3, spot)
            real_b, imag_b = turn(real_b, imag_b, cos_b, sin_b)
            for part, at in ((real, imag), 0), ((real_b, imag_b), LANES):
                a, b = part
                lo = turn(a[:16], b[:16], low_c, low_s)
                hi = turn(a[32:], b[32:], high_c, high_s)
                for ri, whole in enumerate((a, b)):
                    basis_ref[0, ri, comp, spot, 0:16, at : at + LANES] = lo[ri]
                    basis_ref[0, ri, comp, spot, 16:32, at : at + LANES] = whole[16:32]
                    basis_ref[0, ri, comp, spot, 32:48, at : at + LANES] = hi[ri]
            sigma = lines(cond_ref, comp + 6, 6, spot)
            sigma_b = column(comp + 6, spot)
            factor = level_step / basis_scale
            sigma_ref[comp, spot, :, 0:LANES] = sigma * factor
            sigma_ref[comp, spot, :, LANES:SPAN] = sigma_b * factor
        return 0

    lax.fori_loop(0, 3, body, 0)


def apply_step(basis_ref, sigma_ref, k, rows, sigma_row):
    inverse = 1.0 / basis_scale

    def ahead_x(v):
        return pltpu.roll(v, rows - 1, 0) - v

    def back_x(v):
        return pltpu.roll(v, 1, 0) - v

    def ahead_y(v):
        return pltpu.roll(v, SPAN - 1, 1) - v

    def back_y(v):
        return pltpu.roll(v, 1, 1) - v

    def body(z, carry):
        fresh, outs = [], []
        for ri in range(2):
            ex, ey, ez = (basis_ref[k, ri, c, z] for c in range(3))
            hx = ahead_y(ez) - (basis_ref[k, ri, 1, z + 1] - ey)
            hy = (basis_ref[k, ri, 0, z + 1] - ex) - ahead_x(ez)
            hz = ahead_x(ey) - ahead_y(ex)
            old_x, old_y = carry[2 * ri], carry[2 * ri + 1]
            outs.append(
                ((old_y - hy) - back_y(hz), back_x(hz) - (old_x - hx), back_y(hx) - back_x(hy))
            )
            fresh += [hx, hy]
        for c in range(3):
            real, imag = basis_ref[k, 0, c, z], basis_ref[k, 1, c, z]
            sigma = sigma_ref[c, z, sigma_row : sigma_row + rows, :]
            basis_ref[k + 1, 0, c, z] = (outs[0][c] + shift_real * real) * inverse - sigma * imag
            basis_ref[k + 1, 1, c, z] = (outs[1][c] + shift_real * imag) * inverse + sigma * real
        return tuple(fresh)

    zero = jnp.zeros((rows, SPAN), jnp.float32)
    lax.fori_loop(0, NZ, body, (zero,) * 4)


def clear_end(basis_ref, rows):
    for k in range(S):
        for ri in range(2):
            for c in range(2):
                basis_ref[k, ri, c, NZ] = jnp.zeros((rows, SPAN), jnp.float32)


def gram(basis_ref, row, sums_ref, gram_ref):
    def body(plane, sums):
        c, z = plane // NZ, plane % NZ
        for top in range(row, row + ROWS, 8):
            vs = [[basis_ref[k, ri, c, z, top : top + 8, 0:LANES] for ri in range(2)] for k in range(S + 1)]
            fresh, at = [], 0
            for j, k in PAIRS:
                fresh.append(sums[at] + (vs[j][0] * vs[k][0] + vs[j][1] * vs[k][1]))
                at += 1
            for j, k in PAIRS:
                if j != k:
                    fresh.append(sums[at] + (vs[j][0] * vs[k][1] - vs[j][1] * vs[k][0]))
                    at += 1
            sums = tuple(fresh)
        return sums

    count = len(PAIRS) + sum(j != k for j, k in PAIRS)
    sums = lax.fori_loop(0, 3 * NZ, body, (jnp.zeros((8, LANES), jnp.float32),) * count)
    sums_ref[...] = jnp.zeros((LANES, LANES), jnp.float32)
    for at, total in enumerate(sums):
        sums_ref[at : at + 1, :] = jnp.sum(total, axis=0, keepdims=True)
    gram_ref[...] = lax.dot_general(
        jnp.ones(gram_ref.shape, jnp.float32),
        sums_ref[...],
        (((1,), (1,)), ((), ())),
        precision=lax.Precision.HIGHEST,
        preferred_element_type=jnp.float32,
    )


def cmul(a, b):
    return a[0] * b[0] - a[1] * b[1], a[0] * b[1] + a[1] * b[0]


def csub(a, b):
    return a[0] - b[0], a[1] - b[1]


def conj(a):
    return a[0], -a[1]


def coefficients(gathered_ref):
    row = jnp.broadcast_to(jnp.sum(gathered_ref[...], axis=0, keepdims=True), (8, LANES))

    def pick(at):
        return jnp.broadcast_to(row[:, at : at + 1], (8, LANES))

    entry, at = {}, len(PAIRS)
    for index, (j, k) in enumerate(PAIRS):
        if j == k:
            entry[j, k] = (pick(index), None)
        else:
            entry[j, k] = (pick(index), pick(at))
            at += 1
    square = basis_scale * basis_scale
    diag = [entry[k + 1, k + 1][0] * square for k in range(S)]
    extra = (ridge_share / S) * ((diag[0] + diag[1]) + (diag[2] + diag[3]))
    diag = [d + extra for d in diag]
    low = {}
    for j in range(S):
        for k in range(j + 1, S):
            real, imag = entry[j + 1, k + 1]
            low[k, j] = (real * square, -imag * square)
    load = [(entry[0, k + 1][0] * basis_scale, -entry[0, k + 1][1] * basis_scale) for k in range(S)]
    inverse, unit = [], {}
    for k in range(S):
        inverse.append(1.0 / diag[k])
        for i in range(k + 1, S):
            unit[i, k] = (low[i, k][0] * inverse[k], low[i, k][1] * inverse[k])
        for i in range(k + 1, S):
            real, imag = low[i, k]
            diag[i] = diag[i] - (real * real + imag * imag) * inverse[k]
            for j in range(k + 1, i):
                low[i, j] = csub(low[i, j], cmul(unit[i, k], conj(low[j, k])))
            load[i] = csub(load[i], cmul(unit[i, k], load[k]))
    answer = [None] * S
    for k in reversed(range(S)):
        value = (load[k][0] * inverse[k], load[k][1] * inverse[k])
        for j in range(k + 1, S):
            value = csub(value, cmul(conj(unit[j, k]), answer[j]))
        answer[k] = value
    return [(real[0, 0], imag[0, 0]) for real, imag in answer]


def new_residual(basis_ref, coefs, c, z, window):
    real, imag = basis_ref[(0, 0, c, z) + window], basis_ref[(0, 1, c, z) + window]
    for k in range(S):
        cr, ci = coefs[k][0] * basis_scale, coefs[k][1] * basis_scale
        vr, vi = basis_ref[(k + 1, 0, c, z) + window], basis_ref[(k + 1, 1, c, z) + window]
        real = real - (vr * cr - vi * ci)
        imag = imag - (vr * ci + vi * cr)
    return real, imag


def solution_part(basis_ref, coefs, c, z, window):
    total = None
    for k in range(S):
        vr, vi = basis_ref[(k, 0, c, z) + window], basis_ref[(k, 1, c, z) + window]
        part = turn(vr, vi, coefs[k][0], coefs[k][1])
        total = part if total is None else (total[0] + part[0], total[1] + part[1])
    return total


def first_kernel(
    scal_ref, rs_ref, cond_ref, last_ref, first_ref, sides_ref, above_ref, below_ref,
    basis_ref, sigma_ref, gram_ref, sums_ref,
):
    clear_end(basis_ref, WIDE)
    fill(scal_ref, rs_ref, cond_ref, last_ref, first_ref, sides_ref, above_ref, below_ref, basis_ref, sigma_ref)
    for k in range(S):
        apply_step(basis_ref, sigma_ref, k, WIDE, 0)
    gram(basis_ref, 16, sums_ref, gram_ref)


def next_kernel(first, gathered_ref, old_ref, sigma_ref, *refs):
    if first:
        basis_ref, part_ref, gram_ref, sums_ref = refs
        old_part = None
    else:
        old_part, basis_ref, part_ref, gram_ref, sums_ref = refs
    skip = (WIDE - MID) // 2 if first else 0
    coefs = coefficients(gathered_ref)
    clear_end(basis_ref, MID)

    def body(plane, _):
        c, z = plane // NZ, plane % NZ
        for top in range(0, MID, 8):
            for at in range(0, SPAN, LANES):
                window = (slice(skip + top, skip + top + 8), slice(at, at + LANES))
                real, imag = new_residual(old_ref, coefs, c, z, window)
                basis_ref[0, 0, c, z, top : top + 8, at : at + LANES] = real
                basis_ref[0, 1, c, z, top : top + 8, at : at + LANES] = imag
                if at == 0 and 8 <= top < 24:
                    part = solution_part(old_ref, coefs, c, z, window)
                    for ri in range(2):
                        value = part[ri]
                        if old_part is not None:
                            value = value + old_part[ri, c, z, top - 8 : top, :]
                        part_ref[ri, c, z, top - 8 : top, :] = value
        return 0

    lax.fori_loop(0, 3 * NZ, body, 0)
    for k in range(S):
        apply_step(basis_ref, sigma_ref, k, MID, (WIDE - MID) // 2)
    gram(basis_ref, 8, sums_ref, gram_ref)


def last_kernel(gathered_ref, old_ref, old_part, part_ref, residual_ref):
    coefs = coefficients(gathered_ref)

    def body(plane, _):
        c, z = plane // NZ, plane % NZ
        for top in range(0, ROWS, 8):
            window = (slice(8 + top, 16 + top), slice(0, LANES))
            residual = new_residual(old_ref, coefs, c, z, window)
            part = solution_part(old_ref, coefs, c, z, window)
            for ri in range(2):
                residual_ref[ri, c, z, top : top + 8, :] = residual[ri]
                part_ref[ri, c, z, top : top + 8, :] = part[ri] + old_part[ri, c, z, top : top + 8, :]
        return 0

    lax.fori_loop(0, 3 * NZ, body, 0)


def vmem(shape):
    return pltpu.VMEM(shape, jnp.float32)


PART = (2, 3, NZ, ROWS, LANES)


def run_first(peers, scal, right_side, conductivity, last, first, sides, above, below):
    return pl.pallas_call(
        first_kernel,
        out_shape=(vmem((S + 1, 2, 3, NZ + 1, WIDE, SPAN)), vmem((3, NZ, WIDE, SPAN)), jax.ShapeDtypeStruct((peers, LANES), jnp.float32)),
        in_specs=[SMEM] + [VMEM] * 7,
        out_specs=(VMEM,) * 3,
        scratch_shapes=[vmem((LANES, LANES))],
        compiler_params=pltpu.CompilerParams(vmem_limit_bytes=LIMIT),
        name="first_sweep",
    )(scal, right_side.reshape(48, ROWS, LANES), conductivity.reshape(24, ROWS, LANES), last, first, sides, above, below)


def run_next(peers, is_first, gathered, old, sigma, *part):
    return pl.pallas_call(
        functools.partial(next_kernel, is_first),
        out_shape=(vmem((S + 1, 2, 3, NZ + 1, MID, SPAN)), vmem(PART), jax.ShapeDtypeStruct((peers, LANES), jnp.float32)),
        in_specs=[VMEM] * (3 + len(part)),
        out_specs=(VMEM,) * 3,
        scratch_shapes=[vmem((LANES, LANES))],
        compiler_params=pltpu.CompilerParams(vmem_limit_bytes=LIMIT),
        name="second_sweep" if is_first else "third_sweep",
    )(gathered, old, sigma, *part)


def run_last(gathered, old, part):
    shape = jax.ShapeDtypeStruct(PART, jnp.float32)
    return pl.pallas_call(
        last_kernel,
        out_shape=(shape, shape),
        in_specs=[VMEM] * 3,
        out_specs=(VMEM,) * 2,
        compiler_params=pltpu.CompilerParams(vmem_limit_bytes=LIMIT),
        name="last_update",
    )(gathered, old, part)


def spread(partial):
    return lax.all_to_all(partial, ("gx", "gy"), 0, 0, tiled=True)


def phases(bloch_index):
    theta = 2.0 * math.pi * bloch_index.astype(jnp.float32) / bloch_steps
    rows = []
    for axis, angle in (("gx", theta[0]), ("gy", theta[1])):
        spot, peers = lax.axis_index(axis), lax.axis_size(axis)
        cosine, sine = jnp.cos(angle), jnp.sin(angle)
        rows += [jnp.where(spot == 0, cosine, 1.0), jnp.where(spot == 0, -sine, 0.0)]
        rows += [jnp.where(spot == peers - 1, cosine, 1.0), jnp.where(spot == peers - 1, sine, 0.0)]
    return jnp.stack(rows)


def ring(axis, step):
    peers = lax.axis_size(axis)
    return [(i, (i + step) % peers) for i in range(peers)]


def shards(right_side, conductivity, bloch_index):
    peers = lax.axis_size("gx") * lax.axis_size("gy")
    scal = phases(bloch_index)
    last, first, left, right = pack_messages(right_side, conductivity)
    above = lax.ppermute(last, "gx", ring("gx", 1))
    below = lax.ppermute(first, "gx", ring("gx", -1))
    before = lax.ppermute(right, "gy", ring("gy", 1))
    after = lax.ppermute(left, "gy", ring("gy", -1))
    sides = jnp.concatenate([before, after])
    corners_above = lax.ppermute(sides, "gx", ring("gx", 1))
    corners_below = lax.ppermute(sides, "gx", ring("gx", -1))
    basis, sigma, partial = run_first(
        peers, scal, right_side, conductivity, above, below, sides, corners_above, corners_below
    )
    basis, part, partial = run_next(peers, True, spread(partial), basis, sigma)
    basis, part, partial = run_next(peers, False, spread(partial), basis, sigma, part)
    return run_last(spread(partial), basis, part)


def solution(mesh):
    in_specs = (P(None, None, None, "gx", "gy"), P(None, None, "gx", "gy"), P())
    out_specs = (P(None, None, None, "gx", "gy"), P(None, None, None, "gx", "gy"))
    return jax.shard_map(shards, mesh=mesh, in_specs=in_specs, out_specs=out_specs, check_vma=False)
```

time: 563 us -> 106 us (0.19); the launches traced: 553 us -> 105 us
  blocking collectives: 203 us -> 46.6 us
  other arithmetic: 99.2 us -> 0.66 us
  local copies, waits for them, and re-layouts: 91.5 us -> 4.52 us
  starting transfers between devices: 96.6 us -> 12.6 us
  matrix products: 45.3 us -> 0 us
  Pallas kernels: 0 us -> 32.2 us
  waiting for transfers between devices: 11 us -> 5.01 us
    psum x3 -> x0, blocking collectives: 203 us -> none  [shards(): gram_real, gram_imag = lax.psum((local_real, local_imag), ('gx', 'gy'))]
    ppermute x48 -> x6, starting transfers between devices: 96.6 us -> 12.6 us  [the longest x1 4.91 us: shards(): below = lax.ppermute(first, 'gx', ring('gx', -1))]
    all_to_all x0 -> x3, blocking collectives: none -> 46.6 us  [spread(): return lax.all_to_all(partial, ('gx', 'gy'), 0, 0, tiled=True)]
    dot_general x12 -> x0, matrix products: 44.3 us -> none  [the longest x3 11.8 us: gram_matrix(): jnp.dot(real_rows, imag_rows.T, precision=highest)]
    sub x42 -> x0, other arithmetic: 43.2 us -> none  [the longest x15 36.9 us: rotate(): field[0] * cosine - field[1] * sine]
    pallas_call x0 -> x5, Pallas kernels: none -> 32.2 us  [the longest x2 18.5 us: run_next(): pl.pallas_call(functools.partial(next_kernel, is_first), out_shape=(vmem(...]
    unnamed x224 -> x9, local copies, waits for them, and re-layouts: 26 us -> 3.84 us
    ppermute x26 -> x0, local copies, waits for them, and re-layouts: 21.1 us -> none  [the longest x13 11.7 us: with_halo(): after = lax.ppermute(initial, axis, down)]
  transfers between devices with their start and end apart: 48 -> 6, of which waited for: 10 -> 2; matrix products, arithmetic and copies ran while one was open for 13% -> 1% of each run, Pallas kernels for 0% -> 0%
where the time goes in v1:
time: 106 us; the launch traced here: 105 us
  blocking collectives  46.6 us (44%)
  Pallas kernels  32.2 us (30%)
  starting transfers between devices  12.6 us (12%)
  waiting for transfers between devices  5.01 us (5%)
  local copies, waits for them, and re-layouts  4.52 us (4%)
  between operations  3.61 us (3%)
    all_to_all x3, blocking collectives, spread(): return lax.all_to_all(partial, ('gx', 'gy'), 0, 0, tiled=True)  46.6 us
    pallas_call x2, Pallas kernels, run_next(): pl.pallas_call(functools.partial(next_kernel, is_first), out_shape=(vmem(...  18.5 us
    pallas_call x1, Pallas kernels, run_first(): pl.pallas_call(first_kernel, out_shape=(vmem((S + 1, 2, 3, NZ + 1, WIDE,...  11 us
    ppermute x1, starting transfers between devices, shards(): below = lax.ppermute(first, 'gx', ring('gx', -1))  4.91 us
    unnamed x9, local copies, waits for them, and re-layouts  3.84 us
    ppermute x1, starting transfers between devices, shards(): corners_below = lax.ppermute(sides, 'gx', ring('gx', -1))  3.74 us
    ppermute x1, waiting for transfers between devices, shards(): corners_below = lax.ppermute(sides, 'gx', ring('gx', -1))  2.73 us
    ppermute x1, starting transfers between devices, shards(): before = lax.ppermute(right, 'gy', ring('gy', 1))  2.61 us
  transfers between devices with their start and end apart: 6, of which 2 were waited for; matrix products, arithmetic and copies ran while one was open for 1% of the time, Pallas kernels for 0%

profile of v1, /device:TPU:1, one launch (start us, length us, event | category | flops | bytes accessed | tf_op | source)
XLA Modules:
  0.0 105.2 jit_solution(14130716067650373002)
XLA Ops:
  0.6 0.0 copy-start
  0.6 1.0 copy-done
  1.6 0.0 copy-start.2
  1.6 0.9 copy-done.2
  2.6 0.9 pack_messages.1
  3.4 2.6 %collective-permute-start.2 = (f32[9,16,128]{2,1,0:T(8,128)S(1)}, f32[9,16,128]{2,1,0:T(8,128)S(1)}, u32[]{:S(2)}, u32[]{:S(2)}) collective-permute-start(f32[9,16,128]{2,1,0:T(8,128)S(1)} %get-tuple-element.17), channel_id=1, source_target_pairs={{0,1},{1,2},{2,3},{3,4},{4,5},{5,6},{6,7},{7,0},{8,9},{9,10},{10,1... | collective-permute-start | bytes 221192 | tf_op jit(solution)/shard_map/ppermute | solution.py:427
  6.0 0.0 collective-permute-start.3
  6.0 1.3 %collective-permute-start = (f32[108,8,128]{2,1,0:T(8,128)S(1)}, f32[108,8,128]{2,1,0:T(8,128)S(1)}, u32[]{:S(2)}, u32[]{:S(2)}) collective-permute-start(f32[108,8,128]{2,1,0:T(8,128)S(1)} %get-tuple-element.15), channel_id=1, source_target_pairs={{0,8},{8,16},{16,24},{24,32},{32,40},{40,48},{48,56},{56,64},{64,7... | collective-permute-start | bytes 1327112 | tf_op jit(solution)/shard_map/ppermute | solution.py:425
  7.3 4.9 %collective-permute-start.1 = (f32[108,8,128]{2,1,0:T(8,128)S(1)}, f32[108,8,128]{2,1,0:T(8,128)S(1)}, u32[]{:S(2)}, u32[]{:S(2)}) collective-permute-start(f32[108,8,128]{2,1,0:T(8,128)S(1)} %get-tuple-element.16), channel_id=1, source_target_pairs={{0,120},{8,0},{16,8},{24,16},{32,24},{40,32},{48,40},{56,48},{64,5... | collective-permute-start | bytes 1327112 | tf_op jit(solution)/shard_map/ppermute | solution.py:426
  12.3 0.0 collective-permute-done.2
  12.3 0.0 collective-permute-done.3
  12.3 3.7 %collective-permute-start.5 = (f32[18,16,128]{2,1,0:T(8,128)S(1)}, f32[18,16,128]{2,1,0:T(8,128)S(1)}, u32[]{:S(2)}, u32[]{:S(2)}) collective-permute-start(f32[18,16,128]{2,1,0:T(8,128)S(1)} %constant_dynamic-update-slice_fusion.sides_ref), channel_id=1, source_target_pairs={{0,120},{8,0},{16,8},{24,16},{32,24},{40,32},{48,40},{56,48},{64,5... | collective-permute-start | bytes 442376 | tf_op jit(solution)/shard_map/ppermute | solution.py:431
  16.0 0.0 collective-permute-start.4
  16.0 0.7 convert_multiply_fusion
  16.7 0.6 fusion
  20.2 0.1 stack.35.scal_ref
  20.3 2.7 %collective-permute-done.5.below_ref = f32[18,16,128]{2,1,0:T(8,128)S(1)} collective-permute-done((f32[18,16,128]{2,1,0:T(8,128)S(1)}, f32[18,16,128]{2,1,0:T(8,128)S(1)}, u32[]{:S(2)}, u32[]{:S(2)}) %collective-permute-start.5) | collective-permute-done | bytes 147488 | tf_op jit(solution)/shard_map/ppermute | solution.py:431
  23.0 2.3 %collective-permute-done.4.above_ref = f32[18,16,128]{2,1,0:T(8,128)S(1)} collective-permute-done((f32[18,16,128]{2,1,0:T(8,128)S(1)}, f32[18,16,128]{2,1,0:T(8,128)S(1)}, u32[]{:S(2)}, u32[]{:S(2)}) %collective-permute-start.4) | collective-permute-done | bytes 147488 | tf_op jit(solution)/shard_map/ppermute | solution.py:430
  25.3 0.0 collective-permute-done.last_ref
  25.3 0.0 collective-permute-done.1.first_ref
  25.3 0.0 copy-start.1
  25.3 1.0 copy-done.1
  26.3 0.0 copy-start.3
  26.3 0.9 copy-done.3
  27.2 11.0 %first_sweep.1 = (f32[5,2,3,9,48,256]{5,4,3,2,1,0:T(8,128)S(1)}, f32[3,8,48,256]{3,2,1,0:T(8,128)S(1)}, f32[128,128]{1,0:T(8,128)S(1)}) custom-call(f32[8]{0:T(128)S(1)} %stack.35.scal_ref, f32[48,16,128]{2,1,0:T(8,128)S(1)} %bitcast.27, f32[24,16,128]{2,1,0:T(8,128)S(1)} %bitcast.29, f32[108,8,128]{2,1,0:T(8,128)S(1)} %collective-permute-done.last_ref, ...), custom_call_target="tpu_custom_call" | custom-call | tf_op jit(solution)/shard_map/first_sweep/pallas_call | solution.py:366
  38.2 18.8 %all_to_all.33 = f32[128,1,128]{2,1,0:T(1,128)S(1)} all-to-all(f32[128,1,128]{2,1,0:T(1,128)S(1)} %bitcast.33), channel_id=1, replica_groups=mesh['gx'=16,'gy'=8] {'gx','gy'}, dimensions={0} | all-to-all | bytes 131072 | tf_op jit(solution)/shard_map/all_to_all | solution.py:402
  57.0 9.3 %second_sweep.1 = (f32[5,2,3,9,32,256]{5,4,3,2,1,0:T(8,128)S(1)}, f32[2,3,8,16,128]{4,3,2,1,0:T(8,128)S(1)}, f32[128,128]{1,0:T(8,128)S(1)}) custom-call(f32[128,128]{1,0:T(8,128)S(1)} %bitcast.31, f32[5,2,3,9,48,256]{5,4,3,2,1,0:T(8,128)S(1)} %get-tuple-element.20.old_ref, f32[3,8,48,256]{3,2,1,0:T(8,128)S(1)} %get-tuple-element.21.sigma_ref), custom_call_target="tpu_custom_call" | custom-call | tf_op jit(solution)/shard_map/second_sweep/pallas_call | solution.py:378
  66.2 13.9 %all_to_all.34 = f32[128,1,128]{2,1,0:T(1,128)S(1)} all-to-all(f32[128,1,128]{2,1,0:T(1,128)S(1)} %bitcast.35), channel_id=1, replica_groups=mesh['gx'=16,'gy'=8] {'gx','gy'}, dimensions={0} | all-to-all | bytes 131072 | tf_op jit(solution)/shard_map/all_to_all | solution.py:402
  80.1 9.3 %third_sweep.1 = (f32[5,2,3,9,32,256]{5,4,3,2,1,0:T(8,128)S(1)}, f32[2,3,8,16,128]{4,3,2,1,0:T(8,128)S(1)}, f32[128,128]{1,0:T(8,128)S(1)}) custom-call(f32[128,128]{1,0:T(8,128)S(1)} %bitcast.30, f32[5,2,3,9,32,256]{5,4,3,2,1,0:T(8,128)S(1)} %get-tuple-element.23.old_ref, f32[3,8,48,256]{3,2,1,0:T(8,128)S(1)} %get-tuple-element.21.sigma_ref, ...), custom_call_target="tpu_custom_call" | custom-call | tf_op jit(solution)/shard_map/third_sweep/pallas_call | solution.py:378
  89.4 13.9 %all_to_all.35 = f32[128,1,128]{2,1,0:T(1,128)S(1)} all-to-all(f32[128,1,128]{2,1,0:T(1,128)S(1)} %bitcast.34), channel_id=1, replica_groups=mesh['gx'=16,'gy'=8] {'gx','gy'}, dimensions={0} | all-to-all | bytes 131072 | tf_op jit(solution)/shard_map/all_to_all | solution.py:402
  103.3 1.8 %last_update.1 = (f32[2,3,8,16,128]{4,3,2,1,0:T(8,128)}, f32[2,3,8,16,128]{4,3,2,1,0:T(8,128)}) custom-call(f32[128,128]{1,0:T(8,128)S(1)} %bitcast.32, f32[5,2,3,9,32,256]{5,4,3,2,1,0:T(8,128)S(1)} %get-tuple-element.26.old_ref, f32[2,3,8,16,128]{4,3,2,1,0:T(8,128)S(1)} %get-tuple-element.27.old_part), custom_call_target="tpu_custom_call" | custom-call | tf_op jit(solution)/shard_map/last_update/pallas_call | solution.py:391
  (2 shorter events, 0.0 us)
Async XLA Ops:
  0.6 1.0 copy-start
  1.6 0.9 copy-start.2
  3.4 8.8 %collective-permute-start.2 = (f32[9,16,128]{2,1,0:T(8,128)S(1)}, f32[9,16,128]{2,1,0:T(8,128)S(1)}, u32[]{:S(2)}, u32[]{:S(2)}) collective-permute-start(f32[9,16,128]{2,1,0:T(8,128)S(1)} %get-tuple-element.17), channel_id=1, source_target_pairs={{0,1},{1,2},{2,3},{3,4},{4,5},{5,6},{6,7},{7,0},{8,9},{9,10},{10,1... | collective-permute-start | bytes 221192 | tf_op jit(solution)/shard_map/ppermute | solution.py:427
  6.0 6.2 %collective-permute-start.3 = (f32[9,16,128]{2,1,0:T(8,128)S(1)}, f32[9,16,128]{2,1,0:T(8,128)S(1)}, u32[]{:S(2)}, u32[]{:S(2)}) collective-permute-start(f32[9,16,128]{2,1,0:T(8,128)S(1)} %get-tuple-element.18), channel_id=1, source_target_pairs={{0,7},{1,0},{2,1},{3,2},{4,3},{5,4},{6,5},{7,6},{8,15},{9,8},{10,9... | collective-permute-start | bytes 221192 | tf_op jit(solution)/shard_map/ppermute | solution.py:428
  6.0 19.2 %collective-permute-start = (f32[108,8,128]{2,1,0:T(8,128)S(1)}, f32[108,8,128]{2,1,0:T(8,128)S(1)}, u32[]{:S(2)}, u32[]{:S(2)}) collective-permute-start(f32[108,8,128]{2,1,0:T(8,128)S(1)} %get-tuple-element.15), channel_id=1, source_target_pairs={{0,8},{8,16},{16,24},{24,32},{32,40},{40,48},{48,56},{56,64},{64,7... | collective-permute-start | bytes 1327112 | tf_op jit(solution)/shard_map/ppermute | solution.py:425
  7.3 18.0 %collective-permute-start.1 = (f32[108,8,128]{2,1,0:T(8,128)S(1)}, f32[108,8,128]{2,1,0:T(8,128)S(1)}, u32[]{:S(2)}, u32[]{:S(2)}) collective-permute-start(f32[108,8,128]{2,1,0:T(8,128)S(1)} %get-tuple-element.16), channel_id=1, source_target_pairs={{0,120},{8,0},{16,8},{24,16},{32,24},{40,32},{48,40},{56,48},{64,5... | collective-permute-start | bytes 1327112 | tf_op jit(solution)/shard_map/ppermute | solution.py:426
  12.3 10.7 %collective-permute-start.5 = (f32[18,16,128]{2,1,0:T(8,128)S(1)}, f32[18,16,128]{2,1,0:T(8,128)S(1)}, u32[]{:S(2)}, u32[]{:S(2)}) collective-permute-start(f32[18,16,128]{2,1,0:T(8,128)S(1)} %constant_dynamic-update-slice_fusion.sides_ref), channel_id=1, source_target_pairs={{0,120},{8,0},{16,8},{24,16},{32,24},{40,32},{48,40},{56,48},{64,5... | collective-permute-start | bytes 442376 | tf_op jit(solution)/shard_map/ppermute | solution.py:431
  16.0 9.3 %collective-permute-start.4 = (f32[18,16,128]{2,1,0:T(8,128)S(1)}, f32[18,16,128]{2,1,0:T(8,128)S(1)}, u32[]{:S(2)}, u32[]{:S(2)}) collective-permute-start(f32[18,16,128]{2,1,0:T(8,128)S(1)} %constant_dynamic-update-slice_fusion.sides_ref), channel_id=1, source_target_pairs={{0,8},{8,16},{16,24},{24,32},{32,40},{40,48},{48,56},{56,64},{64,7... | collective-permute-start | bytes 442376 | tf_op jit(solution)/shard_map/ppermute | solution.py:430
  25.3 1.0 copy-start.1
  26.3 0.9 copy-start.3

commit v2 on v1

v2 whole, which is shorter than its diff:
```python
import functools
import math

import jax
import jax.numpy as jnp
from jax import lax
from jax.experimental import pallas as pl
from jax.experimental.pallas import tpu as pltpu
from jax.sharding import PartitionSpec as P

S = 4
NZ = 8
ROWS = 16
LANES = 128
HALO = 12
WIDE = ROWS + 2 * HALO

shift_real = 0.5
level_step = 0.4
basis_scale = 16.0
ridge_share = 0.001
bloch_steps = 16.0


VMEM = pl.BlockSpec(memory_space=pltpu.VMEM)
SMEM = pl.BlockSpec(memory_space=pltpu.SMEM)
HBM = pl.BlockSpec(memory_space=pltpu.HBM)
LIMIT = 16 * 1024 * 1024
PAIRS = [(j, k) for j in range(S + 1) for k in range(j, S + 1) if k > 0]
BLOCK = (NZ, LANES)


def vmem(shape):
    return pltpu.VMEM(shape, jnp.float32)


def lane_index(rows):
    return lax.broadcasted_iota(jnp.int32, (rows, LANES), 1)


def roll_lanes(value, shift):
    shift = shift % LANES
    return pltpu.roll(value, shift, 1) if shift else value


def column_order(transposed):
    row = lax.broadcasted_iota(jnp.int32, (LANES, LANES), 0)
    lane = lax.broadcasted_iota(jnp.int32, (LANES, LANES), 1)
    column, place = (lane, row) if transposed else (row, lane)
    wanted = jnp.where(place < 64, 2 * place, 2 * place - (LANES - 1))
    return jnp.where(column == wanted, 1.0, 0.0).astype(jnp.bfloat16)


def reorder(value, order):
    first = value.astype(jnp.bfloat16)
    rest = value - first.astype(jnp.float32)
    second = rest.astype(jnp.bfloat16)
    third = (rest - second.astype(jnp.float32)).astype(jnp.bfloat16)
    parts = [jnp.dot(part, order, preferred_element_type=jnp.float32) for part in (first, second, third)]
    return (parts[0] + parts[1]) + parts[2]


def pack_kernel(rs_hbm, cond_hbm, tile_ref, last_ref, first_ref, strip_ref, rs_ref, cond_ref, sems):
    copies = [
        pltpu.make_async_copy(rs_hbm, rs_ref, sems.at[0]),
        pltpu.make_async_copy(cond_hbm, cond_ref, sems.at[1]),
    ]
    for copy in copies:
        copy.start()
    order = column_order(False)
    eighth = (lane_index(NZ) // 8) % 8

    def pack(source, offset):
        def body(group, _):
            start = (group - offset) * (NZ * ROWS)
            rows = [source[pl.ds(start + x, NZ, stride=ROWS), :] for x in range(ROWS)]
            packed = reorder(jnp.concatenate(rows, axis=0), order)
            rows = [packed[NZ * x : NZ * x + NZ] for x in range(ROWS)]
            for x in range(ROWS):
                tile_ref[group, x] = rows[x]
                if x >= ROWS - HALO:
                    last_ref[group, x - (ROWS - HALO)] = rows[x]
                if x < HALO:
                    first_ref[group, x] = rows[x]
            for four in range(ROWS // 4):
                strip = None
                for j in range(4):
                    moved = roll_lanes(rows[4 * four + j], 64 + 16 * j)
                    if strip is None:
                        strip = moved
                    else:
                        strip = jnp.where((eighth == 2 * j) | (eighth == (7 + 2 * j) % 8), moved, strip)
                strip_ref[group, four] = strip
            return 0

        return body

    copies[0].wait()
    lax.fori_loop(0, 6, pack(rs_ref, 0), 0)
    copies[1].wait()
    lax.fori_loop(6, 9, pack(cond_ref, 6), 0)


def pack_messages(right_side, conductivity):
    rows, edge = (9, ROWS) + BLOCK, (9, HALO) + BLOCK
    return pl.pallas_call(
        pack_kernel,
        out_shape=(vmem(rows), vmem(edge), vmem(edge), vmem((9, ROWS // 4) + BLOCK)),
        in_specs=[HBM, HBM],
        out_specs=(VMEM,) * 4,
        scratch_shapes=[vmem((6 * NZ * ROWS, LANES)), vmem((3 * NZ * ROWS, LANES)), pltpu.SemaphoreType.DMA((2,))],
        compiler_params=pltpu.CompilerParams(vmem_limit_bytes=LIMIT),
        name="pack_messages",
    )(right_side.reshape(6 * NZ * ROWS, LANES), conductivity.reshape(3 * NZ * ROWS, LANES))


def turn(real, imag, cosine, sine):
    return real * cosine - imag * sine, real * sine + imag * cosine


def fill(scal_ref, tile_ref, last_ref, first_ref, sides_ref, above_ref, below_ref, basis_ref, sigma_ref):
    lanes = lane_index(NZ)
    own = lanes < 64
    low_c, low_s, high_c, high_s = (scal_ref[k] for k in range(4))
    cos_y = jnp.where(own, 1.0, jnp.where(lanes < 96, scal_ref[6], scal_ref[4]))
    sin_y = jnp.where(own, 0.0, jnp.where(lanes < 96, scal_ref[7], scal_ref[5]))

    def region(rows_ref, strips_ref, count, base, cosine, sine):
        def body(step, _):
            four, comp = step // 3, step % 3
            for j in range(4):
                x = 4 * four + j

                def pair(group):
                    row = rows_ref[group, x]
                    side = roll_lanes(strips_ref[group, four], -16 * j)
                    return jnp.where(own, row, side), roll_lanes(jnp.where(own, side, row), 64)

                real, imag, sigma = pair(comp), pair(comp + 3), pair(comp + 6)
                for b in range(2):
                    new_real, new_imag = turn(real[b], imag[b], cosine, sine)
                    basis_ref[0, 0, comp, base + x, b] = new_real
                    basis_ref[0, 1, comp, base + x, b] = new_imag
                    sigma_ref[comp, base + x, b] = level_step * sigma[b]
            return 0

        lax.fori_loop(0, 3 * count // 4, body, 0)

    region(last_ref, above_ref, HALO, 0, *turn(cos_y, sin_y, low_c, low_s))
    region(tile_ref, sides_ref, ROWS, HALO, cos_y, sin_y)
    region(first_ref, below_ref, HALO, HALO + ROWS, *turn(cos_y, sin_y, high_c, high_s))


def minus(a, b):
    return a[0] - b[0], a[1] - b[1]


def apply_step(basis_ref, sigma_ref, k, begin, end):
    layer = lax.broadcasted_iota(jnp.int32, BLOCK, 0)
    top, bottom = layer == NZ - 1, layer == 0
    zero = jnp.zeros(BLOCK, jnp.float32)

    def ahead_z(pair):
        return tuple(jnp.where(top, zero, pltpu.roll(v, NZ - 1, 0)) - v for v in pair)

    def back_z(pair):
        return tuple(jnp.where(bottom, zero, pltpu.roll(v, 1, 0)) - v for v in pair)

    def ahead_y(pair):
        return pair[1] - pair[0], roll_lanes(pair[0], -1) - pair[1]

    def back_y(pair):
        return roll_lanes(pair[1], 1) - pair[0], pair[0] - pair[1]

    def load(ri, c, x):
        return basis_ref[k, ri, c, x, 0], basis_ref[k, ri, c, x, 1]

    def curls(ri, x):
        ex, ey, ez = (load(ri, c, x) for c in range(3))
        hy = minus(ahead_z(ex), minus(load(ri, 2, x + 1), ez))
        hz = minus(minus(load(ri, 1, x + 1), ey), ahead_y(ex))
        return ey, ez, hy, hz

    def row(x, carry):
        fresh, outs = [], []
        for ri in range(2):
            ey, ez, hy, hz = curls(ri, x)
            hx = minus(ahead_y(ez), ahead_z(ey))
            old_y, old_z = carry[2 * ri], carry[2 * ri + 1]
            outs.append(
                (
                    minus(back_z(hy), back_y(hz)),
                    minus(minus(old_z, hz), back_z(hx)),
                    minus(back_y(hx), minus(old_y, hy)),
                )
            )
            fresh += [hy, hz]
        for c in range(3):
            real, imag = load(0, c, x), load(1, c, x)
            for b in range(2):
                sigma = sigma_ref[c, x, b]
                basis_ref[k + 1, 0, c, x, b] = (outs[0][c][b] + shift_real * real[b]) - sigma * imag[b]
                basis_ref[k + 1, 1, c, x, b] = (outs[1][c][b] + shift_real * imag[b]) + sigma * real[b]
        return tuple(fresh)

    count = end - begin
    size = next(n for n in (9, 8, 10, 7, 11, 12, 13, 17, 19, 1) if count % n == 0)

    def body(block, carry):
        for spot in range(size):
            carry = row(begin + block * size + spot, carry)
        return carry

    carry = curls(0, begin - 1)[2:] + curls(1, begin - 1)[2:]
    lax.fori_loop(0, count // size, body, carry)


def tree(values):
    while len(values) > 1:
        values = [a + b for a, b in zip(values[::2], values[1::2])] + values[len(values) // 2 * 2 :]
    return values[0]


def gram(basis_ref, sums_ref, gram_ref):
    def body(x, sums):
        reals, imags = [[] for _ in PAIRS], [[] for _ in PAIRS]
        for c in range(3):
            for b in range(2):
                vs = [[basis_ref[k, ri, c, x, b] for ri in range(2)] for k in range(S + 1)]
                for at, (j, k) in enumerate(PAIRS):
                    reals[at].append(vs[j][0] * vs[k][0] + vs[j][1] * vs[k][1])
                    if j != k:
                        imags[at].append(vs[j][0] * vs[k][1] - vs[j][1] * vs[k][0])
        fresh = [tree(terms) for terms in reals + imags if terms]
        return tuple(total + term for total, term in zip(sums, fresh))

    count = len(PAIRS) + sum(j != k for j, k in PAIRS)
    sums = lax.fori_loop(HALO, HALO + ROWS, body, (jnp.zeros(BLOCK, jnp.float32),) * count)
    own = lane_index(1) < 64
    sums_ref[...] = jnp.zeros((LANES, LANES), jnp.float32)
    for at, total in enumerate(sums):
        sums_ref[at : at + 1, :] = jnp.where(own, jnp.sum(total, axis=0, keepdims=True), 0.0)
    gram_ref[...] = lax.dot_general(
        jnp.ones(gram_ref.shape, jnp.float32),
        sums_ref[...],
        (((1,), (1,)), ((), ())),
        precision=lax.Precision.HIGHEST,
        preferred_element_type=jnp.float32,
    )


def cmul(a, b):
    return a[0] * b[0] - a[1] * b[1], a[0] * b[1] + a[1] * b[0]


def csub(a, b):
    return a[0] - b[0], a[1] - b[1]


def conj(a):
    return a[0], -a[1]


def coefficients(gathered_ref):
    row = jnp.broadcast_to(jnp.sum(gathered_ref[...], axis=0, keepdims=True), (8, LANES))

    def pick(at):
        return jnp.broadcast_to(row[:, at : at + 1], (8, LANES))

    entry, at = {}, len(PAIRS)
    for index, (j, k) in enumerate(PAIRS):
        if j == k:
            entry[j, k] = (pick(index), None)
        else:
            entry[j, k] = (pick(index), pick(at))
            at += 1
    unscale = [basis_scale**-k for k in range(2 * S)]
    diag = [entry[k + 1, k + 1][0] * unscale[2 * k] for k in range(S)]
    extra = (ridge_share / S) * ((diag[0] + diag[1]) + (diag[2] + diag[3]))
    diag = [d + extra for d in diag]
    low = {}
    for j in range(S):
        for k in range(j + 1, S):
            real, imag = entry[j + 1, k + 1]
            low[k, j] = (real * unscale[j + k], -imag * unscale[j + k])
    load = [(entry[0, k + 1][0] * unscale[k], -entry[0, k + 1][1] * unscale[k]) for k in range(S)]
    inverse, unit = [], {}
    for k in range(S):
        inverse.append(1.0 / diag[k])
        for i in range(k + 1, S):
            unit[i, k] = (low[i, k][0] * inverse[k], low[i, k][1] * inverse[k])
        for i in range(k + 1, S):
            real, imag = low[i, k]
            diag[i] = diag[i] - (real * real + imag * imag) * inverse[k]
            for j in range(k + 1, i):
                low[i, j] = csub(low[i, j], cmul(unit[i, k], conj(low[j, k])))
            load[i] = csub(load[i], cmul(unit[i, k], load[k]))
    answer = [None] * S
    for k in reversed(range(S)):
        value = (load[k][0] * inverse[k], load[k][1] * inverse[k])
        for j in range(k + 1, S):
            value = csub(value, cmul(conj(unit[j, k]), answer[j]))
        answer[k] = value
    return [(real[0, 0] * unscale[k], imag[0, 0] * unscale[k]) for k, (real, imag) in enumerate(answer)]


def new_residual(basis_ref, coefs, c, x, b):
    real, imag = basis_ref[0, 0, c, x, b], basis_ref[0, 1, c, x, b]
    for k in range(S):
        part = turn(basis_ref[k + 1, 0, c, x, b], basis_ref[k + 1, 1, c, x, b], *coefs[k])
        real, imag = real - part[0], imag - part[1]
    return real, imag


def solution_part(basis_ref, coefs, c, x, b):
    parts = [turn(basis_ref[k, 0, c, x, b], basis_ref[k, 1, c, x, b], *coefs[k]) for k in range(S)]
    return tuple((parts[0][ri] + parts[1][ri]) + (parts[2][ri] + parts[3][ri]) for ri in range(2))


def first_kernel(
    scal_ref, tile_ref, last_ref, first_ref, sides_ref, above_ref, below_ref,
    basis_ref, sigma_ref, gram_ref, sums_ref,
):
    fill(scal_ref, tile_ref, last_ref, first_ref, sides_ref, above_ref, below_ref, basis_ref, sigma_ref)
    for k in range(S):
        apply_step(basis_ref, sigma_ref, k, k + 1, WIDE - k - 1)
    gram(basis_ref, sums_ref, gram_ref)


def next_kernel(sweep, gathered_ref, old_ref, sigma_ref, *refs):
    if sweep == 1:
        basis_ref, part_ref, gram_ref, sums_ref = refs
        old_part = None
    else:
        old_part, basis_ref, part_ref, gram_ref, sums_ref = refs
    coefs = coefficients(gathered_ref)
    begin, end = S * sweep, WIDE - S * sweep

    def residual_row(x, _):
        for c in range(3):
            for b in range(2):
                real, imag = new_residual(old_ref, coefs, c, x, b)
                basis_ref[0, 0, c, x, b] = real
                basis_ref[0, 1, c, x, b] = imag
        return 0

    def tile_row(x, _):
        residual_row(x, 0)
        for c in range(3):
            for b in range(2):
                part = solution_part(old_ref, coefs, c, x, b)
                for ri in range(2):
                    value = part[ri] if old_part is None else part[ri] + old_part[ri, c, x - HALO, b]
                    part_ref[ri, c, x - HALO, b] = value
        return 0

    lax.fori_loop(begin, HALO, residual_row, 0)
    lax.fori_loop(HALO, HALO + ROWS, tile_row, 0)
    lax.fori_loop(HALO + ROWS, end, residual_row, 0)
    for k in range(S):
        apply_step(basis_ref, sigma_ref, k, begin + k + 1, end - k - 1)
    gram(basis_ref, sums_ref, gram_ref)


def last_kernel(gathered_ref, old_ref, old_part, part_ref, residual_ref):
    coefs = coefficients(gathered_ref)
    own = lane_index(NZ) < 64
    order = column_order(True)

    def store(out_ref, group, blocks):
        packed = [jnp.where(own, even, roll_lanes(odd, 64)) for even, odd in blocks]
        rows = reorder(jnp.concatenate(packed, axis=0), order)
        for x in range(ROWS):
            out_ref[pl.ds(group * (NZ * ROWS) + x, NZ, stride=ROWS), :] = rows[NZ * x : NZ * x + NZ]

    def body(c, _):
        residual, part = ([[], []] for _ in range(2))
        for x in range(ROWS):
            rs = [new_residual(old_ref, coefs, c, HALO + x, b) for b in range(2)]
            ps = [solution_part(old_ref, coefs, c, HALO + x, b) for b in range(2)]
            for ri in range(2):
                residual[ri].append((rs[0][ri], rs[1][ri]))
                part[ri].append(tuple(ps[b][ri] + old_part[ri, c, x, b] for b in range(2)))
        for ri in range(2):
            store(residual_ref, 3 * ri + c, residual[ri])
            store(part_ref, 3 * ri + c, part[ri])
        return 0

    lax.fori_loop(0, 3, body, 0)


BASIS = (S + 1, 2, 3, WIDE, 2) + BLOCK
PART = (2, 3, ROWS, 2) + BLOCK


def run_first(peers, *operands):
    return pl.pallas_call(
        first_kernel,
        out_shape=(
            vmem(BASIS), vmem((3, WIDE, 2) + BLOCK), jax.ShapeDtypeStruct((peers, LANES), jnp.float32)
        ),
        in_specs=[SMEM] + [VMEM] * 6,
        out_specs=(VMEM,) * 3,
        scratch_shapes=[vmem((LANES, LANES))],
        compiler_params=pltpu.CompilerParams(vmem_limit_bytes=LIMIT),
        name="first_sweep",
    )(*operands)


def run_next(peers, sweep, *operands):
    return pl.pallas_call(
        functools.partial(next_kernel, sweep),
        out_shape=(vmem(BASIS), vmem(PART), jax.ShapeDtypeStruct((peers, LANES), jnp.float32)),
        in_specs=[VMEM] * len(operands),
        out_specs=(VMEM,) * 3,
        scratch_shapes=[vmem((LANES, LANES))],
        compiler_params=pltpu.CompilerParams(vmem_limit_bytes=LIMIT),
        name="second_sweep" if sweep == 1 else "third_sweep",
    )(*operands)


def run_last(*operands):
    shape = jax.ShapeDtypeStruct((6 * NZ * ROWS, LANES), jnp.float32)
    outs = pl.pallas_call(
        last_kernel,
        out_shape=(shape, shape),
        in_specs=[VMEM] * 3,
        out_specs=(VMEM,) * 2,
        compiler_params=pltpu.CompilerParams(vmem_limit_bytes=LIMIT),
        name="last_update",
    )(*operands)
    return tuple(out.reshape(2, 3, NZ, ROWS, LANES) for out in outs)


def spread(partial):
    return lax.all_to_all(partial, ("gx", "gy"), 0, 0, tiled=True)


def phases(bloch_index):
    theta = 2.0 * math.pi * bloch_index.astype(jnp.float32) / bloch_steps
    rows = []
    for axis, angle in (("gx", theta[0]), ("gy", theta[1])):
        spot, peers = lax.axis_index(axis), lax.axis_size(axis)
        cosine, sine = jnp.cos(angle), jnp.sin(angle)
        rows += [jnp.where(spot == 0, cosine, 1.0), jnp.where(spot == 0, -sine, 0.0)]
        rows += [jnp.where(spot == peers - 1, cosine, 1.0), jnp.where(spot == peers - 1, sine, 0.0)]
    return jnp.stack(rows)


def ring(axis, step):
    peers = lax.axis_size(axis)
    return [(i, (i + step) % peers) for i in range(peers)]


def shards(right_side, conductivity, bloch_index):
    peers = lax.axis_size("gx") * lax.axis_size("gy")
    scal = phases(bloch_index)
    tile, last, first, strips = pack_messages(right_side, conductivity)
    before = lax.ppermute(strips, "gy", ring("gy", 1))
    after = lax.ppermute(strips, "gy", ring("gy", -1))
    above = lax.ppermute(last, "gx", ring("gx", 1))
    below = lax.ppermute(first, "gx", ring("gx", -1))
    from_left = (lax.broadcasted_iota(jnp.int32, strips.shape, 3) // 8) % 2 == 1
    sides = jnp.where(from_left, before, after)
    corners_above = lax.ppermute(sides[:, 1:], "gx", ring("gx", 1))
    corners_below = lax.ppermute(sides[:, :-1], "gx", ring("gx", -1))
    basis, sigma, partial = run_first(peers, scal, tile, above, below, sides, corners_above, corners_below)
    basis, part, partial = run_next(peers, 1, spread(partial), basis, sigma)
    basis, part, partial = run_next(peers, 2, spread(partial), basis, sigma, part)
    return run_last(spread(partial), basis, part)


def solution(mesh):
    in_specs = (P(None, None, None, "gx", "gy"), P(None, None, "gx", "gy"), P())
    out_specs = (P(None, None, None, "gx", "gy"), P(None, None, None, "gx", "gy"))
    return jax.shard_map(shards, mesh=mesh, in_specs=in_specs, out_specs=out_specs, check_vma=False)
```

time: 106 us -> 98.5 us (0.929)
  Pallas kernels: 32.2 us -> 27.9 us
  local copies, waits for them, and re-layouts: 4.52 us -> 2.6 us
  starting transfers between devices: 12.6 us -> 11 us
    pallas_call x4, Pallas kernels: 30.4 us -> 25.3 us  [the longest x2 11.7 us: run_next(): pl.pallas_call(functools.partial(next_kernel, sweep), out_shape=(vmem(BAS...]
    unnamed x9 -> x4, local copies, waits for them, and re-layouts: 3.84 us -> 1.92 us
    ppermute x4, starting transfers between devices: 6.36 us -> 4.81 us  [the longest x1 2.18 us: shards(): corners_below = lax.ppermute(sides[:, :-1], 'gx', ring('gx', -1))]
where the time goes in v2:
time: 98.5 us; the launch traced here: 98.2 us
  blocking collectives  47.1 us (48%)
  Pallas kernels  27.9 us (28%)
  starting transfers between devices  11 us (11%)
  waiting for transfers between devices  5.29 us (5%)
  between operations  3.61 us (4%)
  local copies, waits for them, and re-layouts  2.6 us (3%)
    all_to_all x3, blocking collectives, spread(): return lax.all_to_all(partial, ('gx', 'gy'), 0, 0, tiled=True)  47.1 us
    pallas_call x2, Pallas kernels, run_next(): pl.pallas_call(functools.partial(next_kernel, sweep), out_shape=(vmem(BAS...  11.7 us
    pallas_call x1, Pallas kernels, run_first(): pl.pallas_call(first_kernel, out_shape=(vmem(BASIS), vmem((3, WIDE, 2) +...  10.9 us
    ppermute x1, starting transfers between devices, shards(): below = lax.ppermute(first, 'gx', ring('gx', -1))  4.92 us
    ppermute x1, waiting for transfers between devices, shards(): corners_below = lax.ppermute(sides[:, :-1], 'gx', ring('gx', -1))  4.23 us
    pallas_call x1, Pallas kernels, pack_messages(): pl.pallas_call(pack_kernel, out_shape=(vmem(rows), vmem(edge), vmem(edge)...  2.69 us
    pallas_call x1, Pallas kernels, run_last(): pl.pallas_call(last_kernel, out_shape=(shape, shape), in_specs=[VMEM] * 3...  2.64 us
    ppermute x1, starting transfers between devices, shards(): corners_below = lax.ppermute(sides[:, :-1], 'gx', ring('gx', -1))  2.18 us
  transfers between devices with their start and end apart: 6, of which 2 were waited for; matrix products, arithmetic and copies ran while one was open for 1% of the time, Pallas kernels for 0%

profile of v2, /device:TPU:1, one launch (start us, length us, event | category | flops | bytes accessed | tf_op | source)
XLA Modules:
  0.0 98.2 jit_solution(11587070973849632467)
XLA Ops:
  0.6 0.0 copy-start
  0.6 1.0 %copy-done = f32[2,3,8,16,128]{4,3,2,1,0:T(8,128)S(1)} copy-done((f32[2,3,8,16,128]{4,3,2,1,0:T(8,128)S(1)}, f32[2,3,8,16,128]{4,3,2,1,0:T(8,128)}, u32[]{:S(2)}) %copy-start) | copy-done | bytes 393240
  1.6 0.0 copy-start.1
  1.6 0.9 copy-done.1
  2.6 2.7 %pack_messages.1 = (f32[9,16,8,128]{3,2,1,0:T(8,128)S(1)}, f32[9,12,8,128]{3,2,1,0:T(8,128)S(1)}, f32[9,12,8,128]{3,2,1,0:T(8,128)S(1)}, f32[9,4,8,128]{3,2,1,0:T(8,128)S(1)}) custom-call(f32[768,128]{1,0:T(8,128)S(1)} %bitcast.28, f32[384,128]{1,0:T(8,128)S(1)} %bitcast.32), custom_call_target="tpu_custom_call" | custom-call | tf_op jit(solution)/shard_map/pack_messages/pallas_call | solution.py:106
  5.2 1.4 %collective-permute-start.3 = (f32[9,4,8,128]{3,2,1,0:T(8,128)S(1)}, f32[9,4,8,128]{3,2,1,0:T(8,128)S(1)}, u32[]{:S(2)}, u32[]{:S(2)}) collective-permute-start(f32[9,4,8,128]{3,2,1,0:T(8,128)S(1)} %get-tuple-element.20), channel_id=1, source_target_pairs={{0,7},{1,0},{2,1},{3,2},{4,3},{5,4},{6,5},{7,6},{8,15},{9,8},{10,9... | collective-permute-start | bytes 442376 | tf_op jit(solution)/shard_map/ppermute | solution.py:460
  6.7 1.2 %collective-permute-start.2 = (f32[9,4,8,128]{3,2,1,0:T(8,128)S(1)}, f32[9,4,8,128]{3,2,1,0:T(8,128)S(1)}, u32[]{:S(2)}, u32[]{:S(2)}) collective-permute-start(f32[9,4,8,128]{3,2,1,0:T(8,128)S(1)} %get-tuple-element.20), channel_id=1, source_target_pairs={{0,1},{1,2},{2,3},{3,4},{4,5},{5,6},{6,7},{7,0},{8,9},{9,10},{10,1... | collective-permute-start | bytes 442376 | tf_op jit(solution)/shard_map/ppermute | solution.py:459
  7.9 1.3 %collective-permute-start = (f32[9,12,8,128]{3,2,1,0:T(8,128)S(1)}, f32[9,12,8,128]{3,2,1,0:T(8,128)S(1)}, u32[]{:S(2)}, u32[]{:S(2)}) collective-permute-start(f32[9,12,8,128]{3,2,1,0:T(8,128)S(1)} %get-tuple-element.18), channel_id=1, source_target_pairs={{0,8},{8,16},{16,24},{24,32},{32,40},{40,48},{48,56},{56,64},{64,7... | collective-permute-start | bytes 1327112 | tf_op jit(solution)/shard_map/ppermute | solution.py:461
  9.2 4.9 %collective-permute-start.1 = (f32[9,12,8,128]{3,2,1,0:T(8,128)S(1)}, f32[9,12,8,128]{3,2,1,0:T(8,128)S(1)}, u32[]{:S(2)}, u32[]{:S(2)}) collective-permute-start(f32[9,12,8,128]{3,2,1,0:T(8,128)S(1)} %get-tuple-element.19), channel_id=1, source_target_pairs={{0,120},{8,0},{16,8},{24,16},{32,24},{40,32},{48,40},{56,48},{64,5... | collective-permute-start | bytes 1327112 | tf_op jit(solution)/shard_map/ppermute | solution.py:462
  14.1 0.7 convert_multiply_fusion
  14.8 0.0 collective-permute-done.3
  14.8 0.0 collective-permute-done.2
  14.8 2.2 %collective-permute-start.5 = (f32[9,3,8,128]{3,2,1,0:T(8,128)S(1)}, f32[9,3,8,128]{3,2,1,0:T(8,128)S(1)}, u32[]{:S(2)}, u32[]{:S(2)}) collective-permute-start(f32[9,3,8,128]{3,2,1,0:T(8,128)S(1)} %get-tuple-element.32), channel_id=1, source_target_pairs={{0,120},{8,0},{16,8},{24,16},{32,24},{40,32},{48,40},{56,48},{64,5... | collective-permute-start | bytes 331784 | tf_op jit(solution)/shard_map/ppermute | solution.py:466
  17.0 0.0 collective-permute-start.4
  17.0 0.6 fusion.4
  20.5 0.1 stack.35.scal_ref
  20.6 4.2 %collective-permute-done.5.below_ref = f32[9,3,8,128]{3,2,1,0:T(8,128)S(1)} collective-permute-done((f32[9,3,8,128]{3,2,1,0:T(8,128)S(1)}, f32[9,3,8,128]{3,2,1,0:T(8,128)S(1)}, u32[]{:S(2)}, u32[]{:S(2)}) %collective-permute-start.5) | collective-permute-done | bytes 110624 | tf_op jit(solution)/shard_map/ppermute | solution.py:466
  24.8 1.0 %collective-permute-done.4.above_ref = f32[9,3,8,128]{3,2,1,0:T(8,128)S(1)} collective-permute-done((f32[9,3,8,128]{3,2,1,0:T(8,128)S(1)}, f32[9,3,8,128]{3,2,1,0:T(8,128)S(1)}, u32[]{:S(2)}, u32[]{:S(2)}) %collective-permute-start.4) | collective-permute-done | bytes 110624 | tf_op jit(solution)/shard_map/ppermute | solution.py:465
  25.9 0.0 collective-permute-done.last_ref
  25.9 0.0 collective-permute-done.1.first_ref
  25.9 10.9 %first_sweep.1 = (f32[5,2,3,40,2,8,128]{6,5,4,3,2,1,0:T(8,128)S(1)}, f32[3,40,2,8,128]{4,3,2,1,0:T(8,128)S(1)}, f32[128,128]{1,0:T(8,128)S(1)}) custom-call(f32[8]{0:T(128)S(1)} %stack.35.scal_ref, f32[9,16,8,128]{3,2,1,0:T(8,128)S(1)} %get-tuple-element.17.tile_ref, f32[9,12,8,128]{3,2,1,0:T(8,128)S(1)} %collective-permute-done.last_ref, ...), custom_call_target="tpu_custom_call" | custom-call | tf_op jit(solution)/shard_map/first_sweep/pallas_call | solution.py:397
  36.8 19.2 %all_to_all.33 = f32[128,1,128]{2,1,0:T(1,128)S(1)} all-to-all(f32[128,1,128]{2,1,0:T(1,128)S(1)} %bitcast.33), channel_id=1, replica_groups=mesh['gx'=16,'gy'=8] {'gx','gy'}, dimensions={0} | all-to-all | bytes 131072 | tf_op jit(solution)/shard_map/all_to_all | solution.py:436
  56.0 6.4 %second_sweep.1 = (f32[5,2,3,40,2,8,128]{6,5,4,3,2,1,0:T(8,128)S(1)}, f32[2,3,16,2,8,128]{5,4,3,2,1,0:T(8,128)S(1)}, f32[128,128]{1,0:T(8,128)S(1)}) custom-call(f32[128,128]{1,0:T(8,128)S(1)} %bitcast.30, f32[5,2,3,40,2,8,128]{6,5,4,3,2,1,0:T(8,128)S(1)} %get-tuple-element.22.old_ref, f32[3,40,2,8,128]{4,3,2,1,0:T(8,128)S(1)} %get-tuple-element.23.sigma_ref), custom_call_target="tpu_custom_call" | custom-call | tf_op jit(solution)/shard_map/second_sweep/pallas_call | solution.py:411
  62.4 13.9 %all_to_all.34 = f32[128,1,128]{2,1,0:T(1,128)S(1)} all-to-all(f32[128,1,128]{2,1,0:T(1,128)S(1)} %bitcast.35), channel_id=1, replica_groups=mesh['gx'=16,'gy'=8] {'gx','gy'}, dimensions={0} | all-to-all | bytes 131072 | tf_op jit(solution)/shard_map/all_to_all | solution.py:436
  76.3 5.3 %third_sweep.1 = (f32[5,2,3,40,2,8,128]{6,5,4,3,2,1,0:T(8,128)S(1)}, f32[2,3,16,2,8,128]{5,4,3,2,1,0:T(8,128)S(1)}, f32[128,128]{1,0:T(8,128)S(1)}) custom-call(f32[128,128]{1,0:T(8,128)S(1)} %bitcast.29, f32[5,2,3,40,2,8,128]{6,5,4,3,2,1,0:T(8,128)S(1)} %get-tuple-element.25.old_ref, f32[3,40,2,8,128]{4,3,2,1,0:T(8,128)S(1)} %get-tuple-element.23.sigma_ref, ...), custom_call_target="tpu_custom_call" | custom-call | tf_op jit(solution)/shard_map/third_sweep/pallas_call | solution.py:411
  81.7 13.9 %all_to_all.35 = f32[128,1,128]{2,1,0:T(1,128)S(1)} all-to-all(f32[128,1,128]{2,1,0:T(1,128)S(1)} %bitcast.34), channel_id=1, replica_groups=mesh['gx'=16,'gy'=8] {'gx','gy'}, dimensions={0} | all-to-all | bytes 131072 | tf_op jit(solution)/shard_map/all_to_all | solution.py:436
  95.6 2.6 %last_update.1 = (f32[768,128]{1,0:T(8,128)}, f32[768,128]{1,0:T(8,128)}) custom-call(f32[128,128]{1,0:T(8,128)S(1)} %bitcast.31, f32[5,2,3,40,2,8,128]{6,5,4,3,2,1,0:T(8,128)S(1)} %get-tuple-element.28.old_ref, f32[2,3,16,2,8,128]{5,4,3,2,1,0:T(8,128)S(1)} %get-tuple-element.29.old_part), custom_call_target="tpu_custom_call" | custom-call | tf_op jit(solution)/shard_map/last_update/pallas_call | solution.py:424
  (4 shorter events, 0.1 us)
Async XLA Ops:
  0.6 1.0 %copy-start = (f32[2,3,8,16,128]{4,3,2,1,0:T(8,128)S(1)}, f32[2,3,8,16,128]{4,3,2,1,0:T(8,128)}, u32[]{:S(2)}) copy-start(f32[2,3,8,16,128]{4,3,2,1,0:T(8,128)} %param.3) | copy-start | bytes 1179652
  1.6 0.9 copy-start.1
  5.2 9.5 %collective-permute-start.3 = (f32[9,4,8,128]{3,2,1,0:T(8,128)S(1)}, f32[9,4,8,128]{3,2,1,0:T(8,128)S(1)}, u32[]{:S(2)}, u32[]{:S(2)}) collective-permute-start(f32[9,4,8,128]{3,2,1,0:T(8,128)S(1)} %get-tuple-element.20), channel_id=1, source_target_pairs={{0,7},{1,0},{2,1},{3,2},{4,3},{5,4},{6,5},{7,6},{8,15},{9,8},{10,9... | collective-permute-start | bytes 442376 | tf_op jit(solution)/shard_map/ppermute | solution.py:460
  6.7 8.1 %collective-permute-start.2 = (f32[9,4,8,128]{3,2,1,0:T(8,128)S(1)}, f32[9,4,8,128]{3,2,1,0:T(8,128)S(1)}, u32[]{:S(2)}, u32[]{:S(2)}) collective-permute-start(f32[9,4,8,128]{3,2,1,0:T(8,128)S(1)} %get-tuple-element.20), channel_id=1, source_target_pairs={{0,1},{1,2},{2,3},{3,4},{4,5},{5,6},{6,7},{7,0},{8,9},{9,10},{10,1... | collective-permute-start | bytes 442376 | tf_op jit(solution)/shard_map/ppermute | solution.py:459
  7.9 18.0 %collective-permute-start = (f32[9,12,8,128]{3,2,1,0:T(8,128)S(1)}, f32[9,12,8,128]{3,2,1,0:T(8,128)S(1)}, u32[]{:S(2)}, u32[]{:S(2)}) collective-permute-start(f32[9,12,8,128]{3,2,1,0:T(8,128)S(1)} %get-tuple-element.18), channel_id=1, source_target_pairs={{0,8},{8,16},{16,24},{24,32},{32,40},{40,48},{48,56},{56,64},{64,7... | collective-permute-start | bytes 1327112 | tf_op jit(solution)/shard_map/ppermute | solution.py:461
  9.2 16.7 %collective-permute-start.1 = (f32[9,12,8,128]{3,2,1,0:T(8,128)S(1)}, f32[9,12,8,128]{3,2,1,0:T(8,128)S(1)}, u32[]{:S(2)}, u32[]{:S(2)}) collective-permute-start(f32[9,12,8,128]{3,2,1,0:T(8,128)S(1)} %get-tuple-element.19), channel_id=1, source_target_pairs={{0,120},{8,0},{16,8},{24,16},{32,24},{40,32},{48,40},{56,48},{64,5... | collective-permute-start | bytes 1327112 | tf_op jit(solution)/shard_map/ppermute | solution.py:462
  14.8 10.0 %collective-permute-start.5 = (f32[9,3,8,128]{3,2,1,0:T(8,128)S(1)}, f32[9,3,8,128]{3,2,1,0:T(8,128)S(1)}, u32[]{:S(2)}, u32[]{:S(2)}) collective-permute-start(f32[9,3,8,128]{3,2,1,0:T(8,128)S(1)} %get-tuple-element.32), channel_id=1, source_target_pairs={{0,120},{8,0},{16,8},{24,16},{32,24},{40,32},{48,40},{56,48},{64,5... | collective-permute-start | bytes 331784 | tf_op jit(solution)/shard_map/ppermute | solution.py:466
  17.0 8.9 %collective-permute-start.4 = (f32[9,3,8,128]{3,2,1,0:T(8,128)S(1)}, f32[9,3,8,128]{3,2,1,0:T(8,128)S(1)}, u32[]{:S(2)}, u32[]{:S(2)}) collective-permute-start(f32[9,3,8,128]{3,2,1,0:T(8,128)S(1)} %get-tuple-element.33), channel_id=1, source_target_pairs={{0,8},{8,16},{16,24},{24,32},{32,40},{40,48},{48,56},{56,64},{64,7... | collective-permute-start | bytes 331784 | tf_op jit(solution)/shard_map/ppermute | solution.py:465

commit v3 on v2

--- a/solution.py
+++ b/solution.py
@@ -3,6 +3,7 @@
 
 import jax
 import jax.numpy as jnp
+import numpy as np
 from jax import lax
 from jax.experimental import pallas as pl
 from jax.experimental.pallas import tpu as pltpu
@@ -28,6 +29,14 @@
 LIMIT = 16 * 1024 * 1024
 PAIRS = [(j, k) for j in range(S + 1) for k in range(j, S + 1) if k > 0]
 BLOCK = (NZ, LANES)
+
+DEGREE = 2 * S
+CENTER = (6.25, 0.75)
+BETA = 8.5
+SPREAD_MAX = 3.0e4
+BIG_PAIRS = [(a, a) for a in range(DEGREE + 1)] + [(a, b) for a in range(DEGREE + 1) for b in range(a + 1, DEGREE + 1)]
+BIG_COUNT = len(BIG_PAIRS) + DEGREE * (DEGREE + 1) // 2
+ALL_PAIRS = [(0, 0)] + PAIRS
 
 
 def vmem(shape):
@@ -155,7 +164,9 @@
     return a[0] - b[0], a[1] - b[1]
 
 
-def apply_step(basis_ref, sigma_ref, k, begin, end):
+def apply_step(basis_ref, sigma_ref, k, begin, end, slots=None):
+    before, here, there = (None, k, k + 1) if slots is None else slots
+    beta = 0.0 if k == 0 else 2 * BETA if k == 1 else BETA
     layer = lax.broadcasted_iota(jnp.int32, BLOCK, 0)
     top, bottom = layer == NZ - 1, layer == 0
     zero = jnp.zeros(BLOCK, jnp.float32)
@@ -173,7 +184,7 @@
         return roll_lanes(pair[1], 1) - pair[0], pair[0] - pair[1]
 
     def load(ri, c, x):
-        return basis_ref[k, ri, c, x, 0], basis_ref[k, ri, c, x, 1]
+        return basis_ref[here, ri, c, x, 0], basis_ref[here, ri, c, x, 1]
 
     def curls(ri, x):
         ex, ey, ez = (load(ri, c, x) for c in range(3))
@@ -199,8 +210,16 @@
             real, imag = load(0, c, x), load(1, c, x)
             for b in range(2):
                 sigma = sigma_ref[c, x, b]
-                basis_ref[k + 1, 0, c, x, b] = (outs[0][c][b] + shift_real * real[b]) - sigma * imag[b]
-                basis_ref[k + 1, 1, c, x, b] = (outs[1][c][b] + shift_real * imag[b]) + sigma * real[b]
+                shift = shift_real
+                if slots is not None:
+                    sigma, shift = sigma - CENTER[1], shift_real - CENTER[0]
+                new_real = (outs[0][c][b] + shift * real[b]) - sigma * imag[b]
+                new_imag = (outs[1][c][b] + shift * imag[b]) + sigma * real[b]
+                if slots is not None and k > 0:
+                    new_real = new_real - beta * basis_ref[before, 0, c, x, b]
+                    new_imag = new_imag - beta * basis_ref[before, 1, c, x, b]
+                basis_ref[there, 0, c, x, b] = new_real
+                basis_ref[there, 1, c, x, b] = new_imag
         return tuple(fresh)
 
     count = end - begin
@@ -240,6 +259,10 @@
     sums_ref[...] = jnp.zeros((LANES, LANES), jnp.float32)
     for at, total in enumerate(sums):
         sums_ref[at : at + 1, :] = jnp.where(own, jnp.sum(total, axis=0, keepdims=True), 0.0)
+    total_lanes(sums_ref, gram_ref)
+
+
+def total_lanes(sums_ref, gram_ref):
     gram_ref[...] = lax.dot_general(
         jnp.ones(gram_ref.shape, jnp.float32),
         sums_ref[...],
@@ -261,19 +284,7 @@
     return a[0], -a[1]
 
 
-def coefficients(gathered_ref):
-    row = jnp.broadcast_to(jnp.sum(gathered_ref[...], axis=0, keepdims=True), (8, LANES))
-
-    def pick(at):
-        return jnp.broadcast_to(row[:, at : at + 1], (8, LANES))
-
-    entry, at = {}, len(PAIRS)
-    for index, (j, k) in enumerate(PAIRS):
-        if j == k:
-            entry[j, k] = (pick(index), None)
-        else:
-            entry[j, k] = (pick(index), pick(at))
-            at += 1
+def solve(entry):
     unscale = [basis_scale**-k for k in range(2 * S)]
     diag = [entry[k + 1, k + 1][0] * unscale[2 * k] for k in range(S)]
     extra = (ridge_share / S) * ((diag[0] + diag[1]) + (diag[2] + diag[3]))
@@ -301,7 +312,23 @@
         for j in range(k + 1, S):
             value = csub(value, cmul(conj(unit[j, k]), answer[j]))
         answer[k] = value
-    return [(real[0, 0] * unscale[k], imag[0, 0] * unscale[k]) for k, (real, imag) in enumerate(answer)]
+    return [(real * unscale[k], imag * unscale[k]) for k, (real, imag) in enumerate(answer)]
+
+
+def coefficients(gathered_ref):
+    row = jnp.broadcast_to(jnp.sum(gathered_ref[...], axis=0, keepdims=True), BLOCK)
+
+    def pick(at):
+        return jnp.broadcast_to(row[:, at : at + 1], BLOCK)
+
+    entry, at = {}, len(PAIRS)
+    for index, (j, k) in enumerate(PAIRS):
+        if j == k:
+            entry[j, k] = (pick(index), None)
+        else:
+            entry[j, k] = (pick(index), pick(at))
+            at += 1
+    return [(real[0, 0], imag[0, 0]) for real, imag in solve(entry)]
 
 
 def new_residual(basis_ref, coefs, c, x, b):
@@ -389,6 +416,264 @@
     lax.fori_loop(0, 3, body, 0)
 
 
+def two_sum(a, b):
+    total = a + b
+    other = total - a
+    return total, (a - (total - other)) + (b - other)
+
+
+def quick_sum(a, b):
+    total = a + b
+    return total, b - (total - a)
+
+
+def pair_sum(a, b):
+    total, error = two_sum(a[0], b[0])
+    return quick_sum(total, error + (a[1] + b[1]))
+
+
+def halves(a):
+    scaled = a * 4097.0
+    high = scaled - (scaled - a)
+    return high, a - high
+
+
+def two_product(a, b):
+    product = a * b
+    (ah, al), (bh, bl) = halves(a), halves(b)
+    return product, ((ah * bh - product) + ah * bl + al * bh) + al * bl
+
+
+def pair_product(a, b):
+    product, error = two_product(a[0], b[0])
+    return quick_sum(product, error + (a[0] * b[1] + a[1] * b[0]))
+
+
+def negative(a):
+    return -a[0], -a[1]
+
+
+def choose(mask, a, b):
+    return jnp.where(mask, a[0], b[0]), jnp.where(mask, a[1], b[1])
+
+
+def all_lanes(value):
+    for step in (64, 32, 16, 8, 4, 2, 1):
+        value = pair_sum(value, tuple(roll_lanes(part, step) for part in value))
+    return value
+
+
+def all_devices(gathered_ref):
+    rows = gathered_ref.shape[0] // 2
+    value = two_sum(gathered_ref[:rows, :], gathered_ref[rows:, :])
+    while rows > 8:
+        rows = rows // 2
+        value = pair_sum(tuple(v[:rows] for v in value), tuple(v[rows:] for v in value))
+    step = rows // 2
+    while step:
+        value = pair_sum(value, tuple(pltpu.roll(v, step, 0) for v in value))
+        step = step // 2
+    return tuple(jnp.broadcast_to(v[:1], BLOCK) for v in value)
+
+
+def constants():
+    size = DEGREE + 1
+    step = np.zeros((size + 1, size), np.complex128)
+    for k in range(size):
+        step[k, k] = complex(*CENTER)
+        step[k + 1, k] = 1.0
+        if k:
+            step[k - 1, k] = BETA * (2 if k == 1 else 1)
+    power = [np.eye(size)[0].astype(np.complex128)]
+    for _ in range(S):
+        power.append(step[:size] @ power[-1])
+    lanes = [(a, b, 0) for a, b in BIG_PAIRS] + [(a, b, 1) for a, b in BIG_PAIRS if a != b]
+    table = np.zeros((32, LANES), np.float64)
+    pick_a, pick_b = np.zeros((LANES, LANES)), np.zeros((LANES, LANES))
+    for lane, (a, b, imag) in enumerate(lanes):
+        pick_a[a, lane] = pick_b[b, lane] = 1
+        for row, (j, k) in enumerate(ALL_PAIRS):
+            first = np.conj(power[j][a]) * power[k][b]
+            second = np.conj(power[j][b]) * power[k][a]
+            total = first if a == b else 1j * (first - second) if imag else first + second
+            table[row, lane], table[16 + row, lane] = total.real, total.imag
+    high = table.astype(np.float32)
+    low = (table - high).astype(np.float32)
+    rows = np.zeros((16, LANES), np.float32)
+    for k in range(S + 1):
+        rows[k, :size], rows[8 + k, :size] = power[k].real, power[k].imag
+    picks = np.stack([pick_a, pick_b]).astype(jnp.bfloat16)
+    select = np.zeros((2, 32, 32))
+    for row, pair in enumerate(ALL_PAIRS):
+        for side in range(2):
+            select[side, row, pair[side]] = select[side, 16 + row, 16 + pair[side]] = 1
+    return np.concatenate([high, low, rows]), picks, select.astype(jnp.bfloat16)
+
+
+def pick_rows(select, value):
+    first = value.astype(jnp.bfloat16)
+    rest = value - first.astype(jnp.float32)
+    second = rest.astype(jnp.bfloat16)
+    third = (rest - second.astype(jnp.float32)).astype(jnp.bfloat16)
+    parts = [jnp.dot(select, part, preferred_element_type=jnp.float32) for part in (first, second, third)]
+    return (parts[0] + parts[1]) + parts[2]
+
+
+def entries(rows):
+    return {pair: (rows[p : p + 1], rows[16 + p : 17 + p]) for p, pair in enumerate(ALL_PAIRS)}
+
+
+def both_iterations(gathered_ref, table_ref, picks_ref, select_ref):
+    sums = all_devices(gathered_ref)
+    lane = lane_index(1)
+    four = tuple(jnp.concatenate([v] * 4, axis=0) for v in sums)
+    table = table_ref[0:32, :], table_ref[32:64, :]
+    second = entries(all_lanes(pair_product(table, four))[0])
+    y = solve(second)
+    power = [(table_ref[64 + k : 65 + k, :], table_ref[72 + k : 73 + k, :]) for k in range(S + 1)]
+    residual = power[0]
+    for k in range(S):
+        residual = csub(residual, cmul(y[k], power[k + 1]))
+    down = jnp.where(lane == 0, 2 * BETA, jnp.where(lane < DEGREE, BETA, 0.0))
+    up = jnp.where((lane > 0) & (lane <= DEGREE), 1.0, 0.0)
+    chain = [residual]
+    for _ in range(S):
+        p = chain[-1]
+        side = [down * roll_lanes(v, -1) + up * roll_lanes(v, 1) for v in p]
+        turned = cmul(CENTER, p)
+        chain.append((turned[0] + side[0], turned[1] + side[1]))
+    gap = jnp.zeros((16 - len(chain), LANES), jnp.float32)
+    stack = jnp.concatenate([v[0] for v in chain] + [gap] + [v[1] for v in chain] + [gap], axis=0)
+    at_a, at_b = reorder(stack, picks_ref[0]), reorder(stack, picks_ref[1])
+    aj, ak = pick_rows(select_ref[0], at_a), pick_rows(select_ref[1], at_a)
+    bj, bk = pick_rows(select_ref[0], at_b), pick_rows(select_ref[1], at_b)
+
+    def product(left, right):
+        (lr, li), (rr, ri) = (left[:16], left[16:]), (right[:16], right[16:])
+        real = pair_sum(two_product(lr, rr), two_product(li, ri))
+        return real, pair_sum(two_product(lr, ri), negative(two_product(li, rr)))
+
+    lanes16 = lane_index(16)
+    whole = len(BIG_PAIRS)
+    sign = jnp.where(lanes16 <= DEGREE, 0.0, jnp.where(lanes16 < whole, 1.0, -1.0))
+    first, other = product(aj, bk), product(bj, ak)
+    real, imag = (pair_sum(f, (sign * o[0], sign * o[1])) for f, o in zip(first, other))
+    mixed = lanes16 >= whole
+    parts = choose(mixed, negative(imag), real), choose(mixed, real, imag)
+    rows = tuple(jnp.concatenate([parts[0][n], parts[1][n]], axis=0) for n in range(2))
+    third = entries(all_lanes(pair_product(rows, four))[0])
+    z = solve(third)
+
+    norms = jnp.sqrt(jnp.where(lane <= DEGREE, sums[0][:1], 0.0))
+    sizes = [jnp.abs(v[0]) + jnp.abs(v[1]) for v in chain + power]
+    sizes = jnp.concatenate([size * norms for size in sizes], axis=0)
+    for step in (64, 32, 16, 8, 4, 2, 1):
+        sizes = sizes + roll_lanes(sizes, step)
+    spread = None
+    for at, source in ((0, third), (S + 1, second)):
+        for k in range(S + 1):
+            size = sizes[at + k : at + k + 1]
+            ratio = size * size / source[k, k][0]
+            spread = ratio if spread is None else jnp.where(ratio < spread, spread, ratio)
+    part = None
+    for k in range(S):
+        term = cmul(y[k], power[k])
+        other = cmul(z[k], chain[k])
+        term = (term[0] + other[0], term[1] + other[1])
+        part = term if part is None else (part[0] + term[0], part[1] + term[1])
+        residual = csub(residual, cmul(z[k], chain[k + 1]))
+    return part, residual, spread
+
+
+def packed(even, odd):
+    return jnp.where(lane_index(NZ) < 64, even, roll_lanes(odd, 64))
+
+
+def wide_kernel(gathered_ref, old_ref, sigma_ref, tile_ref, part_ref, gram_ref, basis_ref, acc_ref, sums_ref):
+    coefs = coefficients(gathered_ref)
+    begin, end = S, WIDE - S
+
+    def residual_row(x, _):
+        for c in range(3):
+            for b in range(2):
+                real, imag = new_residual(old_ref, coefs, c, x, b)
+                basis_ref[0, 0, c, x, b] = real
+                basis_ref[0, 1, c, x, b] = imag
+        return 0
+
+    def tile_row(x, _):
+        residual_row(x, 0)
+        for c in range(3):
+            even, odd = (solution_part(old_ref, coefs, c, x, b) for b in range(2))
+            for ri in range(2):
+                part_ref[ri, c, x - HALO] = packed(even[ri], odd[ri])
+        return 0
+
+    lax.fori_loop(begin, HALO, residual_row, 0)
+    lax.fori_loop(HALO, HALO + ROWS, tile_row, 0)
+    lax.fori_loop(HALO + ROWS, end, residual_row, 0)
+    for k in range(DEGREE):
+        apply_step(basis_ref, sigma_ref, k, begin + k + 1, end - k - 1, (k - 1, k, k + 1))
+    acc_ref[...] = jnp.zeros(acc_ref.shape, jnp.float32)
+
+    def gram_row(x, _):
+        for c in range(3):
+            vs = []
+            for k in range(DEGREE + 1):
+                vs.append([packed(basis_ref[k, ri, c, x, 0], basis_ref[k, ri, c, x, 1]) for ri in range(2)])
+                for ri in range(2):
+                    tile_ref[k, ri, c, x - HALO] = vs[k][ri]
+            at = len(BIG_PAIRS)
+            for index, (j, k) in enumerate(BIG_PAIRS):
+                acc_ref[index] += vs[j][0] * vs[k][0] + vs[j][1] * vs[k][1]
+                if j != k:
+                    acc_ref[at] += vs[j][0] * vs[k][1] - vs[j][1] * vs[k][0]
+                    at += 1
+        return 0
+
+    lax.fori_loop(HALO, HALO + ROWS, gram_row, 0)
+    sums_ref[...] = jnp.zeros((LANES, LANES), jnp.float32)
+    for at in range(BIG_COUNT):
+        sums_ref[at : at + 1, :] = jnp.sum(acc_ref[at], axis=0, keepdims=True)
+    total_lanes(sums_ref, gram_ref)
+
+
+def end_kernel(
+    gathered_ref, table_ref, picks_ref, select_ref, tile_ref, old_part, part_ref, residual_ref, spread_ref, coef_ref
+):
+    part, residual, spread = both_iterations(gathered_ref, table_ref, picks_ref, select_ref)
+    spread_ref[...] = jnp.broadcast_to(spread, BLOCK)
+    for a in range(DEGREE + 1):
+        for n, value in enumerate(part + residual):
+            coef_ref[4 * a + n] = jnp.broadcast_to(value[:, a : a + 1], BLOCK)
+    order = column_order(True)
+
+    def body(c, _):
+        sums = [[] for _ in range(4)]
+        for x in range(ROWS):
+            totals = [old_part[0, c, x], old_part[1, c, x], None, None]
+            for a in range(DEGREE + 1):
+                real, imag = tile_ref[a, 0, c, x], tile_ref[a, 1, c, x]
+                for out in range(2):
+                    if out == 0 and a == DEGREE:
+                        continue
+                    term = turn(real, imag, coef_ref[4 * a + 2 * out], coef_ref[4 * a + 2 * out + 1])
+                    for ri in range(2):
+                        old = totals[2 * out + ri]
+                        totals[2 * out + ri] = term[ri] if old is None else old + term[ri]
+            for n in range(4):
+                sums[n].append(totals[n])
+        for n in range(4):
+            rows = reorder(jnp.concatenate(sums[n], axis=0), order)
+            out_ref = residual_ref if n >= 2 else part_ref
+            group = 3 * (n % 2) + c
+            for x in range(ROWS):
+                out_ref[pl.ds(group * (NZ * ROWS) + x, NZ, stride=ROWS), :] = rows[NZ * x : NZ * x + NZ]
+        return 0
+
+    lax.fori_loop(0, 3, body, 0)
+
+
 BASIS = (S + 1, 2, 3, WIDE, 2) + BLOCK
 PART = (2, 3, ROWS, 2) + BLOCK
 
@@ -419,6 +704,39 @@
     )(*operands)
 
 
+def run_wide(peers, *operands):
+    return pl.pallas_call(
+        wide_kernel,
+        out_shape=(
+            vmem((DEGREE + 1, 2, 3, ROWS) + BLOCK),
+            vmem((2, 3, ROWS) + BLOCK),
+            jax.ShapeDtypeStruct((peers, LANES), jnp.float32),
+        ),
+        in_specs=[VMEM] * 3,
+        out_specs=(VMEM,) * 3,
+        scratch_shapes=[
+            vmem((DEGREE + 1, 2, 3, WIDE, 2) + BLOCK), vmem((BIG_COUNT,) + BLOCK), vmem((LANES, LANES))
+        ],
+        compiler_params=pltpu.CompilerParams(vmem_limit_bytes=24 * 1024 * 1024),
+        name="second_third_basis",
+    )(*operands)
+
+
+def run_end(*operands):
+    shape = jax.ShapeDtypeStruct((6 * NZ * ROWS, LANES), jnp.float32)
+    tables = [jnp.asarray(table) for table in constants()]
+    part, residual, spread = pl.pallas_call(
+        end_kernel,
+        out_shape=(shape, shape, jax.ShapeDtypeStruct(BLOCK, jnp.float32)),
+        in_specs=[VMEM] * 6,
+        out_specs=(VMEM,) * 3,
+        scratch_shapes=[vmem((4 * (DEGREE + 1),) + BLOCK)],
+        compiler_params=pltpu.CompilerParams(vmem_limit_bytes=LIMIT),
+        name="second_third_update",
+    )(operands[0], *tables, *operands[1:])
+    return tuple(out.reshape(2, 3, NZ, ROWS, LANES) for out in (part, residual)) + (spread[0, 0],)
+
+
 def run_last(*operands):
     shape = jax.ShapeDtypeStruct((6 * NZ * ROWS, LANES), jnp.float32)
     outs = pl.pallas_call(
@@ -452,7 +770,7 @@
     return [(i, (i + step) % peers) for i in range(peers)]
 
 
-def shards(right_side, conductivity, bloch_index):
+def first_sweep(right_side, conductivity, bloch_index):
     peers = lax.axis_size("gx") * lax.axis_size("gy")
     scal = phases(bloch_index)
     tile, last, first, strips = pack_messages(right_side, conductivity)
@@ -465,9 +783,30 @@
     corners_above = lax.ppermute(sides[:, 1:], "gx", ring("gx", 1))
     corners_below = lax.ppermute(sides[:, :-1], "gx", ring("gx", -1))
     basis, sigma, partial = run_first(peers, scal, tile, above, below, sides, corners_above, corners_below)
-    basis, part, partial = run_next(peers, 1, spread(partial), basis, sigma)
+    return peers, basis, sigma, spread(partial)
+
+
+def three_reductions(*operands):
+    peers, basis, sigma, gathered = first_sweep(*operands)
+    basis, part, partial = run_next(peers, 1, gathered, basis, sigma)
     basis, part, partial = run_next(peers, 2, spread(partial), basis, sigma, part)
     return run_last(spread(partial), basis, part)
+
+
+def two_reductions(*operands):
+    peers, basis, sigma, gathered = first_sweep(*operands)
+    tile, part, partial = run_wide(peers, gathered, basis, sigma)
+    return run_end(spread(partial), tile, part)
+
+
+def shards(*operands):
+    part, residual, cancelled = two_reductions(*operands)
+    state = (jnp.logical_not(cancelled < SPREAD_MAX), part, residual)
+
+    def again(_):
+        return (jnp.array(False),) + three_reductions(*operands)
+
+    return lax.while_loop(lambda state: state[0], again, state)[1:]
 
 
 def solution(mesh):

time: 98.5 us -> 87.2 us (0.89)
  blocking collectives: 47.1 us -> 33.9 us
  waiting for transfers between devices: 5.29 us -> 1.19 us
  Pallas kernels: 27.9 us -> 30.9 us
  starting transfers between devices: 11 us -> 13.6 us
    all_to_all x3 -> x2, blocking collectives: 47.1 us -> 33.9 us  [spread(): return lax.all_to_all(partial, ('gx', 'gy'), 0, 0, tiled=True)]
    ppermute x6, waiting for transfers between devices: 5.29 us -> 1.19 us  [the longest x1 1.17 us: first_sweep(): corners_above = lax.ppermute(sides[:, 1:], 'gx', ring('gx', 1))]
    ppermute x6, starting transfers between devices: 11 us -> 13.6 us  [the longest x1 4.91 us: first_sweep(): below = lax.ppermute(first, 'gx', ring('gx', -1))]
    pallas_call x3 -> x2, Pallas kernels: 14.4 us -> 16.8 us  [the longest x1 12 us: run_wide(): pl.pallas_call(wide_kernel, out_shape=(vmem((DEGREE + 1, 2, 3, ROWS) + BL...]
    unnamed x4 -> x10, local copies, waits for them, and re-layouts: 1.92 us -> 0.03 us
    slice x1 -> x2, local copies, waits for them, and re-layouts: 0.02 us -> 1.24 us  [the longest x1 0.66 us: first_sweep(): corners_below = lax.ppermute(sides[:, :-1], 'gx', ring('gx', -1))]
  transfers between devices with their start and end apart: 6 -> 6, of which waited for: 2 -> 1; matrix products, arithmetic and copies ran while one was open for 1% -> 2% of each run, Pallas kernels for 0% -> 0%
where the time goes in v3:
time: 87.2 us; the launch traced here: 86.9 us
  blocking collectives  33.9 us (39%)
  Pallas kernels  30.9 us (35%)
  starting transfers between devices  13.6 us (16%)
  between operations  4.55 us (5%)
  local copies, waits for them, and re-layouts  1.93 us (2%)
  waiting for transfers between devices  1.19 us (1%)
    all_to_all x2, blocking collectives, spread(): return lax.all_to_all(partial, ('gx', 'gy'), 0, 0, tiled=True)  33.9 us
    pallas_call x1, Pallas kernels, run_wide(): pl.pallas_call(wide_kernel, out_shape=(vmem((DEGREE + 1, 2, 3, ROWS) + BL...  12 us
    pallas_call x1, Pallas kernels, run_first(): pl.pallas_call(first_kernel, out_shape=(vmem(BASIS), vmem((3, WIDE, 2) +...  10.8 us
    ppermute x1, starting transfers between devices, first_sweep(): below = lax.ppermute(first, 'gx', ring('gx', -1))  4.91 us
    ppermute x1, starting transfers between devices, first_sweep(): corners_below = lax.ppermute(sides[:, :-1], 'gx', ring('gx', -1))  4.78 us
    pallas_call x1, Pallas kernels, run_end(): pl.pallas_call(end_kernel, out_shape=(shape, shape, jax.ShapeDtypeStruct(...  4.76 us
    pallas_call x1, Pallas kernels, pack_messages(): pl.pallas_call(pack_kernel, out_shape=(vmem(rows), vmem(edge), vmem(edge)...  3.3 us
    ppermute x1, starting transfers between devices, first_sweep(): before = lax.ppermute(strips, 'gy', ring('gy', 1))  2.61 us
  transfers between devices with their start and end apart: 6, of which 1 were waited for; matrix products, arithmetic and copies ran while one was open for 2% of the time, Pallas kernels for 0%

profile of v3, /device:TPU:1, one launch (start us, length us, event | category | flops | bytes accessed | tf_op | source)
XLA Modules:
  0.0 86.9 jit_solution(11551913502260493321)
XLA Ops:
  0.6 0.0 copy-start.3
  0.6 0.0 copy-start.2
  0.7 0.0 copy-start.4
  0.7 0.0 copy-start.5
  0.7 0.0 copy-start.6
  0.7 3.3 %pack_messages.3 = (f32[9,16,8,128]{3,2,1,0:T(8,128)S(1)}, f32[9,12,8,128]{3,2,1,0:T(8,128)S(1)}, f32[9,12,8,128]{3,2,1,0:T(8,128)S(1)}, f32[9,4,8,128]{3,2,1,0:T(8,128)S(1)}) custom-call(f32[768,128]{1,0:T(8,128)} %bitcast.62, f32[384,128]{1,0:T(8,128)} %bitcast.64), custom_call_target="tpu_custom_call" | custom-call | tf_op jit(solution)/shard_map/pack_messages/pallas_call | solution.py:115
  4.0 2.6 %collective-permute-start.8 = (f32[9,4,8,128]{3,2,1,0:T(8,128)S(1)}, f32[9,4,8,128]{3,2,1,0:T(8,128)S(1)}, u32[]{:S(2)}, u32[]{:S(2)}) collective-permute-start(f32[9,4,8,128]{3,2,1,0:T(8,128)S(1)} %get-tuple-element.63), channel_id=1, source_target_pairs={{0,1},{1,2},{2,3},{3,4},{4,5},{5,6},{6,7},{7,0},{8,9},{9,10},{10,1... | collective-permute-start | bytes 442376 | tf_op jit(solution)/shard_map/ppermute | solution.py:777
  6.6 0.0 collective-permute-start.9
  6.6 1.3 %collective-permute-start.6 = (f32[9,12,8,128]{3,2,1,0:T(8,128)S(1)}, f32[9,12,8,128]{3,2,1,0:T(8,128)S(1)}, u32[]{:S(2)}, u32[]{:S(2)}) collective-permute-start(f32[9,12,8,128]{3,2,1,0:T(8,128)S(1)} %get-tuple-element.61), channel_id=1, source_target_pairs={{0,8},{8,16},{16,24},{24,32},{32,40},{40,48},{48,56},{56,64},{64,7... | collective-permute-start | bytes 1327112 | tf_op jit(solution)/shard_map/ppermute | solution.py:779
  7.9 4.9 %collective-permute-start.7 = (f32[9,12,8,128]{3,2,1,0:T(8,128)S(1)}, f32[9,12,8,128]{3,2,1,0:T(8,128)S(1)}, u32[]{:S(2)}, u32[]{:S(2)}) collective-permute-start(f32[9,12,8,128]{3,2,1,0:T(8,128)S(1)} %get-tuple-element.62), channel_id=1, source_target_pairs={{0,120},{8,0},{16,8},{24,16},{32,24},{40,32},{48,40},{56,48},{64,5... | collective-permute-start | bytes 1327112 | tf_op jit(solution)/shard_map/ppermute | solution.py:780
  12.8 0.7 convert_multiply_fusion.1
  13.5 0.0 collective-permute-done.8
  13.5 0.0 collective-permute-done.9
  13.5 0.7 fusion.8
  14.2 0.0 collective-permute-start.10
  14.2 4.8 %collective-permute-start.11 = (f32[9,3,8,128]{3,2,1,0:T(8,128)S(1)}, f32[9,3,8,128]{3,2,1,0:T(8,128)S(1)}, u32[]{:S(2)}, u32[]{:S(2)}) collective-permute-start(f32[9,3,8,128]{3,2,1,0:T(8,128)S(1)} %get-tuple-element.93), channel_id=1, source_target_pairs={{0,120},{8,0},{16,8},{24,16},{32,24},{40,32},{48,40},{56,48},{64,5... | collective-permute-start | bytes 331784 | tf_op jit(solution)/shard_map/ppermute | solution.py:784
  19.0 0.6 fusion.9
  22.5 0.1 stack.62.scal_ref
  22.6 1.2 %collective-permute-done.10.above_ref = f32[9,3,8,128]{3,2,1,0:T(8,128)S(1)} collective-permute-done((f32[9,3,8,128]{3,2,1,0:T(8,128)}, f32[9,3,8,128]{3,2,1,0:T(8,128)S(1)}, u32[]{:S(2)}, u32[]{:S(2)}) %collective-permute-start.10) | collective-permute-done | bytes 110624 | tf_op jit(solution)/shard_map/ppermute | solution.py:783
  23.8 0.0 collective-permute-done.11.below_ref
  23.8 0.0 collective-permute-done.6.last_ref
  23.8 0.0 collective-permute-done.7.first_ref
  23.8 10.8 %first_sweep.3 = (f32[5,2,3,40,2,8,128]{6,5,4,3,2,1,0:T(8,128)S(1)}, f32[3,40,2,8,128]{4,3,2,1,0:T(8,128)S(1)}, f32[128,128]{1,0:T(8,128)S(1)}) custom-call(f32[8]{0:T(128)S(1)} %stack.62.scal_ref, f32[9,16,8,128]{3,2,1,0:T(8,128)S(1)} %get-tuple-element.60.tile_ref, f32[9,12,8,128]{3,2,1,0:T(8,128)S(1)} %collective-permute-done.6.last_ref, ...), custom_call_target="tpu_custom_call" | custom-call | tf_op jit(solution)/shard_map/first_sweep/pallas_call | solution.py:682
  34.6 20.0 %all_to_all.48 = f32[128,1,128]{2,1,0:T(1,128)S(1)} all-to-all(f32[128,1,128]{2,1,0:T(1,128)S(1)} %bitcast.60), channel_id=1, replica_groups=mesh['gx'=16,'gy'=8] {'gx','gy'}, dimensions={0} | all-to-all | bytes 131072 | tf_op jit(solution)/shard_map/all_to_all | solution.py:754
  54.6 12.0 %second_third_basis.1 = (f32[9,2,3,16,8,128]{5,4,3,2,1,0:T(8,128)S(1)}, f32[2,3,16,8,128]{4,3,2,1,0:T(8,128)S(1)}, f32[128,128]{1,0:T(8,128)S(1)}) custom-call(f32[128,128]{1,0:T(8,128)S(1)} %bitcast.59, f32[5,2,3,40,2,8,128]{6,5,4,3,2,1,0:T(8,128)S(1)} %get-tuple-element.65.old_ref, f32[3,40,2,8,128]{4,3,2,1,0:T(8,128)S(1)} %get-tuple-element.66.sigma_ref), custom_call_target="tpu_custom_call" | custom-call | tf_op jit(solution)/shard_map/second_third_basis/pallas_call | solution.py:708
  66.6 13.9 %all_to_all.49 = f32[128,1,128]{2,1,0:T(1,128)S(1)} all-to-all(f32[128,1,128]{2,1,0:T(1,128)S(1)} %bitcast.61), channel_id=1, replica_groups=mesh['gx'=16,'gy'=8] {'gx','gy'}, dimensions={0} | all-to-all | bytes 131072 | tf_op jit(solution)/shard_map/all_to_all | solution.py:754
  80.5 0.0 copy-done.3
  80.5 0.0 copy-done.2
  80.5 0.0 copy-done.4
  80.5 4.8 %second_third_update.1 = (f32[768,128]{1,0:T(8,128)}, f32[768,128]{1,0:T(8,128)}, f32[8,128]{1,0:T(8,128)S(1)}) custom-call(f32[128,128]{1,0:T(8,128)S(1)} %bitcast.58, f32[80,128]{1,0:T(8,128)S(1)} %copy-done.3, bf16[2,128,128]{2,1,0:T(8,128)(2,1)S(1)} %copy-done.2, bf16[2,32,32]{2,1,0:T(8,128)(2,1)S(1)} %copy-done.4, ...), custom_call_target="tpu_custom_call" | custom-call | tf_op jit(solution)/shard_map/second_third_update/pallas_call | solution.py:728
  85.3 0.6 slice.31
  86.6 0.2 while.11
  (5 shorter events, 0.0 us)
Async XLA Ops:
  0.6 79.9 %copy-start.3 = (f32[80,128]{1,0:T(8,128)S(1)}, f32[80,128]{1,0:T(8,128)}, u32[]{:S(2)}) copy-start(f32[80,128]{1,0:T(8,128)} %constant.123.clone.table_ref) | copy-start | bytes 122884
  0.6 79.9 %copy-start.2 = (bf16[2,128,128]{2,1,0:T(8,128)(2,1)S(1)}, bf16[2,128,128]{2,1,0:T(8,128)(2,1)}, u32[]{:S(2)}) copy-start(bf16[2,128,128]{2,1,0:T(8,128)(2,1)} %constant.124.clone.picks_ref) | copy-start | bytes 196612
  0.7 79.9 %copy-start.4 = (bf16[2,32,32]{2,1,0:T(8,128)(2,1)S(1)}, bf16[2,32,32]{2,1,0:T(8,128)(2,1)}, u32[]{:S(2)}) copy-start(bf16[2,32,32]{2,1,0:T(8,128)(2,1)} %constant.125.clone.select_ref) | copy-start | bytes 12292
  0.7 85.9 %copy-start.5 = (f32[2,3,8,16,128]{4,3,2,1,0:T(8,128)S(1)}, f32[2,3,8,16,128]{4,3,2,1,0:T(8,128)}, u32[]{:S(2)}) copy-start(f32[2,3,8,16,128]{4,3,2,1,0:T(8,128)} %param.8) | copy-start | bytes 1179652
  0.7 85.9 %copy-start.6 = (f32[3,8,16,128]{3,2,1,0:T(8,128)S(1)}, f32[3,8,16,128]{3,2,1,0:T(8,128)}, u32[]{:S(2)}) copy-start(f32[3,8,16,128]{3,2,1,0:T(8,128)} %param.9) | copy-start | bytes 589828
  4.0 9.5 %collective-permute-start.8 = (f32[9,4,8,128]{3,2,1,0:T(8,128)S(1)}, f32[9,4,8,128]{3,2,1,0:T(8,128)S(1)}, u32[]{:S(2)}, u32[]{:S(2)}) collective-permute-start(f32[9,4,8,128]{3,2,1,0:T(8,128)S(1)} %get-tuple-element.63), channel_id=1, source_target_pairs={{0,1},{1,2},{2,3},{3,4},{4,5},{5,6},{6,7},{7,0},{8,9},{9,10},{10,1... | collective-permute-start | bytes 442376 | tf_op jit(solution)/shard_map/ppermute | solution.py:777
  6.6 6.9 %collective-permute-start.9 = (f32[9,4,8,128]{3,2,1,0:T(8,128)S(1)}, f32[9,4,8,128]{3,2,1,0:T(8,128)S(1)}, u32[]{:S(2)}, u32[]{:S(2)}) collective-permute-start(f32[9,4,8,128]{3,2,1,0:T(8,128)S(1)} %get-tuple-element.63), channel_id=1, source_target_pairs={{0,7},{1,0},{2,1},{3,2},{4,3},{5,4},{6,5},{7,6},{8,15},{9,8},{10,9... | collective-permute-start | bytes 442376 | tf_op jit(solution)/shard_map/ppermute | solution.py:778
  6.6 17.2 %collective-permute-start.6 = (f32[9,12,8,128]{3,2,1,0:T(8,128)S(1)}, f32[9,12,8,128]{3,2,1,0:T(8,128)S(1)}, u32[]{:S(2)}, u32[]{:S(2)}) collective-permute-start(f32[9,12,8,128]{3,2,1,0:T(8,128)S(1)} %get-tuple-element.61), channel_id=1, source_target_pairs={{0,8},{8,16},{16,24},{24,32},{32,40},{40,48},{48,56},{56,64},{64,7... | collective-permute-start | bytes 1327112 | tf_op jit(solution)/shard_map/ppermute | solution.py:779
  7.9 15.9 %collective-permute-start.7 = (f32[9,12,8,128]{3,2,1,0:T(8,128)S(1)}, f32[9,12,8,128]{3,2,1,0:T(8,128)S(1)}, u32[]{:S(2)}, u32[]{:S(2)}) collective-permute-start(f32[9,12,8,128]{3,2,1,0:T(8,128)S(1)} %get-tuple-element.62), channel_id=1, source_target_pairs={{0,120},{8,0},{16,8},{24,16},{32,24},{40,32},{48,40},{56,48},{64,5... | collective-permute-start | bytes 1327112 | tf_op jit(solution)/shard_map/ppermute | solution.py:780
  14.2 9.6 %collective-permute-start.10 = (f32[9,3,8,128]{3,2,1,0:T(8,128)}, f32[9,3,8,128]{3,2,1,0:T(8,128)S(1)}, u32[]{:S(2)}, u32[]{:S(2)}) collective-permute-start(f32[9,3,8,128]{3,2,1,0:T(8,128)} %get-tuple-element.94), channel_id=1, source_target_pairs={{0,8},{8,16},{16,24},{24,32},{32,40},{40,48},{48,56},{56,64},{64,7... | collective-permute-start | bytes 331784 | tf_op jit(solution)/shard_map/ppermute | solution.py:783
  14.2 9.6 %collective-permute-start.11 = (f32[9,3,8,128]{3,2,1,0:T(8,128)S(1)}, f32[9,3,8,128]{3,2,1,0:T(8,128)S(1)}, u32[]{:S(2)}, u32[]{:S(2)}) collective-permute-start(f32[9,3,8,128]{3,2,1,0:T(8,128)S(1)} %get-tuple-element.93), channel_id=1, source_target_pairs={{0,120},{8,0},{16,8},{24,16},{32,24},{40,32},{48,40},{56,48},{64,5... | collective-permute-start | bytes 331784 | tf_op jit(solution)/shard_map/ppermute | solution.py:784

commit v4 on v3

--- a/solution.py
+++ b/solution.py
@@ -80,11 +80,11 @@
     eighth = (lane_index(NZ) // 8) % 8
 
     def pack(source, offset):
-        def body(group, _):
+        def body(group):
             start = (group - offset) * (NZ * ROWS)
             rows = [source[pl.ds(start + x, NZ, stride=ROWS), :] for x in range(ROWS)]
-            packed = reorder(jnp.concatenate(rows, axis=0), order)
-            rows = [packed[NZ * x : NZ * x + NZ] for x in range(ROWS)]
+            mixed = reorder(jnp.concatenate(rows, axis=0), order)
+            rows = [mixed[NZ * x : NZ * x + NZ] for x in range(ROWS)]
             for x in range(ROWS):
                 tile_ref[group, x] = rows[x]
                 if x >= ROWS - HALO:
@@ -100,14 +100,13 @@
                     else:
                         strip = jnp.where((eighth == 2 * j) | (eighth == (7 + 2 * j) % 8), moved, strip)
                 strip_ref[group, four] = strip
-            return 0
 
         return body
 
     copies[0].wait()
-    lax.fori_loop(0, 6, pack(rs_ref, 0), 0)
+    each(0, 6, 3, pack(rs_ref, 0))
     copies[1].wait()
-    lax.fori_loop(6, 9, pack(cond_ref, 6), 0)
+    each(6, 9, 3, pack(cond_ref, 6))
 
 
 def pack_messages(right_side, conductivity):
@@ -123,20 +122,29 @@
     )(right_side.reshape(6 * NZ * ROWS, LANES), conductivity.reshape(3 * NZ * ROWS, LANES))
 
 
+def each(begin, end, size, body):
+    def block(step, _):
+        for spot in range(size):
+            body(begin + step * size + spot)
+        return 0
+
+    lax.fori_loop(0, (end - begin) // size, block, 0)
+
+
 def turn(real, imag, cosine, sine):
     return real * cosine - imag * sine, real * sine + imag * cosine
 
 
-def fill(scal_ref, tile_ref, last_ref, first_ref, sides_ref, above_ref, below_ref, basis_ref, sigma_ref):
+def fill_region(scal_ref, rows_ref, strips_ref, count, base, turned, basis_ref, sigma_ref):
     lanes = lane_index(NZ)
     own = lanes < 64
-    low_c, low_s, high_c, high_s = (scal_ref[k] for k in range(4))
-    cos_y = jnp.where(own, 1.0, jnp.where(lanes < 96, scal_ref[6], scal_ref[4]))
-    sin_y = jnp.where(own, 0.0, jnp.where(lanes < 96, scal_ref[7], scal_ref[5]))
-
-    def region(rows_ref, strips_ref, count, base, cosine, sine):
-        def body(step, _):
-            four, comp = step // 3, step % 3
+    cosine = jnp.where(own, 1.0, jnp.where(lanes < 96, scal_ref[6], scal_ref[4]))
+    sine = jnp.where(own, 0.0, jnp.where(lanes < 96, scal_ref[7], scal_ref[5]))
+    if turned is not None:
+        cosine, sine = turn(cosine, sine, scal_ref[turned], scal_ref[turned + 1])
+
+    def body(four):
+        for comp in range(3):
             for j in range(4):
                 x = 4 * four + j
 
@@ -151,20 +159,15 @@
                     basis_ref[0, 0, comp, base + x, b] = new_real
                     basis_ref[0, 1, comp, base + x, b] = new_imag
                     sigma_ref[comp, base + x, b] = level_step * sigma[b]
-            return 0
-
-        lax.fori_loop(0, 3 * count // 4, body, 0)
-
-    region(last_ref, above_ref, HALO, 0, *turn(cos_y, sin_y, low_c, low_s))
-    region(tile_ref, sides_ref, ROWS, HALO, cos_y, sin_y)
-    region(first_ref, below_ref, HALO, HALO + ROWS, *turn(cos_y, sin_y, high_c, high_s))
+
+    each(0, count // 4, 1, body)
 
 
 def minus(a, b):
     return a[0] - b[0], a[1] - b[1]
 
 
-def apply_step(basis_ref, sigma_ref, k, begin, end, slots=None):
+def apply_step(basis_ref, sigma_ref, k, starts, count, slots=None):
     before, here, there = (None, k, k + 1) if slots is None else slots
     beta = 0.0 if k == 0 else 2 * BETA if k == 1 else BETA
     layer = lax.broadcasted_iota(jnp.int32, BLOCK, 0)
@@ -222,15 +225,18 @@
                 basis_ref[there, 1, c, x, b] = new_imag
         return tuple(fresh)
 
-    count = end - begin
-    size = next(n for n in (9, 8, 10, 7, 11, 12, 13, 17, 19, 1) if count % n == 0)
+    size = next(n for n in (9, 8, 10, 7, 11, 12, 13, 17, 19, 1) if count % n == 0) if len(starts) == 1 else 6
 
     def body(block, carry):
+        carry = list(carry)
         for spot in range(size):
-            carry = row(begin + block * size + spot, carry)
-        return carry
-
-    carry = curls(0, begin - 1)[2:] + curls(1, begin - 1)[2:]
+            for n, start in enumerate(starts):
+                carry[4 * n : 4 * n + 4] = row(start + block * size + spot, carry[4 * n : 4 * n + 4])
+        return tuple(carry)
+
+    carry = ()
+    for start in starts:
+        carry += curls(0, start - 1)[2:] + curls(1, start - 1)[2:]
     lax.fori_loop(0, count // size, body, carry)
 
 
@@ -241,10 +247,11 @@
 
 
 def gram(basis_ref, sums_ref, gram_ref):
-    def body(x, sums):
+    def body(step, sums):
         reals, imags = [[] for _ in PAIRS], [[] for _ in PAIRS]
         for c in range(3):
-            for b in range(2):
+            for n in range(4):
+                x, b = HALO + 2 * step + n // 2, n % 2
                 vs = [[basis_ref[k, ri, c, x, b] for ri in range(2)] for k in range(S + 1)]
                 for at, (j, k) in enumerate(PAIRS):
                     reals[at].append(vs[j][0] * vs[k][0] + vs[j][1] * vs[k][1])
@@ -254,7 +261,7 @@
         return tuple(total + term for total, term in zip(sums, fresh))
 
     count = len(PAIRS) + sum(j != k for j, k in PAIRS)
-    sums = lax.fori_loop(HALO, HALO + ROWS, body, (jnp.zeros(BLOCK, jnp.float32),) * count)
+    sums = lax.fori_loop(0, ROWS // 2, body, (jnp.zeros(BLOCK, jnp.float32),) * count)
     own = lane_index(1) < 64
     sums_ref[...] = jnp.zeros((LANES, LANES), jnp.float32)
     for at, total in enumerate(sums):
@@ -344,13 +351,19 @@
     return tuple((parts[0][ri] + parts[1][ri]) + (parts[2][ri] + parts[3][ri]) for ri in range(2))
 
 
+def inner_kernel(scal_ref, tile_ref, sides_ref, basis_ref, sigma_ref):
+    fill_region(scal_ref, tile_ref, sides_ref, ROWS, HALO, None, basis_ref, sigma_ref)
+    for k in range(S):
+        apply_step(basis_ref, sigma_ref, k, (HALO + k + 1,), ROWS - 2 * k - 2)
+
+
 def first_kernel(
-    scal_ref, tile_ref, last_ref, first_ref, sides_ref, above_ref, below_ref,
-    basis_ref, sigma_ref, gram_ref, sums_ref,
+    scal_ref, last_ref, first_ref, above_ref, below_ref, _, __, basis_ref, sigma_ref, gram_ref, sums_ref
 ):
-    fill(scal_ref, tile_ref, last_ref, first_ref, sides_ref, above_ref, below_ref, basis_ref, sigma_ref)
+    fill_region(scal_ref, last_ref, above_ref, HALO, 0, 0, basis_ref, sigma_ref)
+    fill_region(scal_ref, first_ref, below_ref, HALO, HALO + ROWS, 2, basis_ref, sigma_ref)
     for k in range(S):
-        apply_step(basis_ref, sigma_ref, k, k + 1, WIDE - k - 1)
+        apply_step(basis_ref, sigma_ref, k, (k + 1, HALO + ROWS - k - 1), HALO)
     gram(basis_ref, sums_ref, gram_ref)
 
 
@@ -363,29 +376,27 @@
     coefs = coefficients(gathered_ref)
     begin, end = S * sweep, WIDE - S * sweep
 
-    def residual_row(x, _):
+    def residual_row(x):
         for c in range(3):
             for b in range(2):
                 real, imag = new_residual(old_ref, coefs, c, x, b)
                 basis_ref[0, 0, c, x, b] = real
                 basis_ref[0, 1, c, x, b] = imag
-        return 0
-
-    def tile_row(x, _):
-        residual_row(x, 0)
+
+    def tile_row(x):
+        residual_row(x)
         for c in range(3):
             for b in range(2):
                 part = solution_part(old_ref, coefs, c, x, b)
                 for ri in range(2):
                     value = part[ri] if old_part is None else part[ri] + old_part[ri, c, x - HALO, b]
                     part_ref[ri, c, x - HALO, b] = value
-        return 0
-
-    lax.fori_loop(begin, HALO, residual_row, 0)
-    lax.fori_loop(HALO, HALO + ROWS, tile_row, 0)
-    lax.fori_loop(HALO + ROWS, end, residual_row, 0)
+
+    each(begin, HALO, 4, residual_row)
+    each(HALO, HALO + ROWS, 2, tile_row)
+    each(HALO + ROWS, end, 4, residual_row)
     for k in range(S):
-        apply_step(basis_ref, sigma_ref, k, begin + k + 1, end - k - 1)
+        apply_step(basis_ref, sigma_ref, k, (begin + k + 1,), end - begin - 2 * k - 2)
     gram(basis_ref, sums_ref, gram_ref)
 
 
@@ -593,42 +604,41 @@
     coefs = coefficients(gathered_ref)
     begin, end = S, WIDE - S
 
-    def residual_row(x, _):
+    def residual_row(x):
         for c in range(3):
             for b in range(2):
                 real, imag = new_residual(old_ref, coefs, c, x, b)
                 basis_ref[0, 0, c, x, b] = real
                 basis_ref[0, 1, c, x, b] = imag
-        return 0
-
-    def tile_row(x, _):
-        residual_row(x, 0)
+
+    def tile_row(x):
+        residual_row(x)
         for c in range(3):
             even, odd = (solution_part(old_ref, coefs, c, x, b) for b in range(2))
             for ri in range(2):
                 part_ref[ri, c, x - HALO] = packed(even[ri], odd[ri])
-        return 0
-
-    lax.fori_loop(begin, HALO, residual_row, 0)
-    lax.fori_loop(HALO, HALO + ROWS, tile_row, 0)
-    lax.fori_loop(HALO + ROWS, end, residual_row, 0)
+
+    each(begin, HALO, 4, residual_row)
+    each(HALO, HALO + ROWS, 2, tile_row)
+    each(HALO + ROWS, end, 4, residual_row)
     for k in range(DEGREE):
-        apply_step(basis_ref, sigma_ref, k, begin + k + 1, end - k - 1, (k - 1, k, k + 1))
+        apply_step(basis_ref, sigma_ref, k, (begin + k + 1,), end - begin - 2 * k - 2, (k - 1, k, k + 1))
     acc_ref[...] = jnp.zeros(acc_ref.shape, jnp.float32)
 
     def gram_row(x, _):
-        for c in range(3):
-            vs = []
-            for k in range(DEGREE + 1):
-                vs.append([packed(basis_ref[k, ri, c, x, 0], basis_ref[k, ri, c, x, 1]) for ri in range(2)])
-                for ri in range(2):
-                    tile_ref[k, ri, c, x - HALO] = vs[k][ri]
-            at = len(BIG_PAIRS)
-            for index, (j, k) in enumerate(BIG_PAIRS):
-                acc_ref[index] += vs[j][0] * vs[k][0] + vs[j][1] * vs[k][1]
-                if j != k:
-                    acc_ref[at] += vs[j][0] * vs[k][1] - vs[j][1] * vs[k][0]
-                    at += 1
+        vs = []
+        for k in range(DEGREE + 1):
+            vs.append([[packed(basis_ref[k, ri, c, x, 0], basis_ref[k, ri, c, x, 1]) for c in range(3)] for ri in range(2)])
+            for ri in range(2):
+                for c in range(3):
+                    tile_ref[k, ri, c, x - HALO] = vs[k][ri][c]
+        at = len(BIG_PAIRS)
+        for index, (j, k) in enumerate(BIG_PAIRS):
+            left, right = vs[j], vs[k]
+            acc_ref[index] += tree([left[0][c] * right[0][c] + left[1][c] * right[1][c] for c in range(3)])
+            if j != k:
+                acc_ref[at] += tree([left[0][c] * right[1][c] - left[1][c] * right[0][c] for c in range(3)])
+                at += 1
         return 0
 
     lax.fori_loop(HALO, HALO + ROWS, gram_row, 0)
@@ -639,10 +649,10 @@
 
 
 def end_kernel(
-    gathered_ref, table_ref, picks_ref, select_ref, tile_ref, old_part, part_ref, residual_ref, spread_ref, coef_ref
+    gathered_ref, table_ref, picks_ref, select_ref, tile_ref, old_part, part_ref, residual_ref, again_ref, coef_ref
 ):
     part, residual, spread = both_iterations(gathered_ref, table_ref, picks_ref, select_ref)
-    spread_ref[...] = jnp.broadcast_to(spread, BLOCK)
+    again_ref[0, 0] = jnp.where(spread[0, 0] < SPREAD_MAX, 0, 1)
     for a in range(DEGREE + 1):
         for n, value in enumerate(part + residual):
             coef_ref[4 * a + n] = jnp.broadcast_to(value[:, a : a + 1], BLOCK)
@@ -678,6 +688,18 @@
 PART = (2, 3, ROWS, 2) + BLOCK
 
 
+def run_inner(*operands):
+    return pl.pallas_call(
+        inner_kernel,
+        out_shape=(vmem(BASIS), vmem((3, WIDE, 2) + BLOCK)),
+        in_specs=[SMEM] + [VMEM] * 2,
+        out_specs=(VMEM,) * 2,
+        compiler_params=pltpu.CompilerParams(vmem_limit_bytes=LIMIT),
+        cost_estimate=pl.CostEstimate(flops=8_000_000, bytes_accessed=8_000_000, transcendentals=0),
+        name="inner_part",
+    )(*operands)
+
+
 def run_first(peers, *operands):
     return pl.pallas_call(
         first_kernel,
@@ -687,6 +709,7 @@
         in_specs=[SMEM] + [VMEM] * 6,
         out_specs=(VMEM,) * 3,
         scratch_shapes=[vmem((LANES, LANES))],
+        input_output_aliases={5: 0, 6: 1},
         compiler_params=pltpu.CompilerParams(vmem_limit_bytes=LIMIT),
         name="first_sweep",
     )(*operands)
@@ -725,16 +748,16 @@
 def run_end(*operands):
     shape = jax.ShapeDtypeStruct((6 * NZ * ROWS, LANES), jnp.float32)
     tables = [jnp.asarray(table) for table in constants()]
-    part, residual, spread = pl.pallas_call(
+    part, residual, again = pl.pallas_call(
         end_kernel,
-        out_shape=(shape, shape, jax.ShapeDtypeStruct(BLOCK, jnp.float32)),
+        out_shape=(shape, shape, jax.ShapeDtypeStruct((1, 1), jnp.int32)),
         in_specs=[VMEM] * 6,
-        out_specs=(VMEM,) * 3,
+        out_specs=(VMEM, VMEM, SMEM),
         scratch_shapes=[vmem((4 * (DEGREE + 1),) + BLOCK)],
         compiler_params=pltpu.CompilerParams(vmem_limit_bytes=LIMIT),
         name="second_third_update",
     )(operands[0], *tables, *operands[1:])
-    return tuple(out.reshape(2, 3, NZ, ROWS, LANES) for out in (part, residual)) + (spread[0, 0],)
+    return tuple(out.reshape(2, 3, NZ, ROWS, LANES) for out in (part, residual)) + (again[0, 0],)
 
 
 def run_last(*operands):
@@ -782,7 +805,8 @@
     sides = jnp.where(from_left, before, after)
     corners_above = lax.ppermute(sides[:, 1:], "gx", ring("gx", 1))
     corners_below = lax.ppermute(sides[:, :-1], "gx", ring("gx", -1))
-    basis, sigma, partial = run_first(peers, scal, tile, above, below, sides, corners_above, corners_below)
+    inner = run_inner(scal, tile, sides)
+    basis, sigma, partial = run_first(peers, scal, above, below, corners_above, corners_below, *inner)
     return peers, basis, sigma, spread(partial)
 
 
@@ -800,13 +824,12 @@
 
 
 def shards(*operands):
-    part, residual, cancelled = two_reductions(*operands)
-    state = (jnp.logical_not(cancelled < SPREAD_MAX), part, residual)
-
-    def again(_):
-        return (jnp.array(False),) + three_reductions(*operands)
-
-    return lax.while_loop(lambda state: state[0], again, state)[1:]
+    part, residual, again = two_reductions(*operands)
+
+    def repeat(_):
+        return (jnp.int32(0),) + three_reductions(*operands)
+
+    return lax.while_loop(lambda state: state[0] > 0, repeat, (again, part, residual))[1:]
 
 
 def solution(mesh):

time: 87.2 us -> 79.9 us (0.916)
  Pallas kernels: 30.9 us -> 26.6 us
  starting transfers between devices: 13.6 us -> 11 us
  waiting for transfers between devices: 1.19 us -> 2.77 us
  local copies, waits for them, and re-layouts: 1.93 us -> 0.72 us
    pallas_call x1, Pallas kernels: 10.8 us -> 5.82 us  [run_first(): pl.pallas_call(first_kernel, out_shape=(vmem(BASIS), vmem((3, WIDE, 2) +...]
    ppermute x1, starting transfers between devices: 4.78 us -> 2.18 us  [first_sweep(): corners_below = lax.ppermute(sides[:, :-1], 'gx', ring('gx', -1))]
    pallas_call x0 -> x1, Pallas kernels: none -> 2.5 us  [run_inner(): pl.pallas_call(inner_kernel, out_shape=(vmem(BASIS), vmem((3, WIDE, 2) +...]
    ppermute x1, waiting for transfers between devices: 0.01 us -> 1.72 us  [first_sweep(): corners_below = lax.ppermute(sides[:, :-1], 'gx', ring('gx', -1))]
    ppermute x1, starting transfers between devices: 0.01 us -> 1.43 us  [first_sweep(): after = lax.ppermute(strips, 'gy', ring('gy', -1))]
    ppermute x1, starting transfers between devices: 2.61 us -> 1.2 us  [first_sweep(): before = lax.ppermute(strips, 'gy', ring('gy', 1))]
    pallas_call x1, Pallas kernels: 3.3 us -> 1.95 us  [pack_messages(): pl.pallas_call(pack_kernel, out_shape=(vmem(rows), vmem(edge), vmem(edge)...]
  transfers between devices with their start and end apart: 6 -> 6, of which waited for: 1 -> 2; matrix products, arithmetic and copies ran while one was open for 2% -> 2% of each run, Pallas kernels for 0% -> 3%
where the time goes in v4:
time: 79.9 us; the launch traced here: 79.7 us
  blocking collectives  33.2 us (42%)
  Pallas kernels  26.6 us (33%)
  starting transfers between devices  11 us (14%)
  between operations  3.84 us (5%)
  waiting for transfers between devices  2.77 us (3%)
  loops' own time  0.82 us (1%)
    all_to_all x2, blocking collectives, spread(): return lax.all_to_all(partial, ('gx', 'gy'), 0, 0, tiled=True)  33.2 us
    pallas_call x1, Pallas kernels, run_wide(): pl.pallas_call(wide_kernel, out_shape=(vmem((DEGREE + 1, 2, 3, ROWS) + BL...  11.6 us
    pallas_call x1, Pallas kernels, run_first(): pl.pallas_call(first_kernel, out_shape=(vmem(BASIS), vmem((3, WIDE, 2) +...  5.82 us
    ppermute x1, starting transfers between devices, first_sweep(): below = lax.ppermute(first, 'gx', ring('gx', -1))  4.91 us
    pallas_call x1, Pallas kernels, run_end(): pl.pallas_call(end_kernel, out_shape=(shape, shape, jax.ShapeDtypeStruct(...  4.77 us
    pallas_call x1, Pallas kernels, run_inner(): pl.pallas_call(inner_kernel, out_shape=(vmem(BASIS), vmem((3, WIDE, 2) +...  2.5 us
    ppermute x1, starting transfers between devices, first_sweep(): corners_below = lax.ppermute(sides[:, :-1], 'gx', ring('gx', -1))  2.18 us
    pallas_call x1, Pallas kernels, pack_messages(): pl.pallas_call(pack_kernel, out_shape=(vmem(rows), vmem(edge), vmem(edge)...  1.95 us
  transfers between devices with their start and end apart: 6, of which 2 were waited for; matrix products, arithmetic and copies ran while one was open for 2% of the time, Pallas kernels for 3%

profile of v4, /device:TPU:1, one launch (start us, length us, event | category | flops | bytes accessed | tf_op | source)
XLA Modules:
  0.0 79.7 jit_solution(9163833394105376571)
XLA Ops:
  0.6 1.9 %pack_messages.3 = (f32[9,16,8,128]{3,2,1,0:T(8,128)S(1)}, f32[9,12,8,128]{3,2,1,0:T(8,128)S(1)}, f32[9,12,8,128]{3,2,1,0:T(8,128)S(1)}, f32[9,4,8,128]{3,2,1,0:T(8,128)S(1)}) custom-call(f32[768,128]{1,0:T(8,128)} %bitcast.63, f32[384,128]{1,0:T(8,128)} %bitcast.65), custom_call_target="tpu_custom_call" | custom-call | tf_op jit(solution)/shard_map/pack_messages/pallas_call | solution.py:114
  2.6 1.4 %collective-permute-start.9 = (f32[9,4,8,128]{3,2,1,0:T(8,128)S(1)}, f32[9,4,8,128]{3,2,1,0:T(8,128)S(1)}, u32[]{:S(2)}, u32[]{:S(2)}) collective-permute-start(f32[9,4,8,128]{3,2,1,0:T(8,128)S(1)} %get-tuple-element.66), channel_id=1, source_target_pairs={{0,7},{1,0},{2,1},{3,2},{4,3},{5,4},{6,5},{7,6},{8,15},{9,8},{10,9... | collective-permute-start | bytes 442376 | tf_op jit(solution)/shard_map/ppermute | solution.py:801
  4.0 1.2 %collective-permute-start.8 = (f32[9,4,8,128]{3,2,1,0:T(8,128)S(1)}, f32[9,4,8,128]{3,2,1,0:T(8,128)S(1)}, u32[]{:S(2)}, u32[]{:S(2)}) collective-permute-start(f32[9,4,8,128]{3,2,1,0:T(8,128)S(1)} %get-tuple-element.66), channel_id=1, source_target_pairs={{0,1},{1,2},{2,3},{3,4},{4,5},{5,6},{6,7},{7,0},{8,9},{9,10},{10,1... | collective-permute-start | bytes 442376 | tf_op jit(solution)/shard_map/ppermute | solution.py:800
  5.2 1.3 %collective-permute-start.6 = (f32[9,12,8,128]{3,2,1,0:T(8,128)S(1)}, f32[9,12,8,128]{3,2,1,0:T(8,128)S(1)}, u32[]{:S(2)}, u32[]{:S(2)}) collective-permute-start(f32[9,12,8,128]{3,2,1,0:T(8,128)S(1)} %get-tuple-element.64), channel_id=1, source_target_pairs={{0,8},{8,16},{16,24},{24,32},{32,40},{40,48},{48,56},{56,64},{64,7... | collective-permute-start | bytes 1327112 | tf_op jit(solution)/shard_map/ppermute | solution.py:802
  6.5 4.9 %collective-permute-start.7 = (f32[9,12,8,128]{3,2,1,0:T(8,128)S(1)}, f32[9,12,8,128]{3,2,1,0:T(8,128)S(1)}, u32[]{:S(2)}, u32[]{:S(2)}) collective-permute-start(f32[9,12,8,128]{3,2,1,0:T(8,128)S(1)} %get-tuple-element.65), channel_id=1, source_target_pairs={{0,120},{8,0},{16,8},{24,16},{32,24},{40,32},{48,40},{56,48},{64,5... | collective-permute-start | bytes 1327112 | tf_op jit(solution)/shard_map/ppermute | solution.py:803
  11.4 0.7 convert_multiply_fusion.1
  12.1 0.0 collective-permute-done.9
  12.1 0.0 collective-permute-done.8
  12.2 2.2 %collective-permute-start.11 = (f32[9,3,8,128]{3,2,1,0:T(8,128)S(1)}, f32[9,3,8,128]{3,2,1,0:T(8,128)S(1)}, u32[]{:S(2)}, u32[]{:S(2)}) collective-permute-start(f32[9,3,8,128]{3,2,1,0:T(8,128)S(1)} %get-tuple-element.99), channel_id=1, source_target_pairs={{0,120},{8,0},{16,8},{24,16},{32,24},{40,32},{48,40},{56,48},{64,5... | collective-permute-start | bytes 331784 | tf_op jit(solution)/shard_map/ppermute | solution.py:807
  14.4 0.0 collective-permute-start.10
  14.4 0.6 fusion.9
  17.9 0.1 stack.62.scal_ref
  18.0 2.5 %inner_part.3 = (f32[5,2,3,40,2,8,128]{6,5,4,3,2,1,0:T(8,128)S(1)}, f32[3,40,2,8,128]{4,3,2,1,0:T(8,128)S(1)}) custom-call(f32[8]{0:T(128)S(1)} %stack.62.scal_ref, f32[9,16,8,128]{3,2,1,0:T(8,128)S(1)} %get-tuple-element.67.tile_ref, f32[9,4,8,128]{3,2,1,0:T(8,128)S(1)} %fusion.5.sides_ref), custom_call_target="tpu_custom_call" | custom-call | flops 8000000 | bytes 8000000 | tf_op jit(solution)/shard_map/inner_part/pallas_call | solution.py:692
  20.5 1.7 %collective-permute-done.11.below_ref = f32[9,3,8,128]{3,2,1,0:T(8,128)S(1)} collective-permute-done((f32[9,3,8,128]{3,2,1,0:T(8,128)S(1)}, f32[9,3,8,128]{3,2,1,0:T(8,128)S(1)}, u32[]{:S(2)}, u32[]{:S(2)}) %collective-permute-start.11) | collective-permute-done | bytes 110624 | tf_op jit(solution)/shard_map/ppermute | solution.py:807
  22.2 1.0 %collective-permute-done.10.above_ref = f32[9,3,8,128]{3,2,1,0:T(8,128)S(1)} collective-permute-done((f32[9,3,8,128]{3,2,1,0:T(8,128)S(1)}, f32[9,3,8,128]{3,2,1,0:T(8,128)S(1)}, u32[]{:S(2)}, u32[]{:S(2)}) %collective-permute-start.10) | collective-permute-done | bytes 110624 | tf_op jit(solution)/shard_map/ppermute | solution.py:806
  23.2 0.0 collective-permute-done.6.last_ref
  23.2 0.0 collective-permute-done.7.first_ref
  23.2 0.0 copy-start.1
  23.2 0.0 copy-start.2
  23.3 5.8 %first_sweep.3 = (f32[5,2,3,40,2,8,128]{6,5,4,3,2,1,0:T(8,128)S(1)}, f32[3,40,2,8,128]{4,3,2,1,0:T(8,128)S(1)}, f32[128,128]{1,0:T(8,128)S(1)}) custom-call(f32[8]{0:T(128)S(1)} %stack.62.scal_ref, f32[9,12,8,128]{3,2,1,0:T(8,128)S(1)} %collective-permute-done.6.last_ref, ...), custom_call_target="tpu_custom_call", output_to_operand_aliasing={{0}: (5, {}), {1}: (6, {})} | custom-call | tf_op jit(solution)/shard_map/first_sweep/pallas_call | solution.py:704
  29.1 0.0 copy-start.4
  29.1 0.0 copy-start.5
  29.1 19.3 %all_to_all.49 = f32[128,1,128]{2,1,0:T(1,128)S(1)} all-to-all(f32[128,1,128]{2,1,0:T(1,128)S(1)} %bitcast.61), channel_id=1, replica_groups=mesh['gx'=16,'gy'=8] {'gx','gy'}, dimensions={0} | all-to-all | bytes 131072 | tf_op jit(solution)/shard_map/all_to_all | solution.py:777
  48.4 11.6 %second_third_basis.1 = (f32[9,2,3,16,8,128]{5,4,3,2,1,0:T(8,128)S(1)}, f32[2,3,16,8,128]{4,3,2,1,0:T(8,128)S(1)}, f32[128,128]{1,0:T(8,128)S(1)}) custom-call(f32[128,128]{1,0:T(8,128)S(1)} %bitcast.60, f32[5,2,3,40,2,8,128]{6,5,4,3,2,1,0:T(8,128)S(1)} %get-tuple-element.71.old_ref, f32[3,40,2,8,128]{4,3,2,1,0:T(8,128)S(1)} %get-tuple-element.72.sigma_ref), custom_call_target="tpu_custom_call" | custom-call | tf_op jit(solution)/shard_map/second_third_basis/pallas_call | solution.py:731
  60.0 13.9 %all_to_all.50 = f32[128,1,128]{2,1,0:T(1,128)S(1)} all-to-all(f32[128,1,128]{2,1,0:T(1,128)S(1)} %bitcast.62), channel_id=1, replica_groups=mesh['gx'=16,'gy'=8] {'gx','gy'}, dimensions={0} | all-to-all | bytes 131072 | tf_op jit(solution)/shard_map/all_to_all | solution.py:777
  73.9 0.0 copy-done
  73.9 0.0 copy-done.1
  73.9 0.0 copy-done.2
  73.9 4.8 %second_third_update.1 = (f32[768,128]{1,0:T(8,128)}, f32[768,128]{1,0:T(8,128)}, s32[1,1]{1,0:T(1,128)}) custom-call(f32[128,128]{1,0:T(8,128)S(1)} %bitcast.59, f32[80,128]{1,0:T(8,128)S(1)} %copy-done.1, bf16[2,128,128]{2,1,0:T(8,128)(2,1)S(1)} %copy-done, bf16[2,32,32]{2,1,0:T(8,128)(2,1)S(1)} %copy-done.2, ...), custom_call_target="tpu_custom_call" | custom-call | tf_op jit(solution)/shard_map/second_third_update/pallas_call | solution.py:751
  78.7 0.0 copy-done.3
  78.7 0.0 copy-done.4
  78.7 0.8 %while.11 = (s32[]{:T(128)}, f32[2,3,8,16,128]{4,3,2,1,0:T(8,128)}, f32[2,3,8,16,128]{4,3,2,1,0:T(8,128)}, s32[2]{0:T(128)S(1)}, f32[2,3,8,16,128]{4,3,2,1,0:T(8,128)S(1)}, /*index=5*/f32[3,8,16,128]{3,2,1,0:T(8,128)S(1)}) while((s32[]{:T(128)}, f32[2,3,8,16,128]{4,3,2,1,0:T(8,128)}, f32[2,3,8,16,128]{4,3,2,1,0:T(8,128)}, s32[2]{0:T(128)S(1)}, ...), condition=%region_1.2_spmd, body=%region_0.1_spmd | while | flops 8517016 | bytes 14884225 | solution.py:832
  (7 shorter events, 0.1 us)
Async XLA Ops:
  2.6 9.5 %collective-permute-start.9 = (f32[9,4,8,128]{3,2,1,0:T(8,128)S(1)}, f32[9,4,8,128]{3,2,1,0:T(8,128)S(1)}, u32[]{:S(2)}, u32[]{:S(2)}) collective-permute-start(f32[9,4,8,128]{3,2,1,0:T(8,128)S(1)} %get-tuple-element.66), channel_id=1, source_target_pairs={{0,7},{1,0},{2,1},{3,2},{4,3},{5,4},{6,5},{7,6},{8,15},{9,8},{10,9... | collective-permute-start | bytes 442376 | tf_op jit(solution)/shard_map/ppermute | solution.py:801
  4.0 8.1 %collective-permute-start.8 = (f32[9,4,8,128]{3,2,1,0:T(8,128)S(1)}, f32[9,4,8,128]{3,2,1,0:T(8,128)S(1)}, u32[]{:S(2)}, u32[]{:S(2)}) collective-permute-start(f32[9,4,8,128]{3,2,1,0:T(8,128)S(1)} %get-tuple-element.66), channel_id=1, source_target_pairs={{0,1},{1,2},{2,3},{3,4},{4,5},{5,6},{6,7},{7,0},{8,9},{9,10},{10,1... | collective-permute-start | bytes 442376 | tf_op jit(solution)/shard_map/ppermute | solution.py:800
  5.2 18.0 %collective-permute-start.6 = (f32[9,12,8,128]{3,2,1,0:T(8,128)S(1)}, f32[9,12,8,128]{3,2,1,0:T(8,128)S(1)}, u32[]{:S(2)}, u32[]{:S(2)}) collective-permute-start(f32[9,12,8,128]{3,2,1,0:T(8,128)S(1)} %get-tuple-element.64), channel_id=1, source_target_pairs={{0,8},{8,16},{16,24},{24,32},{32,40},{40,48},{48,56},{56,64},{64,7... | collective-permute-start | bytes 1327112 | tf_op jit(solution)/shard_map/ppermute | solution.py:802
  6.5 16.7 %collective-permute-start.7 = (f32[9,12,8,128]{3,2,1,0:T(8,128)S(1)}, f32[9,12,8,128]{3,2,1,0:T(8,128)S(1)}, u32[]{:S(2)}, u32[]{:S(2)}) collective-permute-start(f32[9,12,8,128]{3,2,1,0:T(8,128)S(1)} %get-tuple-element.65), channel_id=1, source_target_pairs={{0,120},{8,0},{16,8},{24,16},{32,24},{40,32},{48,40},{56,48},{64,5... | collective-permute-start | bytes 1327112 | tf_op jit(solution)/shard_map/ppermute | solution.py:803
  12.2 10.0 %collective-permute-start.11 = (f32[9,3,8,128]{3,2,1,0:T(8,128)S(1)}, f32[9,3,8,128]{3,2,1,0:T(8,128)S(1)}, u32[]{:S(2)}, u32[]{:S(2)}) collective-permute-start(f32[9,3,8,128]{3,2,1,0:T(8,128)S(1)} %get-tuple-element.99), channel_id=1, source_target_pairs={{0,120},{8,0},{16,8},{24,16},{32,24},{40,32},{48,40},{56,48},{64,5... | collective-permute-start | bytes 331784 | tf_op jit(solution)/shard_map/ppermute | solution.py:807
  14.4 8.9 %collective-permute-start.10 = (f32[9,3,8,128]{3,2,1,0:T(8,128)S(1)}, f32[9,3,8,128]{3,2,1,0:T(8,128)S(1)}, u32[]{:S(2)}, u32[]{:S(2)}) collective-permute-start(f32[9,3,8,128]{3,2,1,0:T(8,128)S(1)} %get-tuple-element.100), channel_id=1, source_target_pairs={{0,8},{8,16},{16,24},{24,32},{32,40},{40,48},{48,56},{56,64},{64,7... | collective-permute-start | bytes 331784 | tf_op jit(solution)/shard_map/ppermute | solution.py:806
  23.2 50.6 %copy-start = (bf16[2,128,128]{2,1,0:T(8,128)(2,1)S(1)}, bf16[2,128,128]{2,1,0:T(8,128)(2,1)}, u32[]{:S(2)}) copy-start(bf16[2,128,128]{2,1,0:T(8,128)(2,1)} %constant.121.clone.picks_ref) | copy-start | bytes 196612
  23.2 50.6 %copy-start.1 = (f32[80,128]{1,0:T(8,128)S(1)}, f32[80,128]{1,0:T(8,128)}, u32[]{:S(2)}) copy-start(f32[80,128]{1,0:T(8,128)} %constant.120.clone.table_ref) | copy-start | bytes 122884
  23.2 50.6 %copy-start.2 = (bf16[2,32,32]{2,1,0:T(8,128)(2,1)S(1)}, bf16[2,32,32]{2,1,0:T(8,128)(2,1)}, u32[]{:S(2)}) copy-start(bf16[2,32,32]{2,1,0:T(8,128)(2,1)} %constant.122.clone.select_ref) | copy-start | bytes 12292
  29.1 49.6 %copy-start.3 = (f32[2,3,8,16,128]{4,3,2,1,0:T(8,128)S(1)}, f32[2,3,8,16,128]{4,3,2,1,0:T(8,128)}, u32[]{:S(2)}) copy-start(f32[2,3,8,16,128]{4,3,2,1,0:T(8,128)} %param.8) | copy-start | bytes 1179652
  29.1 49.6 %copy-start.4 = (f32[3,8,16,128]{3,2,1,0:T(8,128)S(1)}, f32[3,8,16,128]{3,2,1,0:T(8,128)}, u32[]{:S(2)}) copy-start(f32[3,8,16,128]{3,2,1,0:T(8,128)} %param.9) | copy-start | bytes 589828
  29.1 49.6 %copy-start.5 = (s32[2]{0:T(128)S(1)}, s32[2]{0:T(128)}, u32[]{:S(2)}) copy-start(s32[2]{0:T(128)} %param.10) | copy-start | bytes 28

commit v5 on v4

--- a/solution.py
+++ b/solution.py
@@ -14,6 +14,8 @@
 ROWS = 16
 LANES = 128
 HALO = 12
+NEAR = 4
+FAR = HALO - NEAR
 WIDE = ROWS + 2 * HALO
 
 shift_real = 0.5
@@ -87,9 +89,9 @@
             rows = [mixed[NZ * x : NZ * x + NZ] for x in range(ROWS)]
             for x in range(ROWS):
                 tile_ref[group, x] = rows[x]
-                if x >= ROWS - HALO:
-                    last_ref[group, x - (ROWS - HALO)] = rows[x]
-                if x < HALO:
+                if x >= ROWS - NEAR:
+                    last_ref[group, x - (ROWS - NEAR)] = rows[x]
+                if x < NEAR:
                     first_ref[group, x] = rows[x]
             for four in range(ROWS // 4):
                 strip = None
@@ -110,10 +112,10 @@
 
 
 def pack_messages(right_side, conductivity):
-    rows, edge = (9, ROWS) + BLOCK, (9, HALO) + BLOCK
+    edge = vmem((9, NEAR) + BLOCK)
     return pl.pallas_call(
         pack_kernel,
-        out_shape=(vmem(rows), vmem(edge), vmem(edge), vmem((9, ROWS // 4) + BLOCK)),
+        out_shape=(vmem((9, ROWS) + BLOCK), edge, edge, vmem((9, ROWS // 4) + BLOCK)),
         in_specs=[HBM, HBM],
         out_specs=(VMEM,) * 4,
         scratch_shapes=[vmem((6 * NZ * ROWS, LANES)), vmem((3 * NZ * ROWS, LANES)), pltpu.SemaphoreType.DMA((2,))],
@@ -135,7 +137,7 @@
     return real * cosine - imag * sine, real * sine + imag * cosine
 
 
-def fill_region(scal_ref, rows_ref, strips_ref, count, base, turned, basis_ref, sigma_ref):
+def fill_region(scal_ref, rows_ref, strips_ref, at, count, base, turned, basis_ref, sigma_ref):
     lanes = lane_index(NZ)
     own = lanes < 64
     cosine = jnp.where(own, 1.0, jnp.where(lanes < 96, scal_ref[6], scal_ref[4]))
@@ -150,7 +152,7 @@
 
                 def pair(group):
                     row = rows_ref[group, x]
-                    side = roll_lanes(strips_ref[group, four], -16 * j)
+                    side = roll_lanes(strips_ref[group, at + four], -16 * j)
                     return jnp.where(own, row, side), roll_lanes(jnp.where(own, side, row), 64)
 
                 real, imag, sigma = pair(comp), pair(comp + 3), pair(comp + 6)
@@ -225,7 +227,7 @@
                 basis_ref[there, 1, c, x, b] = new_imag
         return tuple(fresh)
 
-    size = next(n for n in (9, 8, 10, 7, 11, 12, 13, 17, 19, 1) if count % n == 0) if len(starts) == 1 else 6
+    size = next(n for n in (10, 14, 13, 12, 11, 9, 8, 1) if count % n == 0) if len(starts) == 1 else 4
 
     def body(block, carry):
         carry = list(carry)
@@ -246,12 +248,15 @@
     return values[0]
 
 
-def gram(basis_ref, sums_ref, gram_ref):
+COUNT = len(PAIRS) + S * (S + 1) // 2
+
+
+def gram_rows(basis_ref, begin, end, sums):
     def body(step, sums):
         reals, imags = [[] for _ in PAIRS], [[] for _ in PAIRS]
         for c in range(3):
             for n in range(4):
-                x, b = HALO + 2 * step + n // 2, n % 2
+                x, b = begin + 2 * step + n // 2, n % 2
                 vs = [[basis_ref[k, ri, c, x, b] for ri in range(2)] for k in range(S + 1)]
                 for at, (j, k) in enumerate(PAIRS):
                     reals[at].append(vs[j][0] * vs[k][0] + vs[j][1] * vs[k][1])
@@ -260,8 +265,10 @@
         fresh = [tree(terms) for terms in reals + imags if terms]
         return tuple(total + term for total, term in zip(sums, fresh))
 
-    count = len(PAIRS) + sum(j != k for j, k in PAIRS)
-    sums = lax.fori_loop(0, ROWS // 2, body, (jnp.zeros(BLOCK, jnp.float32),) * count)
+    return lax.fori_loop(0, (end - begin) // 2, body, tuple(sums))
+
+
+def gram(sums, sums_ref, gram_ref):
     own = lane_index(1) < 64
     sums_ref[...] = jnp.zeros((LANES, LANES), jnp.float32)
     for at, total in enumerate(sums):
@@ -351,28 +358,40 @@
     return tuple((parts[0][ri] + parts[1][ri]) + (parts[2][ri] + parts[3][ri]) for ri in range(2))
 
 
-def inner_kernel(scal_ref, tile_ref, sides_ref, basis_ref, sigma_ref):
-    fill_region(scal_ref, tile_ref, sides_ref, ROWS, HALO, None, basis_ref, sigma_ref)
+def inner_kernel(scal_ref, tile_ref, sides_ref, basis_ref, sigma_ref, sums_ref):
+    fill_region(scal_ref, tile_ref, sides_ref, 0, ROWS, HALO, None, basis_ref, sigma_ref)
     for k in range(S):
         apply_step(basis_ref, sigma_ref, k, (HALO + k + 1,), ROWS - 2 * k - 2)
+    sums = gram_rows(basis_ref, HALO + S, HALO + ROWS - S, [jnp.zeros(BLOCK, jnp.float32)] * COUNT)
+    for at in range(COUNT):
+        sums_ref[at] = sums[at]
 
 
 def first_kernel(
-    scal_ref, last_ref, first_ref, above_ref, below_ref, _, __, basis_ref, sigma_ref, gram_ref, sums_ref
+    scal_ref, last_ref, first_ref, above_ref, below_ref, inner_ref, _, __, basis_ref, sigma_ref, gram_ref, sums_ref
 ):
-    fill_region(scal_ref, last_ref, above_ref, HALO, 0, 0, basis_ref, sigma_ref)
-    fill_region(scal_ref, first_ref, below_ref, HALO, HALO + ROWS, 2, basis_ref, sigma_ref)
+    fill_region(scal_ref, last_ref, above_ref, 0, NEAR, FAR, 0, basis_ref, sigma_ref)
+    fill_region(scal_ref, first_ref, below_ref, 0, NEAR, HALO + ROWS, 2, basis_ref, sigma_ref)
     for k in range(S):
-        apply_step(basis_ref, sigma_ref, k, (k + 1, HALO + ROWS - k - 1), HALO)
-    gram(basis_ref, sums_ref, gram_ref)
-
-
-def next_kernel(sweep, gathered_ref, old_ref, sigma_ref, *refs):
+        apply_step(basis_ref, sigma_ref, k, (FAR + k + 1, HALO + ROWS - k - 1), NEAR)
+    sums = gram_rows(basis_ref, HALO, HALO + S, [inner_ref[at] for at in range(COUNT)])
+    gram(gram_rows(basis_ref, HALO + ROWS - S, HALO + ROWS, sums), sums_ref, gram_ref)
+
+
+def outer_part(scal_ref, above_ref, below_ref, basis_ref, sigma_ref):
+    fill_region(scal_ref, above_ref, above_ref, FAR, FAR, 0, 0, basis_ref, sigma_ref)
+    fill_region(scal_ref, below_ref, below_ref, FAR, FAR, WIDE - FAR, 2, basis_ref, sigma_ref)
+    for k in range(S):
+        apply_step(basis_ref, sigma_ref, k, (k + 1, WIDE - FAR - k - 1), FAR)
+
+
+def next_kernel(sweep, gathered_ref, *refs):
     if sweep == 1:
-        basis_ref, part_ref, gram_ref, sums_ref = refs
+        scal_ref, above_ref, below_ref, _, __, old_ref, sigma_ref, basis_ref, part_ref, gram_ref, sums_ref = refs
         old_part = None
+        outer_part(scal_ref, above_ref, below_ref, old_ref, sigma_ref)
     else:
-        old_part, basis_ref, part_ref, gram_ref, sums_ref = refs
+        old_ref, sigma_ref, old_part, basis_ref, part_ref, gram_ref, sums_ref = refs
     coefs = coefficients(gathered_ref)
     begin, end = S * sweep, WIDE - S * sweep
 
@@ -397,7 +416,8 @@
     each(HALO + ROWS, end, 4, residual_row)
     for k in range(S):
         apply_step(basis_ref, sigma_ref, k, (begin + k + 1,), end - begin - 2 * k - 2)
-    gram(basis_ref, sums_ref, gram_ref)
+    sums = gram_rows(basis_ref, HALO, HALO + ROWS, [jnp.zeros(BLOCK, jnp.float32)] * COUNT)
+    gram(sums, sums_ref, gram_ref)
 
 
 def last_kernel(gathered_ref, old_ref, old_part, part_ref, residual_ref):
@@ -600,7 +620,11 @@
     return jnp.where(lane_index(NZ) < 64, even, roll_lanes(odd, 64))
 
 
-def wide_kernel(gathered_ref, old_ref, sigma_ref, tile_ref, part_ref, gram_ref, basis_ref, acc_ref, sums_ref):
+def wide_kernel(
+    gathered_ref, scal_ref, above_ref, below_ref, _, __,
+    old_ref, sigma_ref, tile_ref, part_ref, gram_ref, basis_ref, acc_ref, sums_ref,
+):
+    outer_part(scal_ref, above_ref, below_ref, old_ref, sigma_ref)
     coefs = coefficients(gathered_ref)
     begin, end = S, WIDE - S
 
@@ -626,19 +650,18 @@
     acc_ref[...] = jnp.zeros(acc_ref.shape, jnp.float32)
 
     def gram_row(x, _):
-        vs = []
-        for k in range(DEGREE + 1):
-            vs.append([[packed(basis_ref[k, ri, c, x, 0], basis_ref[k, ri, c, x, 1]) for c in range(3)] for ri in range(2)])
-            for ri in range(2):
-                for c in range(3):
-                    tile_ref[k, ri, c, x - HALO] = vs[k][ri][c]
-        at = len(BIG_PAIRS)
-        for index, (j, k) in enumerate(BIG_PAIRS):
-            left, right = vs[j], vs[k]
-            acc_ref[index] += tree([left[0][c] * right[0][c] + left[1][c] * right[1][c] for c in range(3)])
-            if j != k:
-                acc_ref[at] += tree([left[0][c] * right[1][c] - left[1][c] * right[0][c] for c in range(3)])
-                at += 1
+        for c in range(3):
+            vs = []
+            for k in range(DEGREE + 1):
+                vs.append([packed(basis_ref[k, ri, c, x, 0], basis_ref[k, ri, c, x, 1]) for ri in range(2)])
+                for ri in range(2):
+                    tile_ref[k, ri, c, x - HALO] = vs[k][ri]
+            at = len(BIG_PAIRS)
+            for index, (j, k) in enumerate(BIG_PAIRS):
+                acc_ref[index] += vs[j][0] * vs[k][0] + vs[j][1] * vs[k][1]
+                if j != k:
+                    acc_ref[at] += vs[j][0] * vs[k][1] - vs[j][1] * vs[k][0]
+                    at += 1
         return 0
 
     lax.fori_loop(HALO, HALO + ROWS, gram_row, 0)
@@ -685,15 +708,16 @@
 
 
 BASIS = (S + 1, 2, 3, WIDE, 2) + BLOCK
+SIGMA = (3, WIDE, 2) + BLOCK
 PART = (2, 3, ROWS, 2) + BLOCK
 
 
 def run_inner(*operands):
     return pl.pallas_call(
         inner_kernel,
-        out_shape=(vmem(BASIS), vmem((3, WIDE, 2) + BLOCK)),
+        out_shape=(vmem(BASIS), vmem(SIGMA), vmem((COUNT,) + BLOCK)),
         in_specs=[SMEM] + [VMEM] * 2,
-        out_specs=(VMEM,) * 2,
+        out_specs=(VMEM,) * 3,
         compiler_params=pltpu.CompilerParams(vmem_limit_bytes=LIMIT),
         cost_estimate=pl.CostEstimate(flops=8_000_000, bytes_accessed=8_000_000, transcendentals=0),
         name="inner_part",
@@ -704,39 +728,47 @@
     return pl.pallas_call(
         first_kernel,
         out_shape=(
-            vmem(BASIS), vmem((3, WIDE, 2) + BLOCK), jax.ShapeDtypeStruct((peers, LANES), jnp.float32)
+            vmem(BASIS), vmem(SIGMA), jax.ShapeDtypeStruct((peers, LANES), jnp.float32)
         ),
-        in_specs=[SMEM] + [VMEM] * 6,
+        in_specs=[SMEM] + [VMEM] * 7,
         out_specs=(VMEM,) * 3,
         scratch_shapes=[vmem((LANES, LANES))],
-        input_output_aliases={5: 0, 6: 1},
+        input_output_aliases={6: 0, 7: 1},
         compiler_params=pltpu.CompilerParams(vmem_limit_bytes=LIMIT),
         name="first_sweep",
     )(*operands)
 
 
 def run_next(peers, sweep, *operands):
-    return pl.pallas_call(
+    out_shape = (vmem(BASIS), vmem(PART), jax.ShapeDtypeStruct((peers, LANES), jnp.float32))
+    if sweep == 1:
+        out_shape = (vmem(BASIS), vmem(SIGMA)) + out_shape
+    outs = pl.pallas_call(
         functools.partial(next_kernel, sweep),
-        out_shape=(vmem(BASIS), vmem(PART), jax.ShapeDtypeStruct((peers, LANES), jnp.float32)),
-        in_specs=[VMEM] * len(operands),
-        out_specs=(VMEM,) * 3,
+        out_shape=out_shape,
+        in_specs=[VMEM, SMEM] + [VMEM] * 4 if sweep == 1 else [VMEM] * 4,
+        out_specs=(VMEM,) * len(out_shape),
         scratch_shapes=[vmem((LANES, LANES))],
+        input_output_aliases={4: 0, 5: 1} if sweep == 1 else {},
         compiler_params=pltpu.CompilerParams(vmem_limit_bytes=LIMIT),
         name="second_sweep" if sweep == 1 else "third_sweep",
     )(*operands)
+    return outs if sweep == 1 else (None, None) + tuple(outs)
 
 
 def run_wide(peers, *operands):
     return pl.pallas_call(
         wide_kernel,
         out_shape=(
+            vmem(BASIS),
+            vmem(SIGMA),
             vmem((DEGREE + 1, 2, 3, ROWS) + BLOCK),
             vmem((2, 3, ROWS) + BLOCK),
             jax.ShapeDtypeStruct((peers, LANES), jnp.float32),
         ),
-        in_specs=[VMEM] * 3,
-        out_specs=(VMEM,) * 3,
+        in_specs=[VMEM, SMEM] + [VMEM] * 4,
+        out_specs=(VMEM,) * 5,
+        input_output_aliases={4: 0, 5: 1},
         scratch_shapes=[
             vmem((DEGREE + 1, 2, 3, WIDE, 2) + BLOCK), vmem((BIG_COUNT,) + BLOCK), vmem((LANES, LANES))
         ],
@@ -778,14 +810,16 @@
 
 
 def phases(bloch_index):
-    theta = 2.0 * math.pi * bloch_index.astype(jnp.float32) / bloch_steps
-    rows = []
-    for axis, angle in (("gx", theta[0]), ("gy", theta[1])):
-        spot, peers = lax.axis_index(axis), lax.axis_size(axis)
-        cosine, sine = jnp.cos(angle), jnp.sin(angle)
-        rows += [jnp.where(spot == 0, cosine, 1.0), jnp.where(spot == 0, -sine, 0.0)]
-        rows += [jnp.where(spot == peers - 1, cosine, 1.0), jnp.where(spot == peers - 1, sine, 0.0)]
-    return jnp.stack(rows)
+    theta = (2.0 * math.pi * bloch_index.astype(jnp.float32) / bloch_steps)[:, None]
+    axis = lax.broadcasted_iota(jnp.int32, (2, 4), 0)
+    place = lax.broadcasted_iota(jnp.int32, (2, 4), 1)
+    spot = jnp.where(axis == 0, lax.axis_index("gx"), lax.axis_index("gy"))
+    last = jnp.where(axis == 0, lax.axis_size("gx"), lax.axis_size("gy")) - 1
+    at_end = spot == jnp.where(place < 2, 0, last)
+    sine = jnp.where(place < 2, -jnp.sin(theta), jnp.sin(theta))
+    cosine = jnp.cos(theta)
+    even = place % 2 == 0
+    return jnp.where(at_end, jnp.where(even, cosine, sine), jnp.where(even, 1.0, 0.0)).reshape(8)
 
 
 def ring(axis, step):
@@ -803,23 +837,29 @@
     below = lax.ppermute(first, "gx", ring("gx", -1))
     from_left = (lax.broadcasted_iota(jnp.int32, strips.shape, 3) // 8) % 2 == 1
     sides = jnp.where(from_left, before, after)
-    corners_above = lax.ppermute(sides[:, 1:], "gx", ring("gx", 1))
-    corners_below = lax.ppermute(sides[:, :-1], "gx", ring("gx", -1))
-    inner = run_inner(scal, tile, sides)
-    basis, sigma, partial = run_first(peers, scal, above, below, corners_above, corners_below, *inner)
-    return peers, basis, sigma, spread(partial)
+    corners_above = lax.ppermute(sides[:, 3:], "gx", ring("gx", 1))
+    corners_below = lax.ppermute(sides[:, :1], "gx", ring("gx", -1))
+    far = jnp.concatenate([tile[:, NEAR:HALO], sides[:, 1:3]], axis=1)
+    basis, sigma, inner = run_inner(scal, tile, sides)
+    far, inner, above, below, corners_above, corners_below = lax.optimization_barrier(
+        (far, inner, above, below, corners_above, corners_below)
+    )
+    far_above = lax.ppermute(far, "gx", ring("gx", 1))
+    far_below = lax.ppermute(far, "gx", ring("gx", -1))
+    basis, sigma, partial = run_first(peers, scal, above, below, corners_above, corners_below, inner, basis, sigma)
+    return peers, (spread(partial), scal, far_above, far_below, basis, sigma)
 
 
 def three_reductions(*operands):
-    peers, basis, sigma, gathered = first_sweep(*operands)
-    basis, part, partial = run_next(peers, 1, gathered, basis, sigma)
-    basis, part, partial = run_next(peers, 2, spread(partial), basis, sigma, part)
+    peers, state = first_sweep(*operands)
+    _, sigma, basis, part, partial = run_next(peers, 1, *state)
+    _, _, basis, part, partial = run_next(peers, 2, spread(partial), basis, sigma, part)
     return run_last(spread(partial), basis, part)
 
 
 def two_reductions(*operands):
-    peers, basis, sigma, gathered = first_sweep(*operands)
-    tile, part, partial = run_wide(peers, gathered, basis, sigma)
+    peers, state = first_sweep(*operands)
+    _, _, tile, part, partial = run_wide(peers, *state)
     return run_end(spread(partial), tile, part)
 
 

time: 79.9 us -> 79.4 us (level)
  starting transfers between devices: 11 us -> 18.5 us
  blocking collectives: 33.2 us -> 29.8 us
  between operations: 3.84 us -> 1.01 us
  waiting for transfers between devices: 2.77 us -> 0.02 us
  Pallas kernels: 26.6 us -> 28.1 us
    ppermute x2 -> x4, starting transfers between devices: 2.18 us -> 9.69 us  [the longest x1 4.77 us: first_sweep(): corners_below = lax.ppermute(sides[:, :1], 'gx', ring('gx', -1))]
    all_to_all x2, blocking collectives: 33.2 us -> 29.8 us  [spread(): return lax.all_to_all(partial, ('gx', 'gy'), 0, 0, tiled=True)]
    ppermute x2 -> x4, waiting for transfers between devices: 2.76 us -> 0.01 us  [the longest x1 0.01 us: first_sweep(): corners_above = lax.ppermute(sides[:, 3:], 'gx', ring('gx', 1))]
    ppermute x1, starting transfers between devices: 1.43 us -> 0.01 us  [first_sweep(): after = lax.ppermute(strips, 'gy', ring('gy', -1))]
    ppermute x1, starting transfers between devices: 1.2 us -> 2.61 us  [first_sweep(): before = lax.ppermute(strips, 'gy', ring('gy', 1))]
    pallas_call x4, Pallas kernels: 21.9 us -> 23.1 us  [the longest x1 14.4 us: run_wide(): pl.pallas_call(wide_kernel, out_shape=(vmem(BASIS), vmem(SIGMA), vmem((DE...]
  transfers between devices with their start and end apart: 6 -> 8, of which waited for: 2 -> 0; matrix products, arithmetic and copies ran while one was open for 2% -> 1% of each run, Pallas kernels for 3% -> 8%
where the time goes in v5:
time: 79.4 us; the launch traced here: 79.2 us
  blocking collectives  29.8 us (38%)
  Pallas kernels  28.1 us (35%)
  starting transfers between devices  18.5 us (23%)
  between operations  1.01 us (1%)
  other arithmetic  0.85 us (1%)
    all_to_all x2, blocking collectives, spread(): return lax.all_to_all(partial, ('gx', 'gy'), 0, 0, tiled=True)  29.8 us
    pallas_call x1, Pallas kernels, run_wide(): pl.pallas_call(wide_kernel, out_shape=(vmem(BASIS), vmem(SIGMA), vmem((DE...  14.4 us
    pallas_call x1, Pallas kernels, run_end(): pl.pallas_call(end_kernel, out_shape=(shape, shape, jax.ShapeDtypeStruct(...  5.01 us
    ppermute x1, starting transfers between devices, first_sweep(): below = lax.ppermute(first, 'gx', ring('gx', -1))  4.91 us
    ppermute x1, starting transfers between devices, first_sweep(): corners_below = lax.ppermute(sides[:, :1], 'gx', ring('gx', -1))  4.77 us
    ppermute x1, starting transfers between devices, first_sweep(): far_below = lax.ppermute(far, 'gx', ring('gx', -1))  4.77 us
    pallas_call x1, Pallas kernels, run_inner(): pl.pallas_call(inner_kernel, out_shape=(vmem(BASIS), vmem(SIGMA), vmem((C...  3.36 us
    pallas_call x1, Pallas kernels, run_first(): pl.pallas_call(first_kernel, out_shape=(vmem(BASIS), vmem(SIGMA), jax.Sha...  3.32 us
  transfers between devices with their start and end apart: 8, of which 0 were waited for; matrix products, arithmetic and copies ran while one was open for 1% of the time, Pallas kernels for 8%

profile of v5, /device:TPU:1, one launch (start us, length us, event | category | flops | bytes accessed | tf_op | source)
XLA Modules:
  0.0 79.2 jit_solution(12918179683615126077)
XLA Ops:
  0.6 1.9 %pack_messages.3 = (f32[9,16,8,128]{3,2,1,0:T(8,128)S(1)}, f32[9,4,8,128]{3,2,1,0:T(8,128)S(1)}, f32[9,4,8,128]{3,2,1,0:T(8,128)S(1)}, f32[9,4,8,128]{3,2,1,0:T(8,128)S(1)}) custom-call(f32[768,128]{1,0:T(8,128)} %bitcast.38, f32[384,128]{1,0:T(8,128)} %bitcast.40), custom_call_target="tpu_custom_call" | custom-call | tf_op jit(solution)/shard_map/pack_messages/pallas_call | solution.py:116
  2.6 2.6 %collective-permute-start.8 = (f32[9,4,8,128]{3,2,1,0:T(8,128)S(1)}, f32[9,4,8,128]{3,2,1,0:T(8,128)S(1)}, u32[]{:S(2)}, u32[]{:S(2)}) collective-permute-start(f32[9,4,8,128]{3,2,1,0:T(8,128)S(1)} %get-tuple-element.80), channel_id=1, source_target_pairs={{0,1},{1,2},{2,3},{3,4},{4,5},{5,6},{6,7},{7,0},{8,9},{9,10},{10,1... | collective-permute-start | bytes 442376 | tf_op jit(solution)/shard_map/ppermute | solution.py:834
  5.2 0.0 collective-permute-start.9
  5.2 1.3 %collective-permute-start.10 = (f32[9,4,8,128]{3,2,1,0:T(8,128)S(1)}, f32[9,4,8,128]{3,2,1,0:T(8,128)S(1)}, u32[]{:S(2)}, u32[]{:S(2)}) collective-permute-start(f32[9,4,8,128]{3,2,1,0:T(8,128)S(1)} %get-tuple-element.82), channel_id=1, source_target_pairs={{0,8},{8,16},{16,24},{24,32},{32,40},{40,48},{48,56},{56,64},{64,7... | collective-permute-start | bytes 442376 | tf_op jit(solution)/shard_map/ppermute | solution.py:836
  6.5 4.9 %collective-permute-start.11 = (f32[9,4,8,128]{3,2,1,0:T(8,128)S(1)}, f32[9,4,8,128]{3,2,1,0:T(8,128)S(1)}, u32[]{:S(2)}, u32[]{:S(2)}) collective-permute-start(f32[9,4,8,128]{3,2,1,0:T(8,128)S(1)} %get-tuple-element.83), channel_id=1, source_target_pairs={{0,120},{8,0},{16,8},{24,16},{32,24},{40,32},{48,40},{56,48},{64,5... | collective-permute-start | bytes 442376 | tf_op jit(solution)/shard_map/ppermute | solution.py:837
  11.4 0.7 fusion.13
  12.1 0.1 compare_select_fusion.3
  12.2 0.1 reshape.115.scal_ref
  12.3 0.0 collective-permute-done.8
  12.3 0.0 collective-permute-done.9
  12.4 0.1 collective-permute-start.12
  12.5 4.8 %collective-permute-start.13 = (f32[9,1,8,128]{3,2,1,0:T(8,128)S(1)}, f32[9,1,8,128]{3,2,1,0:T(8,128)S(1)}, u32[]{:S(2)}, u32[]{:S(2)}) collective-permute-start(f32[9,1,8,128]{3,2,1,0:T(8,128)S(1)} %get-tuple-element.128), channel_id=1, source_target_pairs={{0,120},{8,0},{16,8},{24,16},{32,24},{40,32},{48,40},{56,48},{64,5... | collective-permute-start | bytes 110600 | tf_op jit(solution)/shard_map/ppermute | solution.py:841
  17.3 3.4 %inner_part.3 = (f32[5,2,3,40,2,8,128]{6,5,4,3,2,1,0:T(8,128)S(1)}, f32[3,40,2,8,128]{4,3,2,1,0:T(8,128)S(1)}, f32[24,8,128]{2,1,0:T(8,128)S(1)}) custom-call(f32[8]{0:T(128)S(1)} %reshape.115.scal_ref, f32[9,16,8,128]{3,2,1,0:T(8,128)S(1)} %get-tuple-element.79.tile_ref, f32[9,4,8,128]{3,2,1,0:T(8,128)S(1)} %fusion.9.sides_ref), custom_call_target="tpu_custom_call" | custom-call | flops 8000000 | bytes 8000000 | tf_op jit(solution)/shard_map/inner_part/pallas_call | solution.py:716
  20.7 0.0 collective-permute-done.10.last_ref
  20.7 0.0 collective-permute-done.11.first_ref
  20.7 0.0 collective-permute-done.12.above_ref
  20.7 0.0 collective-permute-done.13.below_ref
  20.7 0.1 collective-permute-start.14
  20.8 4.8 %collective-permute-start.15 = (f32[9,10,8,128]{3,2,1,0:T(8,128)S(1)}, f32[9,10,8,128]{3,2,1,0:T(8,128)S(1)}, u32[]{:S(2)}, u32[]{:S(2)}) collective-permute-start(f32[9,10,8,128]{3,2,1,0:T(8,128)S(1)} %pad_maximum_fusion.1), channel_id=1, source_target_pairs={{0,120},{8,0},{16,8},{24,16},{32,24},{40,32},{48,40},{56,48},{64,5... | collective-permute-start | bytes 1105928 | tf_op jit(solution)/shard_map/ppermute | solution.py:848
  25.6 3.3 %first_sweep.3 = (f32[5,2,3,40,2,8,128]{6,5,4,3,2,1,0:T(8,128)S(1)}, f32[3,40,2,8,128]{4,3,2,1,0:T(8,128)S(1)}, f32[128,128]{1,0:T(8,128)S(1)}) custom-call(f32[8]{0:T(128)S(1)} %reshape.115.scal_ref, f32[9,4,8,128]{3,2,1,0:T(8,128)S(1)} %collective-permute-done.10.last_ref, ...), custom_call_target="tpu_custom_call", output_to_operand_aliasing={{0}: (6, {}), {1}: (7, {})} | custom-call | tf_op jit(solution)/shard_map/first_sweep/pallas_call | solution.py:728
  28.9 0.0 copy-start.5
  28.9 0.0 copy-start.6
  28.9 0.0 copy-start.7
  28.9 15.9 %all_to_all.48 = f32[128,1,128]{2,1,0:T(1,128)S(1)} all-to-all(f32[128,1,128]{2,1,0:T(1,128)S(1)} %bitcast.37), channel_id=1, replica_groups=mesh['gx'=16,'gy'=8] {'gx','gy'}, dimensions={0} | all-to-all | bytes 131072 | tf_op jit(solution)/shard_map/all_to_all | solution.py:809
  44.9 0.0 collective-permute-done.14.above_ref
  44.9 0.0 collective-permute-done.15.below_ref
  44.9 14.4 %second_third_basis.1 = (f32[5,2,3,40,2,8,128]{6,5,4,3,2,1,0:T(8,128)S(1)}, f32[3,40,2,8,128]{4,3,2,1,0:T(8,128)S(1)}, f32[9,2,3,16,8,128]{5,4,3,2,1,0:T(8,128)S...) custom-call(f32[128,128]{1,0:T(8,128)S(1)} %bitcast.34, ...), custom_call_target="tpu_custom_call", output_to_operand_aliasing={{0}: (4, {}), {1}: (5, {})} | custom-call | tf_op jit(solution)/shard_map/second_third_basis/pallas_call | solution.py:760
  59.3 13.9 %all_to_all.49 = f32[128,1,128]{2,1,0:T(1,128)S(1)} all-to-all(f32[128,1,128]{2,1,0:T(1,128)S(1)} %bitcast.36), channel_id=1, replica_groups=mesh['gx'=16,'gy'=8] {'gx','gy'}, dimensions={0} | all-to-all | bytes 131072 | tf_op jit(solution)/shard_map/all_to_all | solution.py:809
  73.2 0.0 copy-done.2
  73.2 0.0 copy-done.3
  73.2 5.0 %second_third_update.1 = (f32[768,128]{1,0:T(8,128)}, f32[768,128]{1,0:T(8,128)}, s32[1,1]{1,0:T(1,128)}) custom-call(f32[128,128]{1,0:T(8,128)S(1)} %bitcast.35, f32[80,128]{1,0:T(8,128)S(1)} %copy-done.3, bf16[2,128,128]{2,1,0:T(8,128)(2,1)S(1)} %copy-done.2, bf16[2,32,32]{2,1,0:T(8,128)(2,1)S(1)} %copy-done.4, ...), custom_call_target="tpu_custom_call" | custom-call | tf_op jit(solution)/shard_map/second_third_update/pallas_call | solution.py:783
  78.3 0.8 %while.11 = (s32[]{:T(128)}, f32[2,3,8,16,128]{4,3,2,1,0:T(8,128)}, f32[2,3,8,16,128]{4,3,2,1,0:T(8,128)}, s32[2]{0:T(128)S(1)}, f32[2,3,8,16,128]{4,3,2,1,0:T(8,128)S(1)}, /*index=5*/f32[3,8,16,128]{3,2,1,0:T(8,128)S(1)}) while((s32[]{:T(128)}, f32[2,3,8,16,128]{4,3,2,1,0:T(8,128)}, f32[2,3,8,16,128]{4,3,2,1,0:T(8,128)}, s32[2]{0:T(128)S(1)}, ...), condition=%region_1.2_spmd, body=%region_0.1_spmd | while | flops 8609264 | bytes 94772768 | solution.py:872
  (17 shorter events, 0.1 us)
Async XLA Ops:
  2.6 9.8 %collective-permute-start.8 = (f32[9,4,8,128]{3,2,1,0:T(8,128)S(1)}, f32[9,4,8,128]{3,2,1,0:T(8,128)S(1)}, u32[]{:S(2)}, u32[]{:S(2)}) collective-permute-start(f32[9,4,8,128]{3,2,1,0:T(8,128)S(1)} %get-tuple-element.80), channel_id=1, source_target_pairs={{0,1},{1,2},{2,3},{3,4},{4,5},{5,6},{6,7},{7,0},{8,9},{9,10},{10,1... | collective-permute-start | bytes 442376 | tf_op jit(solution)/shard_map/ppermute | solution.py:834
  5.2 7.2 %collective-permute-start.9 = (f32[9,4,8,128]{3,2,1,0:T(8,128)S(1)}, f32[9,4,8,128]{3,2,1,0:T(8,128)S(1)}, u32[]{:S(2)}, u32[]{:S(2)}) collective-permute-start(f32[9,4,8,128]{3,2,1,0:T(8,128)S(1)} %get-tuple-element.80), channel_id=1, source_target_pairs={{0,7},{1,0},{2,1},{3,2},{4,3},{5,4},{6,5},{7,6},{8,15},{9,8},{10,9... | collective-permute-start | bytes 442376 | tf_op jit(solution)/shard_map/ppermute | solution.py:835
  5.2 15.5 %collective-permute-start.10 = (f32[9,4,8,128]{3,2,1,0:T(8,128)S(1)}, f32[9,4,8,128]{3,2,1,0:T(8,128)S(1)}, u32[]{:S(2)}, u32[]{:S(2)}) collective-permute-start(f32[9,4,8,128]{3,2,1,0:T(8,128)S(1)} %get-tuple-element.82), channel_id=1, source_target_pairs={{0,8},{8,16},{16,24},{24,32},{32,40},{40,48},{48,56},{56,64},{64,7... | collective-permute-start | bytes 442376 | tf_op jit(solution)/shard_map/ppermute | solution.py:836
  6.5 14.2 %collective-permute-start.11 = (f32[9,4,8,128]{3,2,1,0:T(8,128)S(1)}, f32[9,4,8,128]{3,2,1,0:T(8,128)S(1)}, u32[]{:S(2)}, u32[]{:S(2)}) collective-permute-start(f32[9,4,8,128]{3,2,1,0:T(8,128)S(1)} %get-tuple-element.83), channel_id=1, source_target_pairs={{0,120},{8,0},{16,8},{24,16},{32,24},{40,32},{48,40},{56,48},{64,5... | collective-permute-start | bytes 442376 | tf_op jit(solution)/shard_map/ppermute | solution.py:837
  12.4 8.3 %collective-permute-start.12 = (f32[9,1,8,128]{3,2,1,0:T(8,128)S(1)}, f32[9,1,8,128]{3,2,1,0:T(8,128)S(1)}, u32[]{:S(2)}, u32[]{:S(2)}) collective-permute-start(f32[9,1,8,128]{3,2,1,0:T(8,128)S(1)} %get-tuple-element.129), channel_id=1, source_target_pairs={{0,8},{8,16},{16,24},{24,32},{32,40},{40,48},{48,56},{56,64},{64,7... | collective-permute-start | bytes 110600 | tf_op jit(solution)/shard_map/ppermute | solution.py:840
  12.5 8.2 %collective-permute-start.13 = (f32[9,1,8,128]{3,2,1,0:T(8,128)S(1)}, f32[9,1,8,128]{3,2,1,0:T(8,128)S(1)}, u32[]{:S(2)}, u32[]{:S(2)}) collective-permute-start(f32[9,1,8,128]{3,2,1,0:T(8,128)S(1)} %get-tuple-element.128), channel_id=1, source_target_pairs={{0,120},{8,0},{16,8},{24,16},{32,24},{40,32},{48,40},{56,48},{64,5... | collective-permute-start | bytes 110600 | tf_op jit(solution)/shard_map/ppermute | solution.py:841
  20.7 24.1 %collective-permute-start.14 = (f32[9,10,8,128]{3,2,1,0:T(8,128)S(1)}, f32[9,10,8,128]{3,2,1,0:T(8,128)S(1)}, u32[]{:S(2)}, u32[]{:S(2)}) collective-permute-start(f32[9,10,8,128]{3,2,1,0:T(8,128)S(1)} %pad_maximum_fusion.1), channel_id=1, source_target_pairs={{0,8},{8,16},{16,24},{24,32},{32,40},{40,48},{48,56},{56,64},{64,7... | collective-permute-start | bytes 1105928 | tf_op jit(solution)/shard_map/ppermute | solution.py:847
  20.8 24.1 %collective-permute-start.15 = (f32[9,10,8,128]{3,2,1,0:T(8,128)S(1)}, f32[9,10,8,128]{3,2,1,0:T(8,128)S(1)}, u32[]{:S(2)}, u32[]{:S(2)}) collective-permute-start(f32[9,10,8,128]{3,2,1,0:T(8,128)S(1)} %pad_maximum_fusion.1), channel_id=1, source_target_pairs={{0,120},{8,0},{16,8},{24,16},{32,24},{40,32},{48,40},{56,48},{64,5... | collective-permute-start | bytes 1105928 | tf_op jit(solution)/shard_map/ppermute | solution.py:848
  25.6 47.6 %copy-start.2 = (bf16[2,128,128]{2,1,0:T(8,128)(2,1)S(1)}, bf16[2,128,128]{2,1,0:T(8,128)(2,1)}, u32[]{:S(2)}) copy-start(bf16[2,128,128]{2,1,0:T(8,128)(2,1)} %constant.149.clone.picks_ref) | copy-start | bytes 196612
  25.6 47.6 %copy-start.3 = (f32[80,128]{1,0:T(8,128)S(1)}, f32[80,128]{1,0:T(8,128)}, u32[]{:S(2)}) copy-start(f32[80,128]{1,0:T(8,128)} %constant.148.clone.table_ref) | copy-start | bytes 122884
  25.6 47.6 %copy-start.4 = (bf16[2,32,32]{2,1,0:T(8,128)(2,1)S(1)}, bf16[2,32,32]{2,1,0:T(8,128)(2,1)}, u32[]{:S(2)}) copy-start(bf16[2,32,32]{2,1,0:T(8,128)(2,1)} %constant.150.clone.select_ref) | copy-start | bytes 12292
  28.9 49.3 %copy-start.5 = (f32[2,3,8,16,128]{4,3,2,1,0:T(8,128)S(1)}, f32[2,3,8,16,128]{4,3,2,1,0:T(8,128)}, u32[]{:S(2)}) copy-start(f32[2,3,8,16,128]{4,3,2,1,0:T(8,128)} %param.8) | copy-start | bytes 1179652
  28.9 49.3 %copy-start.6 = (f32[3,8,16,128]{3,2,1,0:T(8,128)S(1)}, f32[3,8,16,128]{3,2,1,0:T(8,128)}, u32[]{:S(2)}) copy-start(f32[3,8,16,128]{3,2,1,0:T(8,128)} %param.9) | copy-start | bytes 589828
  28.9 49.3 %copy-start.7 = (s32[2]{0:T(128)S(1)}, s32[2]{0:T(128)}, u32[]{:S(2)}) copy-start(s32[2]{0:T(128)} %param.10) | copy-start | bytes 28

commit v6 on v4

--- a/solution.py
+++ b/solution.py
@@ -225,7 +225,7 @@
                 basis_ref[there, 1, c, x, b] = new_imag
         return tuple(fresh)
 
-    size = next(n for n in (9, 8, 10, 7, 11, 12, 13, 17, 19, 1) if count % n == 0) if len(starts) == 1 else 6
+    size = next(n for n in (10, 14, 13, 12, 11, 9, 8, 1) if count % n == 0) if len(starts) == 1 else 6
 
     def body(block, carry):
         carry = list(carry)
@@ -246,12 +246,15 @@
     return values[0]
 
 
-def gram(basis_ref, sums_ref, gram_ref):
+COUNT = len(PAIRS) + S * (S + 1) // 2
+
+
+def gram_rows(basis_ref, begin, end, sums):
     def body(step, sums):
         reals, imags = [[] for _ in PAIRS], [[] for _ in PAIRS]
         for c in range(3):
             for n in range(4):
-                x, b = HALO + 2 * step + n // 2, n % 2
+                x, b = begin + 2 * step + n // 2, n % 2
                 vs = [[basis_ref[k, ri, c, x, b] for ri in range(2)] for k in range(S + 1)]
                 for at, (j, k) in enumerate(PAIRS):
                     reals[at].append(vs[j][0] * vs[k][0] + vs[j][1] * vs[k][1])
@@ -260,8 +263,10 @@
         fresh = [tree(terms) for terms in reals + imags if terms]
         return tuple(total + term for total, term in zip(sums, fresh))
 
-    count = len(PAIRS) + sum(j != k for j, k in PAIRS)
-    sums = lax.fori_loop(0, ROWS // 2, body, (jnp.zeros(BLOCK, jnp.float32),) * count)
+    return lax.fori_loop(0, (end - begin) // 2, body, tuple(sums))
+
+
+def gram(sums, sums_ref, gram_ref):
     own = lane_index(1) < 64
     sums_ref[...] = jnp.zeros((LANES, LANES), jnp.float32)
     for at, total in enumerate(sums):
@@ -351,20 +356,24 @@
     return tuple((parts[0][ri] + parts[1][ri]) + (parts[2][ri] + parts[3][ri]) for ri in range(2))
 
 
-def inner_kernel(scal_ref, tile_ref, sides_ref, basis_ref, sigma_ref):
+def inner_kernel(scal_ref, tile_ref, sides_ref, basis_ref, sigma_ref, sums_ref):
     fill_region(scal_ref, tile_ref, sides_ref, ROWS, HALO, None, basis_ref, sigma_ref)
     for k in range(S):
         apply_step(basis_ref, sigma_ref, k, (HALO + k + 1,), ROWS - 2 * k - 2)
+    sums = gram_rows(basis_ref, HALO + S, HALO + ROWS - S, [jnp.zeros(BLOCK, jnp.float32)] * COUNT)
+    for at in range(COUNT):
+        sums_ref[at] = sums[at]
 
 
 def first_kernel(
-    scal_ref, last_ref, first_ref, above_ref, below_ref, _, __, basis_ref, sigma_ref, gram_ref, sums_ref
+    scal_ref, last_ref, first_ref, above_ref, below_ref, inner_ref, _, __, basis_ref, sigma_ref, gram_ref, sums_ref
 ):
     fill_region(scal_ref, last_ref, above_ref, HALO, 0, 0, basis_ref, sigma_ref)
     fill_region(scal_ref, first_ref, below_ref, HALO, HALO + ROWS, 2, basis_ref, sigma_ref)
     for k in range(S):
         apply_step(basis_ref, sigma_ref, k, (k + 1, HALO + ROWS - k - 1), HALO)
-    gram(basis_ref, sums_ref, gram_ref)
+    sums = gram_rows(basis_ref, HALO, HALO + S, [inner_ref[at] for at in range(COUNT)])
+    gram(gram_rows(basis_ref, HALO + ROWS - S, HALO + ROWS, sums), sums_ref, gram_ref)
 
 
 def next_kernel(sweep, gathered_ref, old_ref, sigma_ref, *refs):
@@ -397,7 +406,8 @@
     each(HALO + ROWS, end, 4, residual_row)
     for k in range(S):
         apply_step(basis_ref, sigma_ref, k, (begin + k + 1,), end - begin - 2 * k - 2)
-    gram(basis_ref, sums_ref, gram_ref)
+    sums = gram_rows(basis_ref, HALO, HALO + ROWS, [jnp.zeros(BLOCK, jnp.float32)] * COUNT)
+    gram(sums, sums_ref, gram_ref)
 
 
 def last_kernel(gathered_ref, old_ref, old_part, part_ref, residual_ref):
@@ -626,19 +636,18 @@
     acc_ref[...] = jnp.zeros(acc_ref.shape, jnp.float32)
 
     def gram_row(x, _):
-        vs = []
-        for k in range(DEGREE + 1):
-            vs.append([[packed(basis_ref[k, ri, c, x, 0], basis_ref[k, ri, c, x, 1]) for c in range(3)] for ri in range(2)])
-            for ri in range(2):
-                for c in range(3):
-                    tile_ref[k, ri, c, x - HALO] = vs[k][ri][c]
-        at = len(BIG_PAIRS)
-        for index, (j, k) in enumerate(BIG_PAIRS):
-            left, right = vs[j], vs[k]
-            acc_ref[index] += tree([left[0][c] * right[0][c] + left[1][c] * right[1][c] for c in range(3)])
-            if j != k:
-                acc_ref[at] += tree([left[0][c] * right[1][c] - left[1][c] * right[0][c] for c in range(3)])
-                at += 1
+        for c in range(3):
+            vs = []
+            for k in range(DEGREE + 1):
+                vs.append([packed(basis_ref[k, ri, c, x, 0], basis_ref[k, ri, c, x, 1]) for ri in range(2)])
+                for ri in range(2):
+                    tile_ref[k, ri, c, x - HALO] = vs[k][ri]
+            at = len(BIG_PAIRS)
+            for index, (j, k) in enumerate(BIG_PAIRS):
+                acc_ref[index] += vs[j][0] * vs[k][0] + vs[j][1] * vs[k][1]
+                if j != k:
+                    acc_ref[at] += vs[j][0] * vs[k][1] - vs[j][1] * vs[k][0]
+                    at += 1
         return 0
 
     lax.fori_loop(HALO, HALO + ROWS, gram_row, 0)
@@ -691,9 +700,9 @@
 def run_inner(*operands):
     return pl.pallas_call(
         inner_kernel,
-        out_shape=(vmem(BASIS), vmem((3, WIDE, 2) + BLOCK)),
+        out_shape=(vmem(BASIS), vmem((3, WIDE, 2) + BLOCK), vmem((COUNT,) + BLOCK)),
         in_specs=[SMEM] + [VMEM] * 2,
-        out_specs=(VMEM,) * 2,
+        out_specs=(VMEM,) * 3,
         compiler_params=pltpu.CompilerParams(vmem_limit_bytes=LIMIT),
         cost_estimate=pl.CostEstimate(flops=8_000_000, bytes_accessed=8_000_000, transcendentals=0),
         name="inner_part",
@@ -706,10 +715,10 @@
         out_shape=(
             vmem(BASIS), vmem((3, WIDE, 2) + BLOCK), jax.ShapeDtypeStruct((peers, LANES), jnp.float32)
         ),
-        in_specs=[SMEM] + [VMEM] * 6,
+        in_specs=[SMEM] + [VMEM] * 7,
         out_specs=(VMEM,) * 3,
         scratch_shapes=[vmem((LANES, LANES))],
-        input_output_aliases={5: 0, 6: 1},
+        input_output_aliases={6: 0, 7: 1},
         compiler_params=pltpu.CompilerParams(vmem_limit_bytes=LIMIT),
         name="first_sweep",
     )(*operands)
@@ -778,14 +787,16 @@
 
 
 def phases(bloch_index):
-    theta = 2.0 * math.pi * bloch_index.astype(jnp.float32) / bloch_steps
-    rows = []
-    for axis, angle in (("gx", theta[0]), ("gy", theta[1])):
-        spot, peers = lax.axis_index(axis), lax.axis_size(axis)
-        cosine, sine = jnp.cos(angle), jnp.sin(angle)
-        rows += [jnp.where(spot == 0, cosine, 1.0), jnp.where(spot == 0, -sine, 0.0)]
-        rows += [jnp.where(spot == peers - 1, cosine, 1.0), jnp.where(spot == peers - 1, sine, 0.0)]
-    return jnp.stack(rows)
+    theta = (2.0 * math.pi * bloch_index.astype(jnp.float32) / bloch_steps)[:, None]
+    axis = lax.broadcasted_iota(jnp.int32, (2, 4), 0)
+    place = lax.broadcasted_iota(jnp.int32, (2, 4), 1)
+    spot = jnp.where(axis == 0, lax.axis_index("gx"), lax.axis_index("gy"))
+    last = jnp.where(axis == 0, lax.axis_size("gx"), lax.axis_size("gy")) - 1
+    at_end = spot == jnp.where(place < 2, 0, last)
+    sine = jnp.where(place < 2, -jnp.sin(theta), jnp.sin(theta))
+    cosine = jnp.cos(theta)
+    even = place % 2 == 0
+    return jnp.where(at_end, jnp.where(even, cosine, sine), jnp.where(even, 1.0, 0.0)).reshape(8)
 
 
 def ring(axis, step):
@@ -805,8 +816,8 @@
     sides = jnp.where(from_left, before, after)
     corners_above = lax.ppermute(sides[:, 1:], "gx", ring("gx", 1))
     corners_below = lax.ppermute(sides[:, :-1], "gx", ring("gx", -1))
-    inner = run_inner(scal, tile, sides)
-    basis, sigma, partial = run_first(peers, scal, above, below, corners_above, corners_below, *inner)
+    basis, sigma, inner = run_inner(scal, tile, sides)
+    basis, sigma, partial = run_first(peers, scal, above, below, corners_above, corners_below, inner, basis, sigma)
     return peers, basis, sigma, spread(partial)
 
 

time: 79.9 us -> 78.5 us (0.982)
  between operations: 3.84 us -> 0.95 us
  starting transfers between devices: 11 us -> 13.7 us
  waiting for transfers between devices: 2.77 us -> 1.86 us
    ppermute x1, starting transfers between devices: 2.18 us -> 4.77 us  [first_sweep(): corners_below = lax.ppermute(sides[:, :-1], 'gx', ring('gx', -1))]
    ppermute x1, waiting for transfers between devices: 1.72 us -> 0.01 us  [first_sweep(): corners_below = lax.ppermute(sides[:, :-1], 'gx', ring('gx', -1))]
    ppermute x1, starting transfers between devices: 1.43 us -> 0.01 us  [first_sweep(): after = lax.ppermute(strips, 'gy', ring('gy', -1))]
    ppermute x1, starting transfers between devices: 1.2 us -> 2.61 us  [first_sweep(): before = lax.ppermute(strips, 'gy', ring('gy', 1))]
    ppermute x1, waiting for transfers between devices: 1.05 us -> 1.85 us  [first_sweep(): corners_above = lax.ppermute(sides[:, 1:], 'gx', ring('gx', 1))]
  transfers between devices with their start and end apart: 6 -> 6, of which waited for: 2 -> 1; matrix products, arithmetic and copies ran while one was open for 2% -> 1% of each run, Pallas kernels for 3% -> 4%
where the time goes in v6:
time: 78.5 us; the launch traced here: 78.3 us
  blocking collectives  33.9 us (43%)
  Pallas kernels  26.2 us (33%)
  starting transfers between devices  13.7 us (17%)
  waiting for transfers between devices  1.86 us (2%)
  between operations  0.95 us (1%)
  other arithmetic  0.83 us (1%)
    all_to_all x2, blocking collectives, spread(): return lax.all_to_all(partial, ('gx', 'gy'), 0, 0, tiled=True)  33.9 us
    pallas_call x1, Pallas kernels, run_wide(): pl.pallas_call(wide_kernel, out_shape=(vmem((DEGREE + 1, 2, 3, ROWS) + BL...  11.2 us
    pallas_call x1, Pallas kernels, run_first(): pl.pallas_call(first_kernel, out_shape=(vmem(BASIS), vmem((3, WIDE, 2) +...  5.03 us
    ppermute x1, starting transfers between devices, first_sweep(): below = lax.ppermute(first, 'gx', ring('gx', -1))  4.91 us
    ppermute x1, starting transfers between devices, first_sweep(): corners_below = lax.ppermute(sides[:, :-1], 'gx', ring('gx', -1))  4.77 us
    pallas_call x1, Pallas kernels, run_end(): pl.pallas_call(end_kernel, out_shape=(shape, shape, jax.ShapeDtypeStruct(...  4.77 us
    pallas_call x1, Pallas kernels, run_inner(): pl.pallas_call(inner_kernel, out_shape=(vmem(BASIS), vmem((3, WIDE, 2) +...  3.29 us
    ppermute x1, starting transfers between devices, first_sweep(): before = lax.ppermute(strips, 'gy', ring('gy', 1))  2.61 us
  transfers between devices with their start and end apart: 6, of which 1 were waited for; matrix products, arithmetic and copies ran while one was open for 1% of the time, Pallas kernels for 4%

profile of v6, /device:TPU:1, one launch (start us, length us, event | category | flops | bytes accessed | tf_op | source)
XLA Modules:
  0.0 78.3 jit_solution(12984528163810453342)
XLA Ops:
  0.6 1.9 %pack_messages.3 = (f32[9,16,8,128]{3,2,1,0:T(8,128)S(1)}, f32[9,12,8,128]{3,2,1,0:T(8,128)S(1)}, f32[9,12,8,128]{3,2,1,0:T(8,128)S(1)}, f32[9,4,8,128]{3,2,1,0:T(8,128)S(1)}) custom-call(f32[768,128]{1,0:T(8,128)} %bitcast.38, f32[384,128]{1,0:T(8,128)} %bitcast.40), custom_call_target="tpu_custom_call" | custom-call | tf_op jit(solution)/shard_map/pack_messages/pallas_call | solution.py:114
  2.6 2.6 %collective-permute-start.8 = (f32[9,4,8,128]{3,2,1,0:T(8,128)S(1)}, f32[9,4,8,128]{3,2,1,0:T(8,128)S(1)}, u32[]{:S(2)}, u32[]{:S(2)}) collective-permute-start(f32[9,4,8,128]{3,2,1,0:T(8,128)S(1)} %get-tuple-element.68), channel_id=1, source_target_pairs={{0,1},{1,2},{2,3},{3,4},{4,5},{5,6},{6,7},{7,0},{8,9},{9,10},{10,1... | collective-permute-start | bytes 442376 | tf_op jit(solution)/shard_map/ppermute | solution.py:811
  5.2 0.0 collective-permute-start.9
  5.2 1.3 %collective-permute-start.6 = (f32[9,12,8,128]{3,2,1,0:T(8,128)S(1)}, f32[9,12,8,128]{3,2,1,0:T(8,128)S(1)}, u32[]{:S(2)}, u32[]{:S(2)}) collective-permute-start(f32[9,12,8,128]{3,2,1,0:T(8,128)S(1)} %get-tuple-element.66), channel_id=1, source_target_pairs={{0,8},{8,16},{16,24},{24,32},{32,40},{40,48},{48,56},{56,64},{64,7... | collective-permute-start | bytes 1327112 | tf_op jit(solution)/shard_map/ppermute | solution.py:813
  6.5 4.9 %collective-permute-start.7 = (f32[9,12,8,128]{3,2,1,0:T(8,128)S(1)}, f32[9,12,8,128]{3,2,1,0:T(8,128)S(1)}, u32[]{:S(2)}, u32[]{:S(2)}) collective-permute-start(f32[9,12,8,128]{3,2,1,0:T(8,128)S(1)} %get-tuple-element.67), channel_id=1, source_target_pairs={{0,120},{8,0},{16,8},{24,16},{32,24},{40,32},{48,40},{56,48},{64,5... | collective-permute-start | bytes 1327112 | tf_op jit(solution)/shard_map/ppermute | solution.py:814
  11.4 0.7 fusion.13
  12.2 0.0 collective-permute-done.8
  12.2 0.0 collective-permute-done.9
  12.2 0.1 collective-permute-start.10
  12.3 4.8 %collective-permute-start.11 = (f32[9,3,8,128]{3,2,1,0:T(8,128)S(1)}, f32[9,3,8,128]{3,2,1,0:T(8,128)S(1)}, u32[]{:S(2)}, u32[]{:S(2)}) collective-permute-start(f32[9,3,8,128]{3,2,1,0:T(8,128)S(1)} %get-tuple-element.109), channel_id=1, source_target_pairs={{0,120},{8,0},{16,8},{24,16},{32,24},{40,32},{48,40},{56,48},{64,5... | collective-permute-start | bytes 331784 | tf_op jit(solution)/shard_map/ppermute | solution.py:818
  17.1 0.1 compare_select_fusion.3
  17.2 0.1 reshape.115.scal_ref
  17.3 3.3 %inner_part.3 = (f32[5,2,3,40,2,8,128]{6,5,4,3,2,1,0:T(8,128)S(1)}, f32[3,40,2,8,128]{4,3,2,1,0:T(8,128)S(1)}, f32[24,8,128]{2,1,0:T(8,128)S(1)}) custom-call(f32[8]{0:T(128)S(1)} %reshape.115.scal_ref, f32[9,16,8,128]{3,2,1,0:T(8,128)S(1)} %get-tuple-element.69.tile_ref, f32[9,4,8,128]{3,2,1,0:T(8,128)S(1)} %fusion.9.sides_ref), custom_call_target="tpu_custom_call" | custom-call | flops 8000000 | bytes 8000000 | tf_op jit(solution)/shard_map/inner_part/pallas_call | solution.py:701
  20.5 1.8 %collective-permute-done.10.above_ref = f32[9,3,8,128]{3,2,1,0:T(8,128)S(1)} collective-permute-done((f32[9,3,8,128]{3,2,1,0:T(8,128)S(1)}, f32[9,3,8,128]{3,2,1,0:T(8,128)S(1)}, u32[]{:S(2)}, u32[]{:S(2)}) %collective-permute-start.10) | collective-permute-done | bytes 110624 | tf_op jit(solution)/shard_map/ppermute | solution.py:817
  22.4 0.0 collective-permute-done.11.below_ref
  22.4 0.0 collective-permute-done.6.last_ref
  22.4 0.0 collective-permute-done.7.first_ref
  22.4 0.0 copy-start.2
  22.4 0.0 copy-start.3
  22.4 0.0 copy-start.4
  22.4 5.0 %first_sweep.3 = (f32[5,2,3,40,2,8,128]{6,5,4,3,2,1,0:T(8,128)S(1)}, f32[3,40,2,8,128]{4,3,2,1,0:T(8,128)S(1)}, f32[128,128]{1,0:T(8,128)S(1)}) custom-call(f32[8]{0:T(128)S(1)} %reshape.115.scal_ref, f32[9,12,8,128]{3,2,1,0:T(8,128)S(1)} %collective-permute-done.6.last_ref, ...), custom_call_target="tpu_custom_call", output_to_operand_aliasing={{0}: (6, {}), {1}: (7, {})} | custom-call | tf_op jit(solution)/shard_map/first_sweep/pallas_call | solution.py:713
  27.5 0.0 copy-start.6
  27.5 0.0 copy-start.7
  27.5 20.0 %all_to_all.48 = f32[128,1,128]{2,1,0:T(1,128)S(1)} all-to-all(f32[128,1,128]{2,1,0:T(1,128)S(1)} %bitcast.36), channel_id=1, replica_groups=mesh['gx'=16,'gy'=8] {'gx','gy'}, dimensions={0} | all-to-all | bytes 131072 | tf_op jit(solution)/shard_map/all_to_all | solution.py:786
  47.5 11.2 %second_third_basis.1 = (f32[9,2,3,16,8,128]{5,4,3,2,1,0:T(8,128)S(1)}, f32[2,3,16,8,128]{4,3,2,1,0:T(8,128)S(1)}, f32[128,128]{1,0:T(8,128)S(1)}) custom-call(f32[128,128]{1,0:T(8,128)S(1)} %bitcast.35, f32[5,2,3,40,2,8,128]{6,5,4,3,2,1,0:T(8,128)S(1)} %get-tuple-element.74.old_ref, f32[3,40,2,8,128]{4,3,2,1,0:T(8,128)S(1)} %get-tuple-element.75.sigma_ref), custom_call_target="tpu_custom_call" | custom-call | tf_op jit(solution)/shard_map/second_third_basis/pallas_call | solution.py:740
  58.7 13.9 %all_to_all.49 = f32[128,1,128]{2,1,0:T(1,128)S(1)} all-to-all(f32[128,1,128]{2,1,0:T(1,128)S(1)} %bitcast.37), channel_id=1, replica_groups=mesh['gx'=16,'gy'=8] {'gx','gy'}, dimensions={0} | all-to-all | bytes 131072 | tf_op jit(solution)/shard_map/all_to_all | solution.py:786
  72.6 0.0 copy-done.2
  72.6 0.0 copy-done.3
  72.6 0.0 copy-done.4
  72.6 4.8 %second_third_update.1 = (f32[768,128]{1,0:T(8,128)}, f32[768,128]{1,0:T(8,128)}, s32[1,1]{1,0:T(1,128)}) custom-call(f32[128,128]{1,0:T(8,128)S(1)} %bitcast.34, f32[80,128]{1,0:T(8,128)S(1)} %copy-done.3, bf16[2,128,128]{2,1,0:T(8,128)(2,1)S(1)} %copy-done.2, bf16[2,32,32]{2,1,0:T(8,128)(2,1)S(1)} %copy-done.4, ...), custom_call_target="tpu_custom_call" | custom-call | tf_op jit(solution)/shard_map/second_third_update/pallas_call | solution.py:760
  77.4 0.0 copy-done.5
  77.4 0.7 while.11
  (10 shorter events, 0.1 us)
Async XLA Ops:
  2.6 9.6 %collective-permute-start.8 = (f32[9,4,8,128]{3,2,1,0:T(8,128)S(1)}, f32[9,4,8,128]{3,2,1,0:T(8,128)S(1)}, u32[]{:S(2)}, u32[]{:S(2)}) collective-permute-start(f32[9,4,8,128]{3,2,1,0:T(8,128)S(1)} %get-tuple-element.68), channel_id=1, source_target_pairs={{0,1},{1,2},{2,3},{3,4},{4,5},{5,6},{6,7},{7,0},{8,9},{9,10},{10,1... | collective-permute-start | bytes 442376 | tf_op jit(solution)/shard_map/ppermute | solution.py:811
  5.2 7.0 %collective-permute-start.9 = (f32[9,4,8,128]{3,2,1,0:T(8,128)S(1)}, f32[9,4,8,128]{3,2,1,0:T(8,128)S(1)}, u32[]{:S(2)}, u32[]{:S(2)}) collective-permute-start(f32[9,4,8,128]{3,2,1,0:T(8,128)S(1)} %get-tuple-element.68), channel_id=1, source_target_pairs={{0,7},{1,0},{2,1},{3,2},{4,3},{5,4},{6,5},{7,6},{8,15},{9,8},{10,9... | collective-permute-start | bytes 442376 | tf_op jit(solution)/shard_map/ppermute | solution.py:812
  5.2 17.2 %collective-permute-start.6 = (f32[9,12,8,128]{3,2,1,0:T(8,128)S(1)}, f32[9,12,8,128]{3,2,1,0:T(8,128)S(1)}, u32[]{:S(2)}, u32[]{:S(2)}) collective-permute-start(f32[9,12,8,128]{3,2,1,0:T(8,128)S(1)} %get-tuple-element.66), channel_id=1, source_target_pairs={{0,8},{8,16},{16,24},{24,32},{32,40},{40,48},{48,56},{56,64},{64,7... | collective-permute-start | bytes 1327112 | tf_op jit(solution)/shard_map/ppermute | solution.py:813
  6.5 15.9 %collective-permute-start.7 = (f32[9,12,8,128]{3,2,1,0:T(8,128)S(1)}, f32[9,12,8,128]{3,2,1,0:T(8,128)S(1)}, u32[]{:S(2)}, u32[]{:S(2)}) collective-permute-start(f32[9,12,8,128]{3,2,1,0:T(8,128)S(1)} %get-tuple-element.67), channel_id=1, source_target_pairs={{0,120},{8,0},{16,8},{24,16},{32,24},{40,32},{48,40},{56,48},{64,5... | collective-permute-start | bytes 1327112 | tf_op jit(solution)/shard_map/ppermute | solution.py:814
  12.2 10.2 %collective-permute-start.10 = (f32[9,3,8,128]{3,2,1,0:T(8,128)S(1)}, f32[9,3,8,128]{3,2,1,0:T(8,128)S(1)}, u32[]{:S(2)}, u32[]{:S(2)}) collective-permute-start(f32[9,3,8,128]{3,2,1,0:T(8,128)S(1)} %get-tuple-element.110), channel_id=1, source_target_pairs={{0,8},{8,16},{16,24},{24,32},{32,40},{40,48},{48,56},{56,64},{64,7... | collective-permute-start | bytes 331784 | tf_op jit(solution)/shard_map/ppermute | solution.py:817
  12.3 10.1 %collective-permute-start.11 = (f32[9,3,8,128]{3,2,1,0:T(8,128)S(1)}, f32[9,3,8,128]{3,2,1,0:T(8,128)S(1)}, u32[]{:S(2)}, u32[]{:S(2)}) collective-permute-start(f32[9,3,8,128]{3,2,1,0:T(8,128)S(1)} %get-tuple-element.109), channel_id=1, source_target_pairs={{0,120},{8,0},{16,8},{24,16},{32,24},{40,32},{48,40},{56,48},{64,5... | collective-permute-start | bytes 331784 | tf_op jit(solution)/shard_map/ppermute | solution.py:818
  22.4 50.2 %copy-start.2 = (bf16[2,128,128]{2,1,0:T(8,128)(2,1)S(1)}, bf16[2,128,128]{2,1,0:T(8,128)(2,1)}, u32[]{:S(2)}) copy-start(bf16[2,128,128]{2,1,0:T(8,128)(2,1)} %constant.149.clone.picks_ref) | copy-start | bytes 196612
  22.4 50.2 %copy-start.3 = (f32[80,128]{1,0:T(8,128)S(1)}, f32[80,128]{1,0:T(8,128)}, u32[]{:S(2)}) copy-start(f32[80,128]{1,0:T(8,128)} %constant.148.clone.table_ref) | copy-start | bytes 122884
  22.4 50.2 %copy-start.4 = (bf16[2,32,32]{2,1,0:T(8,128)(2,1)S(1)}, bf16[2,32,32]{2,1,0:T(8,128)(2,1)}, u32[]{:S(2)}) copy-start(bf16[2,32,32]{2,1,0:T(8,128)(2,1)} %constant.150.clone.select_ref) | copy-start | bytes 12292
  27.5 49.9 %copy-start.5 = (f32[2,3,8,16,128]{4,3,2,1,0:T(8,128)S(1)}, f32[2,3,8,16,128]{4,3,2,1,0:T(8,128)}, u32[]{:S(2)}) copy-start(f32[2,3,8,16,128]{4,3,2,1,0:T(8,128)} %param.8) | copy-start | bytes 1179652
  27.5 49.9 %copy-start.6 = (f32[3,8,16,128]{3,2,1,0:T(8,128)S(1)}, f32[3,8,16,128]{3,2,1,0:T(8,128)}, u32[]{:S(2)}) copy-start(f32[3,8,16,128]{3,2,1,0:T(8,128)} %param.9) | copy-start | bytes 589828
  27.5 49.9 %copy-start.7 = (s32[2]{0:T(128)S(1)}, s32[2]{0:T(128)}, u32[]{:S(2)}) copy-start(s32[2]{0:T(128)} %param.10) | copy-start | bytes 28
